TPU v7x, 128 devices: a whole 4x4x4 slice. The times are simulated.
128 devices in a mesh: gx: 16 (over x, y), gy: 8 (over z, core).
Axes of the slice: x: 4, y: 4, z: 4, core: 2. Of those that a mesh axis runs over, the one named last changes fastest.
Arguments:
- dual_ops: float32 [16, 8, 1536, 1536], P('gx', 'gy')
- loads: float32 [16, 8, 2, 384, 128], P('gx', 'gy'), may hold values from -16 to 16
- coarse_rhs: float32 [16, 8, 6, 128], P('gx', 'gy'), may hold values from -288 to 288
- coarse_modes: float32 [16, 8, 2, 2, 6, 384], P('gx', 'gy'), as said below
- free_mask: int32 [16, 8, 2, 384], P('gx', 'gy'), may hold values from 0 to 1
- face_match: int32 [16, 8, 2, 384], P('gx', 'gy'), may hold values from 0 to 383, each once within a row
- coarse_rows: float32 [16, 8, 3, 6, 768], P('gx', 'gy'), as said below
Outputs:
- multipliers: float32 [16, 8, 2, 384, 128], P('gx', 'gy')
- projected: float32 [16, 8, 2, 384, 128], P('gx', 'gy')
Inputs may be any that keep to these rules, and one draw needn't show every extreme that they name: The draws of coarse_modes, free_mask and coarse_rows belong together. coarse_modes[a,b,0,1] is zero on the last grid column and coarse_modes[a,b,1,1] on the last grid row. With C the symmetric positive definite coarse matrix whose entries are the sums of free times products of the coarse-mode images of two modes over all east and south face multipliers (G^T G restricted to free multipliers, in the order (a, b, mode)), coarse_rows[a,b,0] are the rows of the inverse of C for the modes of (a,b), up to rounding; coarse_rows[a,b,1] equals coarse_rows[a,b+1,0] and coarse_rows[a,b,2] equals coarse_rows[a+1,b,0], zero where that neighbour does not exist.
All inputs are finite; a program needn't handle non-finite values.
Results may differ from a plain program's by a relative error of at most 0.00029.
Values sent between devices are 32-bit elements; how exact they have to be, the bound alone decides.
No kernel may reach another device: no remote copies, remote signals or barrier semaphores. Data moves between devices by JAX's collectives and lax.ppermute only.
A program may use at most 64 MiB of HBM per device.

v0:
```python
import jax
import jax.numpy as jnp
from jax import lax
from jax.sharding import PartitionSpec as P

ITERS = 3


HIGHEST = lax.Precision.HIGHEST


def shifted(shard, axis, by):
    peers = lax.axis_size(axis)
    pairs = [(i, i + by) for i in range(peers) if 0 <= i + by < peers]
    return lax.ppermute(shard, axis, pairs)


def lower_shift(values, dimension):
    widths = [(0, 0)] * values.ndim
    widths[dimension] = (1, 0)
    return lax.slice_in_dim(jnp.pad(values, widths), 0, values.shape[dimension], axis=dimension)


def local(dual_ops, loads, coarse_rhs, coarse_modes, free_mask, face_match, coarse_rows):
    operator = dual_ops[0, 0]
    mode_table = coarse_modes[0, 0]
    free_slots = free_mask[0, 0].astype(jnp.float32)[..., None]
    slot_match = face_match[0, 0]
    inverse_rows = coarse_rows[0, 0]
    face_slots = slot_match.shape[1]
    case_count = loads.shape[-1]
    slot_order = jnp.arange(face_slots, dtype=jnp.int32)
    inverse_west = jnp.zeros((face_slots,), jnp.int32).at[slot_match[0]].set(slot_order)
    inverse_north = jnp.zeros((face_slots,), jnp.int32).at[slot_match[1]].set(slot_order)

    def apply_dual(field):
        from_west = shifted(field[0], "gy", 1)
        from_north = shifted(field[1], "gx", 1)
        west_side = -jnp.take(from_west, slot_match[0], axis=0)
        north_side = -jnp.take(from_north, slot_match[1], axis=0)
        stacked = jnp.concatenate([field[0], field[1], west_side, north_side], axis=0)
        product = jnp.dot(operator, stacked, precision=HIGHEST, preferred_element_type=jnp.float32)
        product = product.reshape(4, face_slots, case_count)
        back_west = shifted(jnp.take(product[2], inverse_west, axis=0), "gy", -1)
        back_north = shifted(jnp.take(product[3], inverse_north, axis=0), "gx", -1)
        return (product[:2] - jnp.stack([back_west, back_north])) * free_slots

    def coarse_terms(field):
        own_terms = jnp.einsum("fjk,fkc->jc", mode_table[:, 0], field, precision=HIGHEST)
        east_terms = jnp.dot(
            mode_table[0, 1], field[0], precision=HIGHEST, preferred_element_type=jnp.float32
        )
        south_terms = jnp.dot(
            mode_table[1, 1], field[1], precision=HIGHEST, preferred_element_type=jnp.float32
        )
        return (own_terms, east_terms, south_terms)

    def coarse_solve(own_terms, east_terms, south_terms):
        stacked = jnp.stack([own_terms, east_terms, south_terms])[None]
        gathered = lax.all_gather(stacked, ("gx", "gy"), axis=0, tiled=True)
        table = gathered.reshape(lax.axis_size("gx"), lax.axis_size("gy"), 3, 6, case_count)
        summed = table[:, :, 0] + lower_shift(table[:, :, 1], 1) + lower_shift(table[:, :, 2], 0)
        flat = summed.reshape(-1, case_count)
        return jnp.einsum("rjn,nc->rjc", inverse_rows, flat, precision=HIGHEST)

    def mode_images(alpha):
        east_face = jnp.einsum("jk,jc->kc", mode_table[0, 0], alpha[0], precision=HIGHEST)
        east_face = east_face + jnp.einsum(
            "jk,jc->kc", mode_table[0, 1], alpha[1], precision=HIGHEST
        )
        south_face = jnp.einsum("jk,jc->kc", mode_table[1, 0], alpha[0], precision=HIGHEST)
        south_face = south_face + jnp.einsum(
            "jk,jc->kc", mode_table[1, 1], alpha[2], precision=HIGHEST
        )
        return jnp.stack([east_face, south_face]) * free_slots

    def project(field):
        own_terms, east_terms, south_terms = coarse_terms(field)
        return field - mode_images(coarse_solve(own_terms, east_terms, south_terms))

    def squares(field):
        return lax.psum(jnp.sum(field * field, axis=(0, 1)), ("gx", "gy"))

    zeros_rhs = jnp.zeros_like(coarse_rhs[0, 0])
    multipliers = mode_images(coarse_solve(coarse_rhs[0, 0], zeros_rhs, zeros_rhs))
    gradient = apply_dual(multipliers) - loads[0, 0] * free_slots
    projected = project(gradient)
    norm_now = squares(projected)
    direction = projected
    for step in range(ITERS):
        image = apply_dual(direction)
        curvature = lax.psum(jnp.sum(direction * image, axis=(0, 1)), ("gx", "gy"))
        step_size = norm_now / curvature
        multipliers = multipliers + step_size * direction
        gradient = gradient + step_size * image
        projected = project(gradient)
        norm_next = squares(projected)
        if step + 1 < ITERS:
            direction = projected + norm_next / norm_now * direction
            norm_now = norm_next
    return (multipliers[None, None], projected[None, None])


def solution(mesh):
    in_specs = (
        P("gx", "gy", None, None),
        P("gx", "gy", None, None, None),
        P("gx", "gy", None, None),
        P("gx", "gy", None, None, None, None),
        P("gx", "gy", None, None),
        P("gx", "gy", None, None),
        P("gx", "gy", None, None, None),
    )
    out_specs = (P("gx", "gy", None, None, None), P("gx", "gy", None, None, None))
    return jax.shard_map(local, mesh=mesh, in_specs=in_specs, out_specs=out_specs, check_vma=False)
```

profile of v0, /device:TPU:1, one launch (start us, length us, event | category | flops | bytes accessed | tf_op | source)
XLA Modules:
  0.0 887.9 jit_solution(10953717720650149989)
XLA Ops:
  10.1 2.9 scatter_custom_fusion
  13.1 2.9 scatter_custom_fusion.1
  17.6 61.6 %all-gather.11.cloned.1.call-done = f32[384,6,128]{2,1,0:T(8,128)} async-done(((f32[3,6,128]{2,1,0:T(8,128)}), f32[384,6,128]{2,1,0:T(8,128)}) %all-gather.11.cloned.1.call-update) | async-done | bytes 1179664 | tf_op jit(solution)/shard_map/all_gather | solution.py:60
  94.0 12.2 %fusion.8 = f32[1536,128]{0,1:T(8,128)S(1)} fusion(f32[1,1,1536,1536]{3,2,1,0:T(8,128)} %param.9, f32[384,128]{0,1:T(8,128)S(1)} %select_negate_fusion.6, f32[384,128]{0,1:T(8,128)S(1)} %select_negate_fusion.7, f32[384,128]{0,1:T(8,128)S(1)} %get-tuple-element.58, f32[384,128]{0,1:T(8,128)S(1)} %get-tuple-element.57), kind=kOutput, calls=%fused_computation.26 | convolution fusion | flops 3624468480 | bytes 11010048 | tf_op jit(solution)/shard_map/dot_general | solution.py:42
  110.4 3.2 collective-permute-start.2
  114.1 3.6 collective-permute-done.3
  122.2 67.8 %all-gather.13.cloned.1.call-done = f32[384,6,128]{2,1,0:T(8,128)} async-done(((f32[3,6,128]{2,1,0:T(8,128)}), f32[384,6,128]{2,1,0:T(8,128)}) %all-gather.13.cloned.1.call-update) | async-done | bytes 1179664 | tf_op jit(solution)/shard_map/all_gather | solution.py:60
  205.3 12.2 %fusion.11 = f32[1536,128]{0,1:T(8,128)S(1)} fusion(f32[1,1,1536,1536]{3,2,1,0:T(8,128)} %param.9, f32[384,128]{0,1:T(8,128)S(1)} %select_negate_fusion.4, f32[384,128]{0,1:T(8,128)S(1)} %select_negate_fusion.5, f32[384,128]{0,1:T(8,128)S(1)} %get-tuple-element.56, f32[384,128]{0,1:T(8,128)S(1)} %get-tuple-element.55), kind=kOutput, calls=%fused_computation.27 | convolution fusion | flops 3624468480 | bytes 11010048 | tf_op jit(solution)/shard_map/dot_general | solution.py:42
  222.4 2.8 collective-permute-start.6
  233.8 68.1 %all-reduce.11 = (f32[128]{0:T(128)S(1)}, f32[128]{0:T(128)S(1)}) all-reduce(f32[128]{0:T(128)S(1)} %get-tuple-element.12, f32[128]{0:T(128)S(1)} %get-tuple-element.11), channel_id=1, replica_groups=mesh['gx'=16,'gy'=8] {'gx','gy'}, use_global_device_ids=true, to_apply=%region_3.5 | all-reduce | flops 256 | bytes 2048 | tf_op jit(solution)/shard_map/psum | solution.py:82
  306.8 61.9 %all-gather.15.cloned.1.call-done = f32[384,6,128]{2,1,0:T(8,128)} async-done(((f32[3,6,128]{2,1,0:T(8,128)}), f32[384,6,128]{2,1,0:T(8,128)}) %all-gather.15.cloned.1.call-update) | async-done | bytes 1179664 | tf_op jit(solution)/shard_map/all_gather | solution.py:60
  373.8 62.4 %psum.44 = f32[128]{0:T(128)S(1)} all-reduce(f32[128]{0:T(128)S(1)} %multiply_reduce_fusion.3), channel_id=1, replica_groups=mesh['gx'=16,'gy'=8] {'gx','gy'}, use_global_device_ids=true, to_apply=%region_7.9 | all-reduce | flops 128 | bytes 1024 | tf_op jit(solution)/shard_map/psum | solution.py:82
  436.3 3.2 collective-permute-start.8
  447.5 12.4 %fusion.14 = f32[1536,128]{0,1:T(8,128)S(1)} fusion(f32[1,1,1536,1536]{3,2,1,0:T(8,128)} %param.9, f32[384,128]{0,1:T(8,128)S(1)} %select_negate_fusion.2, f32[384,128]{0,1:T(8,128)} %select_negate_fusion.3, f32[384,128]{0,1:T(8,128)} %copy-done.44, f32[384,128]{0,1:T(8,128)} %copy-done.43), kind=kOutput, calls=%fused_computation.28 | convolution fusion | flops 3624468480 | bytes 11010048 | tf_op jit(solution)/shard_map/dot_general | solution.py:42
  470.1 5.0 collective-permute-done.11
  482.5 67.0 %psum.45 = f32[128]{0:T(128)S(1)} all-reduce(f32[128]{0:T(128)S(1)} %get-tuple-element.19), channel_id=1, replica_groups=mesh['gx'=16,'gy'=8] {'gx','gy'}, use_global_device_ids=true, to_apply=%region_9.11 | all-reduce | flops 128 | bytes 1024 | tf_op jit(solution)/shard_map/psum | solution.py:92
  556.3 61.8 %all-gather.17.cloned.1.call-done = f32[384,6,128]{2,1,0:T(8,128)} async-done(((f32[3,6,128]{2,1,0:T(8,128)}), f32[384,6,128]{2,1,0:T(8,128)}) %all-gather.17.cloned.1.call-update) | async-done | bytes 1179664 | tf_op jit(solution)/shard_map/all_gather | solution.py:60
  626.8 62.4 %psum.46 = f32[128]{0:T(128)S(1)} all-reduce(f32[128]{0:T(128)S(1)} %multiply_reduce_fusion.1), channel_id=1, replica_groups=mesh['gx'=16,'gy'=8] {'gx','gy'}, use_global_device_ids=true, to_apply=%region_11.13 | all-reduce | flops 128 | bytes 1024 | tf_op jit(solution)/shard_map/psum | solution.py:82
  689.3 3.2 collective-permute-start.12
  700.5 12.2 %fusion.17 = f32[1536,128]{0,1:T(8,128)S(1)} fusion(f32[1,1,1536,1536]{3,2,1,0:T(8,128)} %param.9, f32[384,128]{0,1:T(8,128)S(1)} %select_negate_fusion, f32[384,128]{0,1:T(8,128)S(1)} %select_negate_fusion.1, f32[384,128]{0,1:T(8,128)} %copy-done.42, f32[384,128]{0,1:T(8,128)} %copy-done.41), kind=kOutput, calls=%fused_computation.29 | convolution fusion | flops 3624468480 | bytes 11010048 | tf_op jit(solution)/shard_map/dot_general | solution.py:42
  723.0 2.5 collective-permute-start.14
  725.5 5.0 collective-permute-done.15
  737.2 67.1 %psum.47 = f32[128]{0:T(128)S(1)} all-reduce(f32[128]{0:T(128)S(1)} %multiply_reduce_fusion), channel_id=1, replica_groups=mesh['gx'=16,'gy'=8] {'gx','gy'}, use_global_device_ids=true, to_apply=%region_13.15 | all-reduce | flops 128 | bytes 1024 | tf_op jit(solution)/shard_map/psum | solution.py:92
  814.0 57.5 %all-gather.19.cloned.1.call-done = f32[384,6,128]{2,1,0:T(8,128)} async-done(((f32[3,6,128]{2,1,0:T(8,128)}), f32[384,6,128]{2,1,0:T(8,128)}) %all-gather.19.cloned.1.call-update) | async-done | bytes 1179664 | tf_op jit(solution)/shard_map/all_gather | solution.py:60
  (339 shorter events, 151.1 us)
Async XLA Ops:
  7.2 72.1 %all-gather.11.cloned.1.call-start = ((), (), s32[]{:S(2)}) async-start(), calls=%async_computation | async-start | bytes 1585152 | tf_op jit(solution)/shard_map/all_gather | solution.py:60
  8.5 181.5 %all-gather.13.cloned.1.call-start = ((), (), s32[]{:S(2)}) async-start(), calls=%async_computation.1 | async-start | bytes 1585152 | tf_op jit(solution)/shard_map/all_gather | solution.py:60
  84.2 4.6 collective-permute-start
  86.2 6.4 collective-permute-start.1
  109.1 8.5 collective-permute-start.3
  110.4 7.3 collective-permute-start.2
  122.1 246.5 %all-gather.15.cloned.1.call-start = ((), (), s32[]{:S(2)}) async-start(), calls=%async_computation.2 | async-start | bytes 1585152 | tf_op jit(solution)/shard_map/all_gather | solution.py:60
  195.4 4.5 collective-permute-start.4
  197.4 6.5 collective-permute-start.5
  221.1 8.5 collective-permute-start.7
  222.4 7.5 collective-permute-start.6
  229.6 75.3 %copy-start.14 = (f32[384,128]{0,1:T(8,128)}, f32[384,128]{0,1:T(8,128)S(1)}, u32[]{:S(2)}) copy-start(f32[384,128]{0,1:T(8,128)S(1)} %collective-permute-done.7) | copy-start | bytes 589828
  306.8 311.3 %all-gather.17.cloned.1.call-start = ((), (), s32[]{:S(2)}) async-start(), calls=%async_computation.3 | async-start | bytes 1585152 | tf_op jit(solution)/shard_map/all_gather | solution.py:60
  436.3 5.9 collective-permute-start.8
  439.6 6.5 collective-permute-start.9
  466.3 8.8 collective-permute-start.11
  467.6 7.5 collective-permute-start.10
  475.1 78.3 %copy-start.19 = (f32[384,128]{0,1:T(8,128)}, f32[384,128]{0,1:T(8,128)S(1)}, u32[]{:S(2)}) copy-start(f32[384,128]{0,1:T(8,128)S(1)} %collective-permute-done.11) | copy-start | bytes 589828
  556.3 315.1 %all-gather.19.cloned.1.call-start = ((), (), s32[]{:S(2)}) async-start(), calls=%async_computation.4 | async-start | bytes 1585152 | tf_op jit(solution)/shard_map/all_gather | solution.py:60
  689.3 5.9 collective-permute-start.12
  692.6 6.5 collective-permute-start.13
  721.7 8.8 collective-permute-start.15
  723.0 7.5 collective-permute-start.14
  730.5 77.1 %copy-start.33 = (f32[384,128]{0,1:T(8,128)}, f32[384,128]{0,1:T(8,128)S(1)}, u32[]{:S(2)}) copy-start(f32[384,128]{0,1:T(8,128)S(1)} %collective-permute-done.15) | copy-start | bytes 589828
  (42 other events, 587.3 us)
Sparse Core Ops, SparseCore 0:
  11.4 67.8 all-gather.10
  122.2 67.7 all-gather.12
  306.9 61.7 all-gather.14
  556.4 61.6 all-gather.16
  809.7 61.6 all-gather.18
where the time goes:
time: 898 us; the launch traced here: 888 us
  waiting for transfers between devices  338 us (38%)
  blocking collectives  327 us (36%)
  local copies, waits for them, and re-layouts  77.5 us (9%)
  matrix products  63.8 us (7%)
  starting transfers between devices  35.2 us (4%)
  other arithmetic  30.6 us (3%)
  between operations  15.9 us (2%)
    all_gather x5, waiting for transfers between devices, coarse_solve(): gathered = lax.all_gather(stacked, ('gx', 'gy'), axis=0, tiled=True)  311 us
    psum x3, blocking collectives, squares(): return lax.psum(jnp.sum(field * field, axis=(0, 1)), ('gx', 'gy'))  193 us
    psum x2, blocking collectives, local(): curvature = lax.psum(jnp.sum(direction * image, axis=(0, 1)), ('gx', 'gy'))  134 us
    dot_general x4, matrix products, apply_dual(): jnp.dot(operator, stacked, precision=HIGHEST, preferred_element_type=jnp....  49 us
    ppermute x16, starting transfers between devices, shifted(): return lax.ppermute(shard, axis, pairs)  35 us
    ppermute x16, waiting for transfers between devices, shifted(): return lax.ppermute(shard, axis, pairs)  27.4 us
  transfers between devices with their start and end apart: 21, of which 19 were waited for; matrix products, arithmetic and copies ran while one was open for 2% of the time, Pallas kernels for 0%

commit v1 on v0

v1 whole, which is shorter than its diff:
```python
import functools

import jax
import jax.numpy as jnp
import numpy as np
from jax import lax
from jax.experimental import pallas as pl
from jax.experimental.pallas import tpu as pltpu
from jax.sharding import PartitionSpec as P

F32 = jnp.float32
BF16 = jnp.bfloat16
HIGHEST = lax.Precision.HIGHEST
MODES = 6
GROUP = 8
MEMBERS = 5
ROWS = GROUP * MEMBERS
TROWS = 48
NORM_ROW, ENERGY_ROW, CROSS_ROW = 6, 7, 14


def params(megabytes):
    return pltpu.CompilerParams(vmem_limit_bytes=megabytes * 1024 * 1024)


def split(value):
    high = value.astype(BF16)
    low = (value - high.astype(F32)).astype(BF16)
    return high, low


def mm(left, right):
    return jnp.dot(left, right, preferred_element_type=F32)


def both(value):
    high, low = split(value)
    return jnp.concatenate([high, low], axis=1)


def mm3(left_high, left_low, pair):
    columns = pair.shape[1] // 2
    wide = mm(left_high, pair)
    return wide[:, :columns] + wide[:, columns:] + mm(left_low, pair[:, :columns])


def fold_kernel(match_ref, operator_ref, high_ref, low_ref):
    face = pl.program_id(0)
    slots = match_ref.shape[1]
    order = lax.broadcasted_iota(jnp.int32, (slots, slots), 0)

    def moves(side):
        return jnp.where(order == match_ref[side : side + 1, :], 1.0, 0.0).astype(BF16)

    def columns(parts, near, far):
        for part, out in zip(parts, (high_ref, low_ref)):
            own = part[:, : 2 * slots]
            out[:, : 2 * slots] = own if near > 0 else -own
            for side in range(2):
                piece = part[:, (2 + side) * slots : (3 + side) * slots]
                moved = lax.dot_general(
                    piece, moves(side), (((1,), (1,)), ((), ())), preferred_element_type=F32
                )
                out[:, (2 + side) * slots : (3 + side) * slots] = (far * moved).astype(BF16)

    @pl.when(face < 2)
    def _():
        columns(split(operator_ref[...]), 1.0, -1.0)

    for side in range(2):

        @pl.when(face == 2 + side)
        def _(side=side):
            pick = moves(side)
            parts = split(operator_ref[...])
            columns([mm(pick, part).astype(BF16) for part in parts], -1.0, 1.0)


def fold(operator, match):
    size = operator.shape[0]
    slots = match.shape[1]
    block = pl.BlockSpec((slots, size), lambda i: (i, 0))
    return pl.pallas_call(
        fold_kernel,
        grid=(size // slots,),
        in_specs=[pl.BlockSpec((2, slots), lambda i: (0, 0)), block],
        out_specs=[block, block],
        out_shape=[jax.ShapeDtypeStruct((size, size), BF16)] * 2,
        compiler_params=params(48),
        name="fold",
    )(match, operator)


def pack_kernel(rows_ref, modes_ref, free_ref, rhs_ref, east_ref, south_ref, message_ref):
    slots = free_ref.shape[1]
    for face, out in enumerate((east_ref, south_ref)):
        out[...] = jnp.zeros_like(out)
        out[0:MODES, :] = rows_ref[0]
        out[6:7, :slots] = free_ref[face : face + 1, :].astype(F32)
        for side in range(2):
            out[8 : 8 + MODES, side * slots : (side + 1) * slots] = modes_ref[face, side]
    message_ref[...] = jnp.zeros_like(message_ref)
    for peer in range(message_ref.shape[0]):
        message_ref[peer, 0:MODES, :] = rhs_ref[...]


def pack(rows, modes, free, rhs, peers):
    width = rows.shape[-1]
    return pl.pallas_call(
        pack_kernel,
        out_shape=[
            jax.ShapeDtypeStruct((16, width), F32),
            jax.ShapeDtypeStruct((16, width), F32),
            jax.ShapeDtypeStruct((peers, GROUP, rhs.shape[-1]), F32),
        ],
        name="pack",
    )(rows, modes, free, rhs)


def frame_kernel(
    lines, modes_ref, free_ref, rows_ref, west_ref, north_ref,
    mask_ref, t_high_ref, t_low_ref, g_high_ref, g_low_ref, coarse_ref, pieces_ref, table_ref,
):
    slots = free_ref.shape[1]
    cases = mask_ref.shape[1]
    span = MODES * lines[1]
    table_ref[...] = jnp.zeros_like(table_ref)
    masks = [
        free_ref[0:1, :].astype(F32), free_ref[1:2, :].astype(F32),
        west_ref[6:7, :slots], north_ref[6:7, :slots],
    ]
    entries = [
        (0, 0, modes_ref[0, 0]), (0, 1, modes_ref[1, 0]),
        (1, 0, modes_ref[0, 1]), (2, 1, modes_ref[1, 1]),
        (3, 2, west_ref[8 : 8 + MODES, :slots]), (0, 2, west_ref[8 : 8 + MODES, slots : 2 * slots]),
        (4, 3, north_ref[8 : 8 + MODES, :slots]), (0, 3, north_ref[8 : 8 + MODES, slots : 2 * slots]),
    ]
    for member, face, values in entries:
        table_ref[member * GROUP : member * GROUP + MODES, face * slots : (face + 1) * slots] = (
            values * masks[face]
        )
    table = table_ref[...]
    high, low = split(table[:TROWS])
    t_high_ref[...] = high
    t_low_ref[...] = low
    high, low = split(table.T)
    g_high_ref[...] = high
    g_low_ref[...] = low
    for face in range(4):
        spread = jnp.broadcast_to(masks[face], (cases, slots))
        mask_ref[face * slots : (face + 1) * slots, :] = spread.T
    coarse_ref[...] = jnp.zeros_like(coarse_ref)
    members = [rows_ref[0], rows_ref[1], rows_ref[2], west_ref[0:MODES, :], north_ref[0:MODES, :]]
    for member, values in enumerate(members):
        coarse_ref[member * GROUP : member * GROUP + MODES, :] = values
    edge = jnp.zeros((ROWS, span), F32)
    padded = jnp.concatenate([edge, coarse_ref[...], edge], axis=1)
    rest = jnp.zeros((ROWS, pieces_ref.shape[2] - 3 * span), F32)
    for line in range(lines[0]):
        piece = padded[:, line * span : (line + 3) * span]
        pieces_ref[line] = jnp.concatenate([piece, rest], axis=1)


def frame(lines, modes, free, rows, west, north, cases):
    slots = free.shape[1]
    size = 4 * slots
    width = rows.shape[-1]
    return pl.pallas_call(
        functools.partial(frame_kernel, lines),
        out_shape=[
            jax.ShapeDtypeStruct((size, cases), F32),
            jax.ShapeDtypeStruct((TROWS, size), BF16),
            jax.ShapeDtypeStruct((TROWS, size), BF16),
            jax.ShapeDtypeStruct((size, 128), BF16),
            jax.ShapeDtypeStruct((size, 128), BF16),
            jax.ShapeDtypeStruct((ROWS, width), F32),
            jax.ShapeDtypeStruct((lines[0], ROWS, 256), F32),
        ],
        scratch_shapes=[pltpu.VMEM((128, size), F32)],
        compiler_params=params(32),
        name="frame",
    )(modes, free, rows, west, north)


def expansion(lines):
    span = MODES * lines[1]
    out = np.zeros((256, lines[1] * ROWS), np.float32)
    for source in range(lines[1]):
        places = [(0, source), (0, source + 1), (1, source), (0, source - 1), (-1, source)]
        for member, (down, column) in enumerate(places):
            if 0 <= column < lines[1]:
                for mode in range(MODES):
                    at = span * (1 + down) + MODES * column + mode
                    out[at, source * ROWS + member * GROUP + mode] = 1.0
    return jnp.asarray(out, BF16)


def spread_kernel(received_ref, expand_ref, high_ref, low_ref):
    flat = received_ref[...].reshape(high_ref.shape[0], received_ref.shape[2])
    for part, out in zip(split(flat), (high_ref, low_ref)):
        out[...] = mm(part, expand_ref[...]).astype(BF16)


def spread(received, expand):
    shape = (received.shape[0] * ROWS, expand.shape[1])
    return pl.pallas_call(
        spread_kernel,
        out_shape=[jax.ShapeDtypeStruct(shape, BF16)] * 2,
        name="spread",
    )(received, expand)


def solve_kernel(terms_ref, high_ref, low_ref, out_ref):
    terms = terms_ref[...]
    peers, rows, cases = terms.shape
    result = mm3(high_ref[...], low_ref[...], both(terms.reshape(peers * rows, cases)))
    result = result.reshape(out_ref.shape)
    total = jnp.sum(terms, axis=0)
    place = lax.broadcasted_iota(jnp.int32, (rows, cases), 0)
    scalar = (place % GROUP) >= MODES
    out_ref[...] = jnp.where(scalar[None], total[None], result)


def solve(terms, high, low):
    lines = high.shape[0] // ROWS
    return pl.pallas_call(
        solve_kernel,
        out_shape=jax.ShapeDtypeStruct((lines, ROWS, terms.shape[2]), F32),
        name="solve",
    )(terms, high, low)


def lift(alpha, g_high_ref, g_low_ref):
    filler = jnp.zeros((g_high_ref.shape[1] - alpha.shape[0], alpha.shape[1]), F32)
    pair = both(jnp.concatenate([alpha, filler], axis=0))
    return mm3(g_high_ref[...], g_low_ref[...], pair)


def field_image(z_ref, halo_refs, mask_ref, even_x, even_y, faces=4):
    x_first, x_second, y_first, y_second = halo_refs
    received = [
        jnp.where(even_y, y_first[...], y_second[...]),
        jnp.where(even_x, x_first[...], x_second[...]),
    ]
    if faces == 4:
        received.append(jnp.where(even_y, y_second[...], y_first[...]))
        received.append(jnp.where(even_x, x_second[...], x_first[...]))
    slots = received[0].shape[0]
    return jnp.concatenate(
        [
            mask_ref[f * slots : (f + 1) * slots, :] * (z_ref[f] + received[f])
            for f in range(faces)
        ],
        axis=0,
    )


def member_alpha(total):
    place = lax.broadcasted_iota(jnp.int32, total.shape, 0)
    return jnp.where((place % GROUP) < MODES, total, 0.0)


def step_kernel(phase, names, *refs):
    r = dict(zip(names, refs))
    face = pl.program_id(0)
    even_x = r["parity"][0] == 0
    even_y = r["parity"][1] == 0
    slots = r["a_high"].shape[0]
    half = 2 * slots

    @pl.when(face == 0)
    def _():
        r["terms"][...] = jnp.zeros_like(r["terms"])
        if phase == 0:
            alpha = jnp.dot(
                r["coarse"][...], r["rhs"][...], precision=HIGHEST, preferred_element_type=F32
            )
            field = lift(alpha, r["g_high"], r["g_low"])
            r["lam_out"][...] = field[:half]
        else:
            total = jnp.sum(r["parts"][...], axis=0)
            halos = (r["x_first"], r["x_second"], r["y_first"], r["y_second"])
            image = field_image(r["z"], halos, r["mask"], even_x, even_y)
            moved = image - lift(member_alpha(total), r["g_high"], r["g_low"])
            if phase == 1:
                field = moved
            elif phase == 2:
                norm = total[NORM_ROW : NORM_ROW + 1, :]
                energy = total[ENERGY_ROW : ENERGY_ROW + 1, :]
                step = norm / energy
                field = r["p"][...] + step * moved
                r["q_out"][...] = moved
                r["lam_out"][...] = r["lam"][...] + step * r["p"][:half, :]
                r["scal_out"][0:1, :] = norm
                r["scal_out"][1:2, :] = energy
            else:
                step, beta, curvature, norm = step_terms(total, r["scal"])
                direction = r["p"][...] + beta * r["d"][...]
                image_p = moved + beta * r["q"][...]
                field = r["p"][...] + step * image_p
                r["d_out"][...] = direction
                r["q_out"][...] = image_p
                r["lam_out"][...] = r["lam"][...] + step * direction[:half]
                r["scal_out"][0:1, :] = norm
                r["scal_out"][1:2, :] = curvature
                for f in range(4):
                    r["zd_out"][f] = r["z"][f] + beta * r["zd"][f]
        if phase >= 1:
            r["p_out"][...] = field
            r["norm"][...] = jnp.sum(field[:half] * field[:half], axis=0, keepdims=True)
            r["energy"][...] = jnp.zeros_like(r["energy"])
            r["cross"][...] = jnp.zeros_like(r["cross"])
        r["pair"][...] = both(field)

    out = mm3(r["a_high"][...], r["a_low"][...], r["pair"][...])
    if phase == 0:
        out = out - jnp.where(face < 2, r["loads"][jnp.minimum(face, 1)], 0.0)
    r["z_out"][0] = out
    r["terms"][...] += mm3(r["t_high"][...], r["t_low"][...], both(out))
    if phase >= 1:
        rows = pl.ds(pl.multiple_of(face * slots, slots), slots)
        mine = r["p_out"][rows, :]
        r["energy"][...] += jnp.sum(mine * out, axis=0, keepdims=True)
        if phase == 2:
            cross = mine * r["z"][face] + r["p"][rows, :] * out
            r["cross"][...] += jnp.sum(cross, axis=0, keepdims=True)
        elif phase == 3:
            cross = mine * r["zd_out"][face] + r["d_out"][rows, :] * out
            r["cross"][...] += jnp.sum(cross, axis=0, keepdims=True)

    for target, even, first, second in (
        ("send_x_first", even_x, 1, 3), ("send_x_second", even_x, 3, 1),
        ("send_y_first", even_y, 0, 2), ("send_y_second", even_y, 2, 0),
    ):

        @pl.when(face == jnp.where(even, first, second))
        def _(target=target):
            r[target][...] = out

    @pl.when(face == 3)
    def _():
        terms = r["terms"][0:ROWS, :]
        if phase >= 1:
            place = lax.broadcasted_iota(jnp.int32, terms.shape, 0)
            terms = jnp.where(place == NORM_ROW, r["norm"][...], terms)
            terms = jnp.where(place == ENERGY_ROW, r["energy"][...], terms)
            terms = jnp.where(place == CROSS_ROW, r["cross"][...], terms)
        for peer in range(r["message"].shape[0]):
            r["message"][peer] = terms


def step_terms(total, scal_ref):
    norm = total[NORM_ROW : NORM_ROW + 1, :]
    energy = total[ENERGY_ROW : ENERGY_ROW + 1, :]
    cross = total[CROSS_ROW : CROSS_ROW + 1, :]
    beta = norm / scal_ref[0:1, :]
    curvature = energy + beta * cross + beta * beta * scal_ref[1:2, :]
    return norm / curvature, beta, curvature, norm


def step(phase, peers, operator, table, inputs):
    a_high, a_low = operator
    size = a_high.shape[0]
    slots = size // 4
    cases = 128
    values = dict(inputs)
    values.update(a_high=a_high, a_low=a_low, t_high=table[0], t_low=table[1])
    specs = []
    for name, value in values.items():
        if name == "parity":
            specs.append(pl.BlockSpec(memory_space=pltpu.SMEM))
        elif name in ("a_high", "a_low"):
            specs.append(pl.BlockSpec((slots, size), lambda i: (i, 0)))
        elif name in ("t_high", "t_low"):
            specs.append(pl.BlockSpec((TROWS, slots), lambda i: (0, i)))
        else:
            specs.append(whole(value.shape))
    shapes = {
        "z_out": (4, slots, cases),
        "send_x_first": (slots, cases), "send_x_second": (slots, cases),
        "send_y_first": (slots, cases), "send_y_second": (slots, cases),
        "message": (peers, ROWS, cases),
    }
    if phase in (0, 2, 3):
        shapes["lam_out"] = (2 * slots, cases)
    if phase >= 1:
        shapes["p_out"] = (size, cases)
    if phase >= 2:
        shapes["q_out"] = (size, cases)
    if phase == 3:
        shapes["d_out"] = (size, cases)
        shapes["zd_out"] = (4, slots, cases)
    if phase >= 2:
        shapes["scal_out"] = (8, cases)
    out_specs = []
    for name, shape in shapes.items():
        if name == "z_out":
            out_specs.append(pl.BlockSpec((1, slots, cases), lambda i: (i, 0, 0)))
        else:
            out_specs.append(whole(shape))
    scratch = {
        "pair": pltpu.VMEM((size, 2 * cases), BF16),
        "terms": pltpu.VMEM((TROWS, cases), F32),
        "norm": pltpu.VMEM((1, cases), F32),
        "energy": pltpu.VMEM((1, cases), F32),
        "cross": pltpu.VMEM((1, cases), F32),
    }
    names = list(values) + list(shapes) + list(scratch)
    outs = pl.pallas_call(
        functools.partial(step_kernel, phase, names),
        grid=(4,),
        in_specs=specs,
        out_specs=out_specs,
        out_shape=[jax.ShapeDtypeStruct(shape, F32) for shape in shapes.values()],
        scratch_shapes=list(scratch.values()),
        compiler_params=params(48),
        name=f"step{phase}",
    )(*values.values())
    return dict(zip(shapes, outs))


def whole(shape):
    return pl.BlockSpec(shape, lambda i, rank=len(shape): (0,) * rank)


def final_kernel(names, *refs):
    r = dict(zip(names, refs))
    even_x = r["parity"][0] == 0
    even_y = r["parity"][1] == 0
    half = r["lam"].shape[0]
    total = jnp.sum(r["parts"][...], axis=0)
    halos = (r["x_first"], r["x_second"], r["y_first"], r["y_second"])
    image = field_image(r["z"], halos, r["mask"], even_x, even_y, faces=2)
    moved = image - lift(member_alpha(total), r["g_high"], r["g_low"])
    step_size, beta, _, _ = step_terms(total, r["scal"])
    direction = r["p"][...] + beta * r["d"][...]
    r["lam_out"][...] = r["lam"][...] + step_size * direction
    r["p_out"][...] = r["p"][...] + step_size * (moved + beta * r["q"][...])


def final(inputs):
    half, cases = inputs["lam"].shape
    slots = half // 2
    specs = []
    for name, value in inputs.items():
        if name == "parity":
            specs.append(pl.BlockSpec(memory_space=pltpu.SMEM))
        elif name in ("z",):
            specs.append(pl.BlockSpec((2, slots, cases), lambda i: (0, 0, 0)))
        elif name in ("mask", "g_high", "g_low", "p", "d", "q"):
            specs.append(pl.BlockSpec((half, value.shape[1]), lambda i: (0, 0)))
        else:
            specs.append(whole(value.shape))
    names = list(inputs) + ["lam_out", "p_out"]
    return pl.pallas_call(
        functools.partial(final_kernel, names),
        grid=(1,),
        in_specs=specs,
        out_specs=[whole((half, cases))] * 2,
        out_shape=[jax.ShapeDtypeStruct((half, cases), F32)] * 2,
        compiler_params=params(32),
        name="final",
    )(*inputs.values())


def swap_first(peers):
    return [(i, i ^ 1) for i in range(peers)]


def swap_second(peers):
    return [(i, i + 1 if i % 2 else i - 1) for i in range(1, peers - 1)]


def local(dual_ops, loads, coarse_rhs, coarse_modes, free_mask, face_match, coarse_rows):
    operator = dual_ops[0, 0]
    modes = coarse_modes[0, 0]
    free = free_mask[0, 0]
    rows = coarse_rows[0, 0]
    slots, cases = loads.shape[-2:]
    lines = (lax.axis_size("gx"), lax.axis_size("gy"))
    peers = lines[0] * lines[1]
    parity = jnp.stack([lax.axis_index("gx") % 2, lax.axis_index("gy") % 2]).astype(jnp.int32)

    pack_east, pack_south, message = pack(rows, modes, free, coarse_rhs[0, 0], peers)
    west = lax.ppermute(pack_east, "gy", [(i, i + 1) for i in range(lines[1] - 1)])
    north = lax.ppermute(pack_south, "gx", [(i, i + 1) for i in range(lines[0] - 1)])
    gathered = lax.all_to_all(message, ("gx", "gy"), 0, 0)
    rhs = gathered[:, :MODES].reshape(peers * MODES, cases)
    folded = fold(operator, face_match[0, 0])
    mask, t_high, t_low, g_high, g_low, coarse, pieces = frame(
        lines, modes, free, rows, west, north, cases
    )
    received = lax.all_to_all(pieces, "gx", 0, 0)
    solver = spread(received, expansion(lines))

    def exchange(out):
        halo = {
            "x_first": lax.ppermute(out["send_x_first"], "gx", swap_first(lines[0])),
            "x_second": lax.ppermute(out["send_x_second"], "gx", swap_second(lines[0])),
            "y_first": lax.ppermute(out["send_y_first"], "gy", swap_first(lines[1])),
            "y_second": lax.ppermute(out["send_y_second"], "gy", swap_second(lines[1])),
        }
        terms = lax.all_to_all(out["message"], "gy", 0, 0)
        parts = lax.all_to_all(solve(terms, *solver), "gx", 0, 0)
        return dict(parity=parity, parts=parts, z=out["z_out"], mask=mask, g_high=g_high, g_low=g_low, **halo)

    table = (t_high, t_low)
    start = step(
        0, lines[1], folded, table,
        dict(parity=parity, rhs=rhs, coarse=coarse, g_high=g_high, g_low=g_low, loads=loads[0, 0]),
    )
    first = step(1, lines[1], folded, table, exchange(start))
    second = step(
        2, lines[1], folded, table, dict(exchange(first), p=first["p_out"], lam=start["lam_out"])
    )
    third = step(
        3, lines[1], folded, table,
        dict(
            exchange(second), p=second["p_out"], d=first["p_out"], q=second["q_out"],
            zd=first["z_out"], scal=second["scal_out"], lam=second["lam_out"],
        ),
    )
    multipliers, projected = final(
        dict(
            exchange(third), p=third["p_out"], d=third["d_out"], q=third["q_out"],
            scal=third["scal_out"], lam=third["lam_out"],
        )
    )
    shape = (1, 1, 2, slots, cases)
    return multipliers.reshape(shape), projected.reshape(shape)


def solution(mesh):
    in_specs = (
        P("gx", "gy", None, None),
        P("gx", "gy", None, None, None),
        P("gx", "gy", None, None),
        P("gx", "gy", None, None, None, None),
        P("gx", "gy", None, None),
        P("gx", "gy", None, None),
        P("gx", "gy", None, None, None),
    )
    out_specs = (P("gx", "gy", None, None, None), P("gx", "gy", None, None, None))
    return jax.shard_map(local, mesh=mesh, in_specs=in_specs, out_specs=out_specs, check_vma=False)
```

time: 898 us -> 241 us (0.27)
  waiting for transfers between devices: 338 us -> 22.1 us
  blocking collectives: 327 us -> 27.7 us
  matrix products: 63.8 us -> 0 us
  Pallas kernels: 0 us -> 62 us
  starting transfers between devices: 35.2 us -> 83.6 us
  local copies, waits for them, and re-layouts: 77.5 us -> 39.9 us
  other arithmetic: 30.6 us -> 0.07 us
  between operations: 15.9 us -> 0.89 us
    psum x5 -> x0, blocking collectives: 327 us -> none  [the longest x3 193 us: squares(): return lax.psum(jnp.sum(field * field, axis=(0, 1)), ('gx', 'gy'))]
    all_gather x5 -> x0, waiting for transfers between devices: 311 us -> none  [coarse_solve(): gathered = lax.all_gather(stacked, ('gx', 'gy'), axis=0, tiled=True)]
    dot_general x41 -> x0, matrix products: 63.8 us -> none  [the longest x4 49 us: apply_dual(): jnp.dot(operator, stacked, precision=HIGHEST, preferred_element_type=jnp....]
    pallas_call x0 -> x13, Pallas kernels: none -> 62 us  [the longest x4 34.2 us: step(): pl.pallas_call(functools.partial(step_kernel, phase, names), grid=(4,), i...]
    all_to_all x0 -> x7, starting transfers between devices: none -> 53 us  [the longest x4 29.7 us: exchange(): parts = lax.all_to_all(solve(terms, *solver), 'gx', 0, 0)]
    unnamed x97 -> x93, local copies, waits for them, and re-layouts: 7.77 us -> 39.8 us
    all_to_all x0 -> x3, blocking collectives: none -> 27.7 us  [exchange(): terms = lax.all_to_all(out['message'], 'gy', 0, 0)]
    gather x32 -> x0, local copies, waits for them, and re-layouts: 25.8 us -> none  [the longest x8 7.91 us: apply_dual(): back_north = shifted(jnp.take(product[3], inverse_north, axis=0), 'gx', -1)]
  transfers between devices with their start and end apart: 21 -> 25, of which waited for: 19 -> 11; matrix products, arithmetic and copies ran while one was open for 2% -> 0% of each run, Pallas kernels for 0% -> 10%
where the time goes in v1:
time: 241 us; the launch traced here: 236 us
  starting transfers between devices  83.6 us (35%)
  Pallas kernels  62 us (26%)
  local copies, waits for them, and re-layouts  39.9 us (17%)
  blocking collectives  27.7 us (11%)
  waiting for transfers between devices  22.1 us (9%)
    unnamed x93, local copies, waits for them, and re-layouts  39.8 us
    pallas_call x4, Pallas kernels, step(): pl.pallas_call(functools.partial(step_kernel, phase, names), grid=(4,), i...  34.2 us
    all_to_all x4, starting transfers between devices, exchange(): parts = lax.all_to_all(solve(terms, *solver), 'gx', 0, 0)  29.7 us
    all_to_all x3, blocking collectives, exchange(): terms = lax.all_to_all(out['message'], 'gy', 0, 0)  27.7 us
    all_to_all x1, starting transfers between devices, local(): gathered = lax.all_to_all(message, ('gx', 'gy'), 0, 0)  11.5 us
    ppermute x4, waiting for transfers between devices, exchange(): lax.ppermute(out['send_x_first'], 'gx', swap_first(lines[0]))  11.5 us
    pallas_call x1, Pallas kernels, fold(): pl.pallas_call(fold_kernel, grid=(size // slots,), in_specs=[pl.BlockSpec...  10.3 us
    pallas_call x4, Pallas kernels, solve(): pl.pallas_call(solve_kernel, out_shape=jax.ShapeDtypeStruct((lines, ROWS,...  9.72 us
  transfers between devices with their start and end apart: 25, of which 11 were waited for; matrix products, arithmetic and copies ran while one was open for 0% of the time, Pallas kernels for 10%

profile of v1, /device:TPU:1, one launch (start us, length us, event | category | flops | bytes accessed | tf_op | source)
XLA Modules:
  0.0 236.1 jit_solution(13228535869941146923)
XLA Ops:
  6.5 11.5 %all-to-all-start = ((f32[128,8,128]{2,1,0:T(8,128)}), f32[128,8,128]{2,1,0:T(8,128)S(1)}, u32[]{:S(2)}, u32[]{:S(2)}) async-start(f32[128,8,128]{2,1,0:T(8,128)} %get-tuple-element.53), calls=%async_computation | async-start | bytes 1048576 | tf_op jit(solution)/shard_map/all_to_all | solution.py:487
  18.0 3.7 %collective-permute-start = (f32[16,768]{1,0:T(8,128)}, f32[16,768]{1,0:T(8,128)S(1)}, u32[]{:S(2)}, u32[]{:S(2)}) collective-permute-start(f32[16,768]{1,0:T(8,128)} %get-tuple-element.54), channel_id=1, source_target_pairs={{0,1},{1,2},{2,3},{3,4},{4,5},{5,6},{6,7},{8,9},{9,10},{10,11},{11... | collective-permute-start | bytes 147464 | tf_op jit(solution)/shard_map/ppermute | solution.py:485
  21.7 3.2 %collective-permute-start.1 = (f32[16,768]{1,0:T(8,128)}, f32[16,768]{1,0:T(8,128)S(1)}, u32[]{:S(2)}, u32[]{:S(2)}) collective-permute-start(f32[16,768]{1,0:T(8,128)} %get-tuple-element.55), channel_id=1, source_target_pairs={{0,8},{8,16},{16,24},{24,32},{32,40},{40,48},{48,56},{56,64},{64,7... | collective-permute-start | bytes 147464 | tf_op jit(solution)/shard_map/ppermute | solution.py:486
  31.7 6.9 %all-to-all-start.2 = ((f32[16,40,256]{2,1,0:T(8,128)}), f32[16,40,256]{2,1,0:T(8,128)}, u32[]{:S(2)}, u32[]{:S(2)}) async-start(f32[16,40,256]{2,1,0:T(8,128)} %get-tuple-element.64), calls=%async_computation.2 | async-start | bytes 1310720 | tf_op jit(solution)/shard_map/all_to_all | solution.py:493
  39.3 10.3 %fold.1 = (bf16[1536,1536]{1,0:T(8,128)(2,1)S(1)}, bf16[1536,1536]{1,0:T(8,128)(2,1)}) custom-call(s32[2,384]{1,0:T(2,128)S(1)} %bitcast.25, f32[1536,1536]{1,0:T(8,128)} %bitcast.26), custom_call_target="tpu_custom_call" | custom-call | tf_op jit(solution)/shard_map/fold/pallas_call | solution.py:83
  52.0 8.0 %step0.1 = (f32[4,384,128]{2,1,0:T(8,128)S(1)}, f32[384,128]{1,0:T(8,128)}, f32[384,128]{1,0:T(8,128)}, f32[384,128]{1,0:T(8,128)}, f32[384,128]{1,0:T(8,128)S(1...) custom-call(s32[2]{0:T(128)S(1)} %pad_add_fusion.refs_0_, f32[768,128]{1,0:T(8,128)S(1)} %reshape.13.refs_1_, ...), custom_call_target="tpu_custom_call" | custom-call | tf_op jit(solution)/shard_map/step0/pallas_call | solution.py:409
  60.7 4.9 %all-to-all-start.1 = ((f32[8,40,128]{2,1,0:T(8,128)}), f32[8,40,128]{2,1,0:T(8,128)S(1)}, u32[]{:S(2)}, u32[]{:S(2)}) async-start(f32[8,40,128]{2,1,0:T(8,128)} %get-tuple-element.63), calls=%async_computation.1 | async-start | bytes 327680 | tf_op jit(solution)/shard_map/all_to_all | solution.py:503
  65.6 2.5 %spread.1 = (bf16[640,320]{1,0:T(8,128)(2,1)}, bf16[640,320]{1,0:T(8,128)(2,1)}) custom-call(f32[16,40,256]{2,1,0:T(8,128)} %all-to-all-done.2.received_ref, bf16[256,320]{1,0:T(8,128)(2,1)} %constant.28.clone.expand_ref), custom_call_target="tpu_custom_call" | custom-call | tf_op jit(solution)/shard_map/spread/pallas_call | solution.py:206
  68.1 3.1 %all-to-all-done.1.terms_ref = f32[8,40,128]{2,1,0:T(8,128)S(1)} async-done(((f32[8,40,128]{2,1,0:T(8,128)}), f32[8,40,128]{2,1,0:T(8,128)S(1)}, u32[]{:S(2)}, u32[]{:S(2)}) %all-to-all-start.1) | async-done | bytes 163872 | tf_op jit(solution)/shard_map/all_to_all | solution.py:503
  74.3 6.9 %all-to-all-start.3 = ((f32[16,40,128]{2,1,0:T(8,128)}), f32[16,40,128]{2,1,0:T(8,128)S(1)}, u32[]{:S(2)}, u32[]{:S(2)}) async-start(f32[16,40,128]{2,1,0:T(8,128)} %solve.4), calls=%async_computation.3 | async-start | bytes 655360 | tf_op jit(solution)/shard_map/all_to_all | solution.py:504
  87.1 2.9 %collective-permute-done.2.refs_6_ = f32[384,128]{1,0:T(8,128)S(1)} collective-permute-done((f32[384,128]{1,0:T(8,128)}, f32[384,128]{1,0:T(8,128)S(1)}, u32[]{:S(2)}, u32[]{:S(2)}) %collective-permute-start.2) | collective-permute-done | bytes 196640 | tf_op jit(solution)/shard_map/ppermute | solution.py:498
  92.2 7.2 %step1.1 = (f32[4,384,128]{2,1,0:T(8,128)S(1)}, f32[384,128]{1,0:T(8,128)S(1)}, f32[384,128]{1,0:T(8,128)S(1)}, f32[384,128]{1,0:T(8,128)S(1)}, f32[384,128]{1,0...) custom-call(s32[2]{0:T(128)S(1)} %pad_add_fusion.refs_0_, f32[16,40,128]{2,1,0:T(8,128)S(1)} %all-to-all-done.3.refs_1_, ...), custom_call_target="tpu_custom_call" | custom-call | tf_op jit(solution)/shard_map/step1/pallas_call | solution.py:409
  103.9 8.6 %all_to_all.50.terms_ref = f32[8,40,128]{2,1,0:T(8,128)} all-to-all(f32[8,40,128]{2,1,0:T(8,128)S(1)} %get-tuple-element.73), channel_id=1, replica_groups=mesh['gx'=16,'gy'=8] {'gy'}, dimensions={0} | all-to-all | bytes 327680 | tf_op jit(solution)/shard_map/all_to_all | solution.py:503
  112.5 2.4 %solve.5 = f32[16,40,128]{2,1,0:T(8,128)} custom-call(f32[8,40,128]{2,1,0:T(8,128)} %all_to_all.50.terms_ref, bf16[640,320]{1,0:T(8,128)(2,1)} %get-tuple-element.65.high_ref, bf16[640,320]{1,0:T(8,128)(2,1)} %get-tuple-element.66.low_ref), custom_call_target="tpu_custom_call" | custom-call | tf_op jit(solution)/shard_map/solve/pallas_call | solution.py:226
  114.9 8.0 %all-to-all-start.5 = ((f32[16,40,128]{2,1,0:T(8,128)}), f32[16,40,128]{2,1,0:T(8,128)S(1)}, u32[]{:S(2)}, u32[]{:S(2)}) async-start(f32[16,40,128]{2,1,0:T(8,128)} %solve.5), calls=%async_computation.5 | async-start | bytes 655360 | tf_op jit(solution)/shard_map/all_to_all | solution.py:504
  128.9 2.9 %collective-permute-done.6.refs_6_ = f32[384,128]{1,0:T(8,128)S(1)} collective-permute-done((f32[384,128]{1,0:T(8,128)}, f32[384,128]{1,0:T(8,128)S(1)}, u32[]{:S(2)}, u32[]{:S(2)}) %collective-permute-start.6) | collective-permute-done | bytes 196640 | tf_op jit(solution)/shard_map/ppermute | solution.py:498
  134.0 8.7 %step2.1 = (f32[4,384,128]{2,1,0:T(8,128)S(1)}, f32[384,128]{1,0:T(8,128)S(1)}, f32[384,128]{1,0:T(8,128)S(1)}, f32[384,128]{1,0:T(8,128)S(1)}, f32[384,128]{1,0...) custom-call(s32[2]{0:T(128)S(1)} %pad_add_fusion.refs_0_, ...), custom_call_target="tpu_custom_call" | custom-call | tf_op jit(solution)/shard_map/step2/pallas_call | solution.py:409
  147.3 8.6 %all_to_all.51.terms_ref = f32[8,40,128]{2,1,0:T(8,128)} all-to-all(f32[8,40,128]{2,1,0:T(8,128)S(1)} %get-tuple-element.81), channel_id=1, replica_groups=mesh['gx'=16,'gy'=8] {'gy'}, dimensions={0} | all-to-all | bytes 327680 | tf_op jit(solution)/shard_map/all_to_all | solution.py:503
  158.2 8.0 %all-to-all-start.7 = ((f32[16,40,128]{2,1,0:T(8,128)}), f32[16,40,128]{2,1,0:T(8,128)S(1)}, u32[]{:S(2)}, u32[]{:S(2)}) async-start(f32[16,40,128]{2,1,0:T(8,128)} %solve.6), calls=%async_computation.7 | async-start | bytes 655360 | tf_op jit(solution)/shard_map/all_to_all | solution.py:504
  172.2 2.9 %collective-permute-done.10.refs_6_ = f32[384,128]{1,0:T(8,128)S(1)} collective-permute-done((f32[384,128]{1,0:T(8,128)S(1)}, f32[384,128]{1,0:T(8,128)S(1)}, u32[]{:S(2)}, u32[]{:S(2)}) %collective-permute-start.10) | collective-permute-done | bytes 196640 | tf_op jit(solution)/shard_map/ppermute | solution.py:498
  182.7 10.2 %step3.1 = (f32[4,384,128]{2,1,0:T(8,128)S(1)}, f32[384,128]{1,0:T(8,128)S(1)}, f32[384,128]{1,0:T(8,128)S(1)}, f32[384,128]{1,0:T(8,128)S(1)}, f32[384,128]{1,0...) custom-call(s32[2]{0:T(128)S(1)} %pad_add_fusion.refs_0_, ...), custom_call_target="tpu_custom_call" | custom-call | tf_op jit(solution)/shard_map/step3/pallas_call | solution.py:409
  196.5 10.5 %all_to_all.52.terms_ref = f32[8,40,128]{2,1,0:T(8,128)} all-to-all(f32[8,40,128]{2,1,0:T(8,128)S(1)} %get-tuple-element.91), channel_id=1, replica_groups=mesh['gx'=16,'gy'=8] {'gy'}, dimensions={0} | all-to-all | bytes 327680 | tf_op jit(solution)/shard_map/all_to_all | solution.py:503
  209.4 6.9 %all-to-all-start.9 = ((f32[16,40,128]{2,1,0:T(8,128)}), f32[16,40,128]{2,1,0:T(8,128)S(1)}, u32[]{:S(2)}, u32[]{:S(2)}) async-start(f32[16,40,128]{2,1,0:T(8,128)} %solve.7), calls=%async_computation.9 | async-start | bytes 655360 | tf_op jit(solution)/shard_map/all_to_all | solution.py:504
  222.4 2.9 %collective-permute-done.14.refs_6_ = f32[384,128]{1,0:T(8,128)S(1)} collective-permute-done((f32[384,128]{1,0:T(8,128)}, f32[384,128]{1,0:T(8,128)S(1)}, u32[]{:S(2)}, u32[]{:S(2)}) %collective-permute-start.14) | collective-permute-done | bytes 196640 | tf_op jit(solution)/shard_map/ppermute | solution.py:498
  (137 shorter events, 83.7 us)
Async XLA Ops:
  6.5 25.2 %all-to-all-start = ((f32[128,8,128]{2,1,0:T(8,128)}), f32[128,8,128]{2,1,0:T(8,128)S(1)}, u32[]{:S(2)}, u32[]{:S(2)}) async-start(f32[128,8,128]{2,1,0:T(8,128)} %get-tuple-element.53), calls=%async_computation | async-start | bytes 1048576 | tf_op jit(solution)/shard_map/all_to_all | solution.py:487
  18.0 6.8 %collective-permute-start = (f32[16,768]{1,0:T(8,128)}, f32[16,768]{1,0:T(8,128)S(1)}, u32[]{:S(2)}, u32[]{:S(2)}) collective-permute-start(f32[16,768]{1,0:T(8,128)} %get-tuple-element.54), channel_id=1, source_target_pairs={{0,1},{1,2},{2,3},{3,4},{4,5},{5,6},{6,7},{8,9},{9,10},{10,11},{11... | collective-permute-start | bytes 147464 | tf_op jit(solution)/shard_map/ppermute | solution.py:485
  31.7 29.0 %all-to-all-start.2 = ((f32[16,40,256]{2,1,0:T(8,128)}), f32[16,40,256]{2,1,0:T(8,128)}, u32[]{:S(2)}, u32[]{:S(2)}) async-start(f32[16,40,256]{2,1,0:T(8,128)} %get-tuple-element.64), calls=%async_computation.2 | async-start | bytes 1310720 | tf_op jit(solution)/shard_map/all_to_all | solution.py:493
  60.7 10.5 %all-to-all-start.1 = ((f32[8,40,128]{2,1,0:T(8,128)}), f32[8,40,128]{2,1,0:T(8,128)S(1)}, u32[]{:S(2)}, u32[]{:S(2)}) async-start(f32[8,40,128]{2,1,0:T(8,128)} %get-tuple-element.63), calls=%async_computation.1 | async-start | bytes 327680 | tf_op jit(solution)/shard_map/all_to_all | solution.py:503
  74.3 17.9 %all-to-all-start.3 = ((f32[16,40,128]{2,1,0:T(8,128)}), f32[16,40,128]{2,1,0:T(8,128)S(1)}, u32[]{:S(2)}, u32[]{:S(2)}) async-start(f32[16,40,128]{2,1,0:T(8,128)} %solve.4), calls=%async_computation.3 | async-start | bytes 655360 | tf_op jit(solution)/shard_map/all_to_all | solution.py:504
  81.2 8.8 %collective-permute-start.2 = (f32[384,128]{1,0:T(8,128)}, f32[384,128]{1,0:T(8,128)S(1)}, u32[]{:S(2)}, u32[]{:S(2)}) collective-permute-start(f32[384,128]{1,0:T(8,128)} %get-tuple-element.69), channel_id=1, source_target_pairs={{0,8},{8,0},{16,24},{24,16},{32,40},{40,32},{48,56},{56,48},{64,72... | collective-permute-start | bytes 589832 | tf_op jit(solution)/shard_map/ppermute | solution.py:498
  82.5 7.5 %collective-permute-start.3 = (f32[384,128]{1,0:T(8,128)}, f32[384,128]{1,0:T(8,128)S(1)}, u32[]{:S(2)}, u32[]{:S(2)}) collective-permute-start(f32[384,128]{1,0:T(8,128)} %get-tuple-element.70), channel_id=1, source_target_pairs={{8,16},{16,8},{24,32},{32,24},{40,48},{48,40},{56,64},{64,56},{72,... | collective-permute-start | bytes 589832 | tf_op jit(solution)/shard_map/ppermute | solution.py:499
  83.2 6.8 %collective-permute-start.4 = (f32[384,128]{1,0:T(8,128)}, f32[384,128]{1,0:T(8,128)S(1)}, u32[]{:S(2)}, u32[]{:S(2)}) collective-permute-start(f32[384,128]{1,0:T(8,128)} %get-tuple-element.71), channel_id=1, source_target_pairs={{0,1},{1,0},{2,3},{3,2},{4,5},{5,4},{6,7},{7,6},{8,9},{9,8},{10,11... | collective-permute-start | bytes 589832 | tf_op jit(solution)/shard_map/ppermute | solution.py:500
  85.0 7.2 %collective-permute-start.5 = (f32[384,128]{1,0:T(8,128)}, f32[384,128]{1,0:T(8,128)S(1)}, u32[]{:S(2)}, u32[]{:S(2)}) collective-permute-start(f32[384,128]{1,0:T(8,128)} %copy-done.33), channel_id=1, source_target_pairs={{1,2},{2,1},{3,4},{4,3},{5,6},{6,5},{9,10},{10,9},{11,12},{12,11},... | collective-permute-start | bytes 589832 | tf_op jit(solution)/shard_map/ppermute | solution.py:501
  114.9 19.0 %all-to-all-start.5 = ((f32[16,40,128]{2,1,0:T(8,128)}), f32[16,40,128]{2,1,0:T(8,128)S(1)}, u32[]{:S(2)}, u32[]{:S(2)}) async-start(f32[16,40,128]{2,1,0:T(8,128)} %solve.5), calls=%async_computation.5 | async-start | bytes 655360 | tf_op jit(solution)/shard_map/all_to_all | solution.py:504
  122.9 8.8 %collective-permute-start.6 = (f32[384,128]{1,0:T(8,128)}, f32[384,128]{1,0:T(8,128)S(1)}, u32[]{:S(2)}, u32[]{:S(2)}) collective-permute-start(f32[384,128]{1,0:T(8,128)} %copy-done.43), channel_id=1, source_target_pairs={{0,8},{8,0},{16,24},{24,16},{32,40},{40,32},{48,56},{56,48},{64,72... | collective-permute-start | bytes 589832 | tf_op jit(solution)/shard_map/ppermute | solution.py:498
  124.3 7.5 %collective-permute-start.7 = (f32[384,128]{1,0:T(8,128)}, f32[384,128]{1,0:T(8,128)S(1)}, u32[]{:S(2)}, u32[]{:S(2)}) collective-permute-start(f32[384,128]{1,0:T(8,128)} %copy-done.42), channel_id=1, source_target_pairs={{8,16},{16,8},{24,32},{32,24},{40,48},{48,40},{56,64},{64,56},{72,... | collective-permute-start | bytes 589832 | tf_op jit(solution)/shard_map/ppermute | solution.py:499
  124.9 6.8 %collective-permute-start.8 = (f32[384,128]{1,0:T(8,128)}, f32[384,128]{1,0:T(8,128)S(1)}, u32[]{:S(2)}, u32[]{:S(2)}) collective-permute-start(f32[384,128]{1,0:T(8,128)} %copy-done.40), channel_id=1, source_target_pairs={{0,1},{1,0},{2,3},{3,2},{4,5},{5,4},{6,7},{7,6},{8,9},{9,8},{10,11... | collective-permute-start | bytes 589832 | tf_op jit(solution)/shard_map/ppermute | solution.py:500
  126.8 7.2 %collective-permute-start.9 = (f32[384,128]{1,0:T(8,128)}, f32[384,128]{1,0:T(8,128)S(1)}, u32[]{:S(2)}, u32[]{:S(2)}) collective-permute-start(f32[384,128]{1,0:T(8,128)} %copy-done.38), channel_id=1, source_target_pairs={{1,2},{2,1},{3,4},{4,3},{5,6},{6,5},{9,10},{10,9},{11,12},{12,11},... | collective-permute-start | bytes 589832 | tf_op jit(solution)/shard_map/ppermute | solution.py:501
  158.2 19.7 %all-to-all-start.7 = ((f32[16,40,128]{2,1,0:T(8,128)}), f32[16,40,128]{2,1,0:T(8,128)S(1)}, u32[]{:S(2)}, u32[]{:S(2)}) async-start(f32[16,40,128]{2,1,0:T(8,128)} %solve.6), calls=%async_computation.7 | async-start | bytes 655360 | tf_op jit(solution)/shard_map/all_to_all | solution.py:504
  166.2 8.8 %collective-permute-start.10 = (f32[384,128]{1,0:T(8,128)S(1)}, f32[384,128]{1,0:T(8,128)S(1)}, u32[]{:S(2)}, u32[]{:S(2)}) collective-permute-start(f32[384,128]{1,0:T(8,128)S(1)} %get-tuple-element.83), channel_id=1, source_target_pairs={{0,8},{8,0},{16,24},{24,16},{32,40},{40,32},{48,56},{56,48},{64,72... | collective-permute-start | bytes 589832 | tf_op jit(solution)/shard_map/ppermute | solution.py:498
  167.6 8.1 %collective-permute-start.11 = (f32[384,128]{1,0:T(8,128)}, f32[384,128]{1,0:T(8,128)S(1)}, u32[]{:S(2)}, u32[]{:S(2)}) collective-permute-start(f32[384,128]{1,0:T(8,128)} %copy-done.41), channel_id=1, source_target_pairs={{8,16},{16,8},{24,32},{32,24},{40,48},{48,40},{56,64},{64,56},{72,... | collective-permute-start | bytes 589832 | tf_op jit(solution)/shard_map/ppermute | solution.py:499
  168.3 8.1 %collective-permute-start.12 = (f32[384,128]{1,0:T(8,128)}, f32[384,128]{1,0:T(8,128)S(1)}, u32[]{:S(2)}, u32[]{:S(2)}) collective-permute-start(f32[384,128]{1,0:T(8,128)} %copy-done.39), channel_id=1, source_target_pairs={{0,1},{1,0},{2,3},{3,2},{4,5},{5,4},{6,7},{7,6},{8,9},{9,8},{10,11... | collective-permute-start | bytes 589832 | tf_op jit(solution)/shard_map/ppermute | solution.py:500
  170.1 7.2 %collective-permute-start.13 = (f32[384,128]{1,0:T(8,128)}, f32[384,128]{1,0:T(8,128)S(1)}, u32[]{:S(2)}, u32[]{:S(2)}) collective-permute-start(f32[384,128]{1,0:T(8,128)} %copy-done.37), channel_id=1, source_target_pairs={{1,2},{2,1},{3,4},{4,3},{5,6},{6,5},{9,10},{10,9},{11,12},{12,11},... | collective-permute-start | bytes 589832 | tf_op jit(solution)/shard_map/ppermute | solution.py:501
  209.4 18.7 %all-to-all-start.9 = ((f32[16,40,128]{2,1,0:T(8,128)}), f32[16,40,128]{2,1,0:T(8,128)S(1)}, u32[]{:S(2)}, u32[]{:S(2)}) async-start(f32[16,40,128]{2,1,0:T(8,128)} %solve.7), calls=%async_computation.9 | async-start | bytes 655360 | tf_op jit(solution)/shard_map/all_to_all | solution.py:504
  216.4 8.8 %collective-permute-start.14 = (f32[384,128]{1,0:T(8,128)}, f32[384,128]{1,0:T(8,128)S(1)}, u32[]{:S(2)}, u32[]{:S(2)}) collective-permute-start(f32[384,128]{1,0:T(8,128)} %copy-done.36), channel_id=1, source_target_pairs={{0,8},{8,0},{16,24},{24,16},{32,40},{40,32},{48,56},{56,48},{64,72... | collective-permute-start | bytes 589832 | tf_op jit(solution)/shard_map/ppermute | solution.py:498
  217.7 7.5 %collective-permute-start.15 = (f32[384,128]{1,0:T(8,128)}, f32[384,128]{1,0:T(8,128)S(1)}, u32[]{:S(2)}, u32[]{:S(2)}) collective-permute-start(f32[384,128]{1,0:T(8,128)} %copy-done.35), channel_id=1, source_target_pairs={{8,16},{16,8},{24,32},{32,24},{40,48},{48,40},{56,64},{64,56},{72,... | collective-permute-start | bytes 589832 | tf_op jit(solution)/shard_map/ppermute | solution.py:499
  218.4 7.5 %collective-permute-start.16 = (f32[384,128]{1,0:T(8,128)}, f32[384,128]{1,0:T(8,128)S(1)}, u32[]{:S(2)}, u32[]{:S(2)}) collective-permute-start(f32[384,128]{1,0:T(8,128)} %copy-done.34), channel_id=1, source_target_pairs={{0,1},{1,0},{2,3},{3,2},{4,5},{5,4},{6,7},{7,6},{8,9},{9,8},{10,11... | collective-permute-start | bytes 589832 | tf_op jit(solution)/shard_map/ppermute | solution.py:500
  220.2 7.2 %collective-permute-start.17 = (f32[384,128]{1,0:T(8,128)}, f32[384,128]{1,0:T(8,128)S(1)}, u32[]{:S(2)}, u32[]{:S(2)}) collective-permute-start(f32[384,128]{1,0:T(8,128)} %copy-done.32), channel_id=1, source_target_pairs={{1,2},{2,1},{3,4},{4,3},{5,6},{6,5},{9,10},{10,9},{11,12},{12,11},... | collective-permute-start | bytes 589832 | tf_op jit(solution)/shard_map/ppermute | solution.py:501
  (46 other events, 98.7 us)

commit v2 on v0

v2 whole, which is shorter than its diff:
```python
import functools
from types import SimpleNamespace

import jax
import jax.numpy as jnp
import numpy as np
from jax import lax
from jax.experimental import pallas as pl
from jax.experimental.pallas import tpu as pltpu
from jax.sharding import PartitionSpec as P

F32 = jnp.float32
BF16 = jnp.bfloat16
HIGHEST = lax.Precision.HIGHEST
MODES = 6
GROUP = 8
MEMBERS = 5
ROWS = GROUP * MEMBERS
TROWS = 48
LAST = 3
FLAGS = 6
KEPT = 3 * GROUP
TAIL = 16
STEP_MB = 16
NORM_ROW, ENERGY_ROW, CROSS_ROW = 6, 7, 14


VMEM_SPEC = pl.BlockSpec(memory_space=pltpu.VMEM)
SMEM_SPEC = pl.BlockSpec(memory_space=pltpu.SMEM)


def params(megabytes):
    return pltpu.CompilerParams(vmem_limit_bytes=megabytes * 1024 * 1024)


def split(value):
    high = value.astype(BF16)
    low = (value - high.astype(F32)).astype(BF16)
    return high, low


def mm(left, right):
    return jnp.dot(left, right, preferred_element_type=F32)


def both(value):
    high, low = split(value)
    return jnp.concatenate([high, low], axis=1)


def mm3(left_high, left_low, pair):
    columns = pair.shape[1] // 2
    wide = mm(left_high, pair)
    return wide[:, :columns] + wide[:, columns:] + mm(left_low, pair[:, :columns])


def pack_kernel(rows_ref, modes_ref, free_ref, rhs_ref, east_ref, south_ref, message_ref):
    slots = free_ref.shape[1]
    for face, out in enumerate((east_ref, south_ref)):
        out[...] = jnp.zeros_like(out)
        out[0:MODES, :] = rows_ref[0]
        out[6:7, :slots] = free_ref[face : face + 1, :].astype(F32)
        for side in range(2):
            out[8 : 8 + MODES, side * slots : (side + 1) * slots] = modes_ref[face, side]
    message_ref[...] = jnp.zeros_like(message_ref)
    for peer in range(message_ref.shape[0]):
        message_ref[peer, 0:MODES, :] = rhs_ref[...]


def pack(rows, modes, free, rhs, peers):
    width = rows.shape[-1]
    return pl.pallas_call(
        pack_kernel,
        in_specs=[VMEM_SPEC] * 4,
        out_specs=[VMEM_SPEC] * 3,
        out_shape=[
            jax.ShapeDtypeStruct((16, width), F32),
            jax.ShapeDtypeStruct((16, width), F32),
            jax.ShapeDtypeStruct((peers, GROUP, rhs.shape[-1]), F32),
        ],
        compiler_params=params(8),
        name="pack",
    )(rows, modes, free, rhs)


def frame_kernel(
    lines, place_ref, modes_ref, free_ref, match_ref, rows_ref, west_ref, north_ref, rhs_ref,
    mask_ref, t_high_ref, t_low_ref, g_high_ref, g_low_ref, gives_ref, takes_ref,
    coarse_ref, pieces_ref, table_ref, held_ref,
):
    slots = free_ref.shape[1]
    cases = mask_ref.shape[1]
    span = MODES * lines[1]
    no_north, no_west = place_ref[4] != 0, place_ref[5] != 0
    west = jnp.where(no_west, 0.0, west_ref[...])
    north = jnp.where(no_north, 0.0, north_ref[...])
    table_ref[...] = jnp.zeros_like(table_ref)
    masks = [
        free_ref[0:1, :].astype(F32), free_ref[1:2, :].astype(F32),
        west[6:7, :slots], north[6:7, :slots],
    ]
    entries = [
        (0, 0, modes_ref[0, 0]), (0, 1, modes_ref[1, 0]),
        (1, 0, modes_ref[0, 1]), (2, 1, modes_ref[1, 1]),
        (3, 2, west[8 : 8 + MODES, :slots]), (0, 2, west[8 : 8 + MODES, slots : 2 * slots]),
        (4, 3, north[8 : 8 + MODES, :slots]), (0, 3, north[8 : 8 + MODES, slots : 2 * slots]),
    ]
    for member, face, values in entries:
        table_ref[member * GROUP : member * GROUP + MODES, face * slots : (face + 1) * slots] = (
            values * masks[face]
        )
    table = table_ref[...]
    high, low = split(table[:TROWS])
    t_high_ref[...] = high
    t_low_ref[...] = low
    high, low = split(table.T)
    g_high_ref[...] = high
    g_low_ref[...] = low
    for face in range(4):
        spread = jnp.broadcast_to(masks[face], (cases, slots))
        mask_ref[face * slots : (face + 1) * slots, :] = spread.T
    order = lax.broadcasted_iota(jnp.int32, (slots, slots), 0)
    for side in range(2):
        moves = jnp.where(order == match_ref[side : side + 1, :], 1.0, 0.0)
        gives_ref[side] = moves.astype(BF16)
        takes_ref[side] = moves.T.astype(BF16)
    coarse_ref[...] = jnp.zeros_like(coarse_ref)
    members = [rows_ref[0], rows_ref[1], rows_ref[2], west[0:MODES, :], north[0:MODES, :]]
    for member, values in enumerate(members):
        coarse_ref[member * GROUP : member * GROUP + MODES, :] = values
    edge = jnp.zeros((ROWS, span), F32)
    padded = jnp.concatenate([edge, coarse_ref[...], edge], axis=1)
    for source in range(lines[1]):
        held_ref[source * MODES : (source + 1) * MODES, :] = rhs_ref[source, 0:MODES]
    tail = 3 * span - cases
    for line in range(lines[0]):
        first = line * span
        pieces_ref[line, 0:ROWS] = padded[:, first : first + cases]
        last = padded[:, first + cases : first + 3 * span]
        pieces_ref[line, ROWS : ROWS + GROUP] = jnp.zeros((GROUP, cases), F32)
        for member in range(MEMBERS):
            pieces_ref[line, ROWS : ROWS + GROUP, member * tail : (member + 1) * tail] = last[
                member * GROUP : (member + 1) * GROUP
            ]
        pieces_ref[line, ROWS + GROUP :] = held_ref[...]


def frame(lines, place, modes, free, match, rows, west, north, rhs):
    slots = free.shape[1]
    size = 4 * slots
    width = rows.shape[-1]
    cases = rhs.shape[-1]
    span = MODES * lines[1]
    return pl.pallas_call(
        functools.partial(frame_kernel, lines),
        in_specs=[SMEM_SPEC] + [VMEM_SPEC] * 7,
        out_specs=[VMEM_SPEC] * 9,
        out_shape=[
            jax.ShapeDtypeStruct((size, cases), F32),
            jax.ShapeDtypeStruct((TROWS, size), BF16),
            jax.ShapeDtypeStruct((TROWS, size), BF16),
            jax.ShapeDtypeStruct((size, 128), BF16),
            jax.ShapeDtypeStruct((size, 128), BF16),
            jax.ShapeDtypeStruct((2, slots, slots), BF16),
            jax.ShapeDtypeStruct((2, slots, slots), BF16),
            jax.ShapeDtypeStruct((ROWS, width), F32),
            jax.ShapeDtypeStruct((lines[0], ROWS + GROUP + span, cases), F32),
        ],
        scratch_shapes=[pltpu.VMEM((128, size), F32), pltpu.VMEM((span, cases), F32)],
        compiler_params=params(12),
        name="frame",
    )(place, modes, free, match, rows, west, north, rhs)


def expansion(lines):
    span = MODES * lines[1]
    out = np.zeros((256, lines[1] * ROWS), np.float32)
    for source in range(lines[1]):
        places = [(0, source), (0, source + 1), (1, source), (0, source - 1), (-1, source)]
        for member, (down, column) in enumerate(places):
            if 0 <= column < lines[1]:
                for mode in range(MODES):
                    at = span * (1 + down) + MODES * column + mode
                    out[at, source * ROWS + member * GROUP + mode] = 1.0
    return jnp.asarray(out, BF16)


def spread_kernel(
    received_ref, expand_ref, operator_ref,
    high_ref, low_ref, a_high_ref, a_low_ref, tail_ref, held_ref, sems,
):
    size = operator_ref.shape[0]
    count = sems.shape[0]
    block = size // count
    copies = []
    for part in range(count):
        rows = pl.ds(part * block, block)
        copies.append(
            pltpu.make_async_copy(operator_ref.at[rows], held_ref.at[rows], sems.at[part])
        )
        copies[-1].start()
    lines, _, cases = received_ref.shape
    tail = TAIL
    tail_ref[...] = jnp.zeros_like(tail_ref)
    packed = received_ref[:, ROWS : ROWS + GROUP, :]
    for member in range(MEMBERS):
        tail_ref[:, member * GROUP : (member + 1) * GROUP, 0:tail] = packed[
            :, :, member * tail : (member + 1) * tail
        ]
    head = split(received_ref[:, 0:ROWS, :].reshape(lines * ROWS, cases))
    rest = split(tail_ref[...].reshape(lines * ROWS, cases))
    for first, last, out in zip(head, rest, (high_ref, low_ref)):
        result = mm(first, expand_ref[0:cases]) + mm(last, expand_ref[cases : 2 * cases])
        out[...] = result.astype(BF16)
    for part in range(count):
        copies[part].wait()
        rows = slice(part * block, (part + 1) * block)
        high, low = split(held_ref[rows, :])
        a_high_ref[rows, :] = high
        a_low_ref[rows, :] = low


def spread(received, expand, operator):
    lines, _, cases = received.shape
    shape = (lines * ROWS, expand.shape[1])
    size = operator.shape[0]
    return pl.pallas_call(
        spread_kernel,
        in_specs=[VMEM_SPEC] * 2 + [pl.BlockSpec(memory_space=pl.ANY)],
        out_specs=[VMEM_SPEC] * 4,
        out_shape=[jax.ShapeDtypeStruct(shape, BF16)] * 2
        + [jax.ShapeDtypeStruct((size, size), BF16)] * 2,
        scratch_shapes=[
            pltpu.VMEM((lines, ROWS, cases), F32), pltpu.VMEM((size, size), F32),
            pltpu.SemaphoreType.DMA((8,)),
        ],
        compiler_params=params(40),
        name="spread",
    )(received, expand, operator)


def solve_kernel(terms_ref, high_ref, low_ref, out_ref):
    terms = terms_ref[...]
    peers, rows, cases = terms.shape
    result = mm3(high_ref[...], low_ref[...], both(terms.reshape(peers * rows, cases)))
    kept = out_ref.shape[1]
    result = result.reshape(out_ref.shape[0], rows, cases)
    total = jnp.sum(terms, axis=0)
    place = lax.broadcasted_iota(jnp.int32, (rows, cases), 0)
    scalar = (place % GROUP) >= MODES
    out_ref[...] = jnp.where(scalar[None], total[None], result)[:, :kept]


def solve(terms, high, low, kept):
    lines = high.shape[0] // ROWS
    return pl.pallas_call(
        solve_kernel,
        in_specs=[VMEM_SPEC] * 3,
        out_specs=VMEM_SPEC,
        out_shape=jax.ShapeDtypeStruct((lines, kept, terms.shape[2]), F32),
        compiler_params=params(8),
        name="solve",
    )(terms, high, low)


def lift(alpha, g_high_ref, g_low_ref):
    filler = jnp.zeros((g_high_ref.shape[1] - alpha.shape[0], alpha.shape[1]), F32)
    pair = both(jnp.concatenate([alpha, filler], axis=0))
    return mm3(g_high_ref[...], g_low_ref[...], pair)


def field_image(r):
    even_x, even_y = r.parity[0] == 0, r.parity[1] == 0
    last_x, last_y = r.parity[2] != 0, r.parity[3] != 0
    slots = r.z_y.shape[1]

    def face(number, own, received):
        mask = r.mask[number * slots : (number + 1) * slots, :]
        return mask * (own + received)

    x_first, x_second = r.x_first[...], r.x_second[...]
    y_first, y_second = r.y_first[...], r.y_second[...]
    result = [
        face(0, r.z_y[0], jnp.where(even_y, y_first, jnp.where(last_y, 0.0, y_second))),
        face(1, r.z_x[0], jnp.where(even_x, x_first, jnp.where(last_x, 0.0, x_second))),
        face(2, r.z_y[1], jnp.where(even_y, y_second, y_first)),
        face(3, r.z_x[1], jnp.where(even_x, x_second, x_first)),
    ]
    return jnp.concatenate(result, axis=0)


def owned_image(r):
    last_x, last_y = r.parity[2] != 0, r.parity[3] != 0
    half = r.mask.shape[0] // 2
    east = r.z_y[0] + jnp.where(last_y, 0.0, r.y_first[...])
    south = r.z_x[0] + jnp.where(last_x, 0.0, r.x_first[...])
    return r.mask[:half, :] * jnp.concatenate([east, south], axis=0)


def member_alpha(total):
    place = lax.broadcasted_iota(jnp.int32, total.shape, 0)
    return jnp.where((place % GROUP) < MODES, total, 0.0)


def apply_faces(r, side, z_ref, first_ref, second_ref, loaded):
    slots = r.gives.shape[1]
    for index in range(2):
        face = side + 2 * index
        rows = slice(face * slots, (face + 1) * slots)
        out = mm3(r.a_high[rows, :], r.a_low[rows, :], r.pair[...])
        if index == 0 and loaded:
            out = out - r.loads[side]
        if index == 1:
            moved = mm(r.gives[side], both(out))
            columns = out.shape[1]
            out = -(moved[:, :columns] + moved[:, columns:])
        z_ref[index] = out
    if second_ref is None:
        first_ref[...] = z_ref[1]
    else:
        flip = r.parity[1 - side]
        first_ref[...] = z_ref[flip]
        second_ref[...] = z_ref[1 - flip]


def update_kernel(phase, names, *refs):
    r = SimpleNamespace(**dict(zip(names, refs)))
    slots = r.gives.shape[1]
    half = 2 * slots
    if phase == 0:
        lines, _, cases = r.received.shape
        span = r.rhs.shape[0] // lines
        for line in range(lines):
            r.rhs[line * span : (line + 1) * span, :] = r.received[line, ROWS + GROUP :]
        alpha = jnp.dot(
            r.coarse[...], r.rhs[...], precision=HIGHEST, preferred_element_type=F32
        )
        field = lift(alpha, r.g_high, r.g_low)
        r.lam_out[...] = field[:half]
    else:
        total = jnp.sum(r.parts[...], axis=0)
        moved = field_image(r) - lift(member_alpha(total), r.g_high, r.g_low)
        if phase == 1:
            field = moved
        elif phase == 2:
            norm = total[NORM_ROW : NORM_ROW + 1, :]
            energy = total[ENERGY_ROW : ENERGY_ROW + 1, :]
            step = norm / energy
            field = r.p[...] + step * moved
            r.q_out[...] = moved
            for place, value in enumerate((norm, energy, step)):
                r.scal_out[place : place + 1, :] = value
        else:
            step, beta, curvature, norm = step_terms(total, r.scal)
            image_p = moved + beta * r.q[...]
            field = r.p[...] + step * image_p
            r.q_out[...] = image_p
            for place, value in enumerate((norm, curvature, step, beta)):
                r.scal_out[place : place + 1, :] = value
        r.p_out[...] = field
    pair = both(field)
    r.pair[:half, :] = pair[:half]
    for side in range(2):
        rows = slice((2 + side) * slots, (3 + side) * slots)
        r.pair[rows, :] = (-mm(r.takes[side], pair[rows])).astype(BF16)
    second = None if phase == LAST else r.send_x_second
    apply_faces(r, 1, r.z_x_out, r.send_x_first, second, phase == 0)


def apply_kernel(phase, names, *refs):
    r = SimpleNamespace(**dict(zip(names, refs)))
    second = None if phase == LAST else r.send_y_second
    apply_faces(r, 0, r.z_y_out, r.send_y_first, second, phase == 0)


def terms_kernel(phase, names, *refs):
    r = SimpleNamespace(**dict(zip(names, refs)))
    slots = r.z_x.shape[1]
    half = 2 * slots
    terms = norm = energy = cross = 0.0
    if phase == 2:
        r.lam_out[...] = r.lam[...] + r.scal[2:3, :] * r.d[:half, :]
    if phase == 3:
        beta = r.scal[3:4, :]
        direction = r.p_old[...] + beta * r.d[...]
        r.d_out[...] = direction
        r.lam_out[...] = r.lam[...] + r.scal[2:3, :] * direction[:half]
    for face in range(4):
        rows = slice(face * slots, (face + 1) * slots)
        own, at = (r.z_x if face % 2 else r.z_y), face // 2
        out = own[at]
        terms = terms + mm3(r.t_high[:, rows], r.t_low[:, rows], both(out))
        if phase >= 1:
            mine = r.p[rows, :]
            energy = energy + jnp.sum(mine * out, axis=0, keepdims=True)
            if face < 2:
                norm = norm + jnp.sum(mine * mine, axis=0, keepdims=True)
        if phase >= 2:
            image = (r.z_x_old if face % 2 else r.z_y_old)[at]
            towards = r.d[rows, :]
            if phase == 3:
                image = image + beta * (r.z_x_older if face % 2 else r.z_y_older)[at]
                towards = r.d_out[rows, :]
            cross = cross + jnp.sum(mine * image + towards * out, axis=0, keepdims=True)
    terms = terms[0:ROWS, :]
    if phase >= 1:
        place = lax.broadcasted_iota(jnp.int32, terms.shape, 0)
        terms = jnp.where(place == NORM_ROW, norm, terms)
        terms = jnp.where(place == ENERGY_ROW, energy, terms)
        if phase >= 2:
            terms = jnp.where(place == CROSS_ROW, cross, terms)
    for peer in range(r.message.shape[0]):
        r.message[peer] = terms


def step_terms(total, scal_ref):
    norm = total[NORM_ROW : NORM_ROW + 1, :]
    energy = total[ENERGY_ROW : ENERGY_ROW + 1, :]
    cross = total[CROSS_ROW : CROSS_ROW + 1, :]
    beta = norm / scal_ref[0:1, :]
    curvature = energy + beta * cross + beta * beta * scal_ref[1:2, :]
    return norm / curvature, beta, curvature, norm


def call(kernel, name, inputs, shapes, scratch=None, halves=(), flops=0):
    scratch = scratch or {}
    keys = list(inputs) + list(shapes) + list(scratch)
    outs = pl.pallas_call(
        functools.partial(kernel, keys),
        in_specs=[VMEM_SPEC if v.shape != (FLAGS,) else SMEM_SPEC for v in inputs.values()],
        out_specs=[VMEM_SPEC] * len(shapes),
        out_shape=[
            jax.ShapeDtypeStruct(shape, BF16 if shape in halves else F32)
            for shape in shapes.values()
        ],
        scratch_shapes=list(scratch.values()),
        compiler_params=params(STEP_MB),
        cost_estimate=pl.CostEstimate(flops=flops, bytes_accessed=4096, transcendentals=0),
        name=name,
    )(*inputs.values())
    return SimpleNamespace(**dict(zip(shapes, outs)))


def step(phase, lines, table, before, exchange, state):
    slots = table.gives.shape[1]
    size = 4 * slots
    cases = table.mask.shape[1]
    face, pair, field = (slots, cases), (2, slots, cases), (size, cases)
    wide = (size, 2 * cases)
    half_flops = size * size * cases * 4
    inputs = dict(
        parity=table.parity, a_high=table.a_high, a_low=table.a_low, gives=table.gives,
        takes=table.takes, g_high=table.g_high, g_low=table.g_low,
    )
    inputs.update(state if before is None else dict(received_by(before), mask=table.mask))
    if phase == 2:
        inputs.update(p=state.p)
    if phase == 3:
        inputs.update(p=state.p, q=state.q, scal=state.scal)
    shapes = dict(pair=wide, z_x_out=pair, send_x_first=face)
    if phase < LAST:
        shapes.update(send_x_second=face)
    scratch = {}
    if phase == 0:
        shapes.update(lam_out=(2 * slots, cases))
        scratch = dict(rhs=pltpu.VMEM((MODES * lines[0] * lines[1], cases), F32))
    else:
        shapes.update(p_out=field)
    if phase >= 2:
        shapes.update(q_out=field, scal_out=(8, cases))
    update = call(
        functools.partial(update_kernel, phase), f"update{phase}", inputs, shapes, scratch,
        (wide,), half_flops,
    )
    inputs = dict(
        parity=table.parity, a_high=table.a_high, a_low=table.a_low, gives=table.gives,
        pair=update.pair,
    )
    if phase == 0:
        inputs.update(loads=state["loads"])
    shapes = dict(z_y_out=pair, send_y_first=face)
    if phase < LAST:
        shapes.update(send_y_second=face)
    apply = call(
        functools.partial(apply_kernel, phase), f"apply{phase}", inputs, shapes, flops=half_flops
    )
    inputs = dict(t_high=table.t_high, t_low=table.t_low, z_x=update.z_x_out, z_y=apply.z_y_out)
    shapes = dict(message=(lines[1], ROWS, cases))
    if phase:
        inputs.update(p=update.p_out)
    if phase >= 2:
        inputs.update(
            scal=update.scal_out, lam=state.lam, d=state.d, z_x_old=before.z_x, z_y_old=before.z_y
        )
        shapes.update(lam_out=(2 * slots, cases))
    if phase == 3:
        inputs.update(p_old=state.p, z_x_older=state.z_x_old, z_y_older=state.z_y_old)
        shapes.update(d_out=field)
    terms = call(
        functools.partial(terms_kernel, phase), f"terms{phase}", inputs, shapes,
        flops=half_flops // 4,
    )
    out = SimpleNamespace(**{**vars(update), **vars(apply), **vars(terms)})
    exchange(out, phase == LAST)
    return out


def received_by(out):
    inputs = dict(parts=out.parts, z_x=out.z_x, z_y=out.z_y, x_first=out.x_first, y_first=out.y_first)
    if out.x_second is not None:
        inputs.update(x_second=out.x_second, y_second=out.y_second)
    return inputs


def final_kernel(names, *refs):
    r = SimpleNamespace(**dict(zip(names, refs)))
    half = r.lam.shape[0]
    top = slice(0, half)
    total = jnp.sum(r.parts[...], axis=0)
    moved = owned_image(r) - lift(
        member_alpha(total), r.g_high.at[top], r.g_low.at[top]
    )
    step_size, beta, _, _ = step_terms(total, r.scal)
    direction = r.p[top, :] + beta * r.d[top, :]
    r.lam_out[...] = r.lam[...] + step_size * direction
    r.p_out[...] = r.p[top, :] + step_size * (moved + beta * r.q[top, :])


def shift(peers, by):
    return [(i, (i + by) % peers) for i in range(peers)]


def swap_first(peers):
    return [(i, i ^ 1) for i in range(peers)]


def swap_second(peers):
    return [(i, (i + (1 if i % 2 else -1)) % peers) for i in range(peers)]


def local(dual_ops, loads, coarse_rhs, coarse_modes, free_mask, face_match, coarse_rows):
    operator = dual_ops[0, 0]
    modes = coarse_modes[0, 0]
    free = free_mask[0, 0]
    rows = coarse_rows[0, 0]
    slots, cases = loads.shape[-2:]
    lines = (lax.axis_size("gx"), lax.axis_size("gy"))
    peers = lines[0] * lines[1]
    at = (lax.axis_index("gx"), lax.axis_index("gy"))
    parity = jnp.stack(
        [
            at[0] % 2, at[1] % 2, at[0] == lines[0] - 1, at[1] == lines[1] - 1,
            at[0] == 0, at[1] == 0,
        ]
    ).astype(jnp.int32)

    pack_east, pack_south, message = pack(rows, modes, free, coarse_rhs[0, 0], lines[1])
    west = lax.ppermute(pack_east, "gy", shift(lines[1], 1))
    north = lax.ppermute(pack_south, "gx", shift(lines[0], 1))
    gathered = lax.all_to_all(message, "gy", 0, 0)
    gathered, west, north, parity = lax.optimization_barrier((gathered, west, north, parity))
    mask, t_high, t_low, g_high, g_low, gives, takes, coarse, pieces = frame(
        lines, parity, modes, free, face_match[0, 0], rows, west, north, gathered
    )
    received = lax.all_to_all(pieces, "gx", 0, 0)
    *solver, a_high, a_low = spread(received, expansion(lines), operator)
    table = SimpleNamespace(
        parity=parity, a_high=a_high, a_low=a_low, mask=mask, t_high=t_high, t_low=t_low,
        g_high=g_high, g_low=g_low, gives=gives, takes=takes,
    )

    def exchange(out, last):
        if last:
            halos = [
                lax.ppermute(out.send_x_first, "gx", shift(lines[0], -1)),
                lax.ppermute(out.send_y_first, "gy", shift(lines[1], -1)),
            ]
        else:
            halos = [
                lax.ppermute(out.send_x_first, "gx", swap_first(lines[0])),
                lax.ppermute(out.send_y_first, "gy", swap_first(lines[1])),
                lax.ppermute(out.send_x_second, "gx", swap_second(lines[0])),
                lax.ppermute(out.send_y_second, "gy", swap_second(lines[1])),
            ]
        terms = lax.all_to_all(out.message, "gy", 0, 0)
        terms, *halos = lax.optimization_barrier((terms, *halos))
        out.x_first, out.y_first = halos[:2]
        out.x_second, out.y_second = (None, None) if last else halos[2:]
        out.parts = lax.all_to_all(solve(terms, *solver, KEPT if last else ROWS), "gx", 0, 0)
        out.z_x, out.z_y = out.z_x_out, out.z_y_out

    run = functools.partial(step, lines=lines, table=table, exchange=exchange)
    start = run(0, before=None, state=dict(received=received, coarse=coarse, loads=loads[0, 0]))
    first = run(1, before=start, state=None)
    second = run(
        2, before=first, state=SimpleNamespace(p=first.p_out, d=first.p_out, lam=start.lam_out)
    )
    third = run(
        3, before=second,
        state=SimpleNamespace(
            p=second.p_out, d=first.p_out, q=second.q_out, scal=second.scal_out,
            lam=second.lam_out, z_x_old=first.z_x, z_y_old=first.z_y,
        ),
    )
    half = (2 * slots, cases)
    out = call(
        final_kernel, "final",
        dict(
            received_by(third), parity=parity, mask=mask, g_high=g_high, g_low=g_low,
            p=third.p_out, d=third.d_out, q=third.q_out, scal=third.scal_out, lam=third.lam_out,
        ),
        dict(lam_out=half, p_out=half),
    )
    shape = (1, 1, 2, slots, cases)
    return out.lam_out.reshape(shape), out.p_out.reshape(shape)


def solution(mesh):
    in_specs = (
        P("gx", "gy", None, None),
        P("gx", "gy", None, None, None),
        P("gx", "gy", None, None),
        P("gx", "gy", None, None, None, None),
        P("gx", "gy", None, None),
        P("gx", "gy", None, None),
        P("gx", "gy", None, None, None),
    )
    out_specs = (P("gx", "gy", None, None, None), P("gx", "gy", None, None, None))
    return jax.shard_map(local, mesh=mesh, in_specs=in_specs, out_specs=out_specs, check_vma=False)
```

time: 898 us -> 174 us (0.19)
  waiting for transfers between devices: 338 us -> 4.68 us
  blocking collectives: 327 us -> 103 us
  local copies, waits for them, and re-layouts: 77.5 us -> 5.34 us
  matrix products: 63.8 us -> 0 us
  Pallas kernels: 0 us -> 33.1 us
  other arithmetic: 30.6 us -> 0 us
  between operations: 15.9 us -> 0.85 us
  starting transfers between devices: 35.2 us -> 25.8 us
    psum x5 -> x0, blocking collectives: 327 us -> none  [the longest x3 193 us: squares(): return lax.psum(jnp.sum(field * field, axis=(0, 1)), ('gx', 'gy'))]
    all_gather x5 -> x0, waiting for transfers between devices: 311 us -> none  [coarse_solve(): gathered = lax.all_gather(stacked, ('gx', 'gy'), axis=0, tiled=True)]
    all_to_all x0 -> x9, blocking collectives: none -> 103 us  [the longest x4 45.8 us: exchange(): lax.all_to_all(solve(terms, *solver, KEPT if last else ROWS), 'gx', 0, 0)]
    dot_general x41 -> x0, matrix products: 63.8 us -> none  [the longest x4 49 us: apply_dual(): jnp.dot(operator, stacked, precision=HIGHEST, preferred_element_type=jnp....]
    pallas_call x0 -> x20, Pallas kernels: none -> 33.1 us  [the longest x13 25.1 us: call(): pl.pallas_call(functools.partial(kernel, keys), in_specs=[VMEM_SPEC if v....]
    ppermute x16, waiting for transfers between devices: 27.4 us -> 0.04 us  [the longest x3 0.01 us: exchange(): lax.ppermute(out.send_y_second, 'gy', swap_second(lines[1]))]
    gather x32 -> x0, local copies, waits for them, and re-layouts: 25.8 us -> none  [the longest x8 7.91 us: apply_dual(): back_north = shifted(jnp.take(product[3], inverse_north, axis=0), 'gx', -1)]
    another operation x15 -> x1, local copies, waits for them, and re-layouts: 15.1 us -> 0.08 us  [local(): jnp.stack([at[0] % 2, at[1] % 2, at[0] == lines[0] - 1, at[1] == lines[1]...]
  transfers between devices with their start and end apart: 21 -> 17, of which waited for: 19 -> 1; matrix products, arithmetic and copies ran while one was open for 2% -> 0% of each run, Pallas kernels for 0% -> 1%
where the time goes in v2:
time: 174 us; the launch traced here: 173 us
  blocking collectives  103 us (59%)
  Pallas kernels  33.1 us (19%)
  starting transfers between devices  25.8 us (15%)
  local copies, waits for them, and re-layouts  5.34 us (3%)
  waiting for transfers between devices  4.68 us (3%)
    all_to_all x4, blocking collectives, exchange(): lax.all_to_all(solve(terms, *solver, KEPT if last else ROWS), 'gx', 0, 0)  45.8 us
    all_to_all x4, blocking collectives, exchange(): terms = lax.all_to_all(out.message, 'gy', 0, 0)  37.4 us
    pallas_call x13, Pallas kernels, call(): pl.pallas_call(functools.partial(kernel, keys), in_specs=[VMEM_SPEC if v....  25.1 us
    all_to_all x1, blocking collectives, local(): received = lax.all_to_all(pieces, 'gx', 0, 0)  19.6 us
    ppermute x3, starting transfers between devices, exchange(): lax.ppermute(out.send_y_first, 'gy', swap_first(lines[1]))  6.63 us
    ppermute x3, starting transfers between devices, exchange(): lax.ppermute(out.send_x_second, 'gx', swap_second(lines[0]))  5.32 us
    unnamed x13, local copies, waits for them, and re-layouts  5.26 us
    all_to_all x1, starting transfers between devices, local(): gathered = lax.all_to_all(message, 'gy', 0, 0)  4.97 us
  transfers between devices with their start and end apart: 17, of which 1 were waited for; matrix products, arithmetic and copies ran while one was open for 0% of the time, Pallas kernels for 1%

profile of v2, /device:TPU:1, one launch (start us, length us, event | category | flops | bytes accessed | tf_op | source)
XLA Modules:
  0.0 172.6 jit_solution(18102416686146002728)
XLA Ops:
  4.2 3.0 %collective-permute-start = (f32[16,768]{1,0:T(8,128)S(1)}, f32[16,768]{1,0:T(8,128)S(1)}, u32[]{:S(2)}, u32[]{:S(2)}) collective-permute-start(f32[16,768]{1,0:T(8,128)S(1)} %get-tuple-element.82), channel_id=1, source_target_pairs={{0,1},{1,2},{2,3},{3,4},{4,5},{5,6},{6,7},{7,0},{8,9},{9,10},{10,1... | collective-permute-start | bytes 147464 | tf_op jit(solution)/shard_map/ppermute | solution.py:558
  8.6 5.0 %all-to-all-start = ((f32[8,8,128]{2,1,0:T(8,128)}), f32[8,8,128]{2,1,0:T(8,128)S(1)}, u32[]{:S(2)}, u32[]{:S(2)}) async-start(f32[8,8,128]{2,1,0:T(8,128)} %get-tuple-element.81), calls=%async_computation | async-start | bytes 65536 | tf_op jit(solution)/shard_map/all_to_all | solution.py:560
  13.6 4.6 %all-to-all-done.rhs_ref = f32[8,8,128]{2,1,0:T(8,128)S(1)} async-done(((f32[8,8,128]{2,1,0:T(8,128)}), f32[8,8,128]{2,1,0:T(8,128)S(1)}, u32[]{:S(2)}, u32[]{:S(2)}) %all-to-all-start) | async-done | bytes 32800 | tf_op jit(solution)/shard_map/all_to_all | solution.py:560
  21.1 19.6 %all_to_all.50.received_ref.refs_7_ = f32[16,96,128]{2,1,0:T(8,128)S(1)} all-to-all(f32[16,96,128]{2,1,0:T(8,128)S(1)} %get-tuple-element.90), channel_id=1, replica_groups=mesh['gx'=16,'gy'=8] {'gx'}, dimensions={0} | all-to-all | bytes 1572864 | tf_op jit(solution)/shard_map/all_to_all | solution.py:565
  41.6 4.1 %spread.1 = (bf16[640,320]{1,0:T(8,128)(2,1)S(1)}, bf16[640,320]{1,0:T(8,128)(2,1)S(1)}, bf16[1536,1536]{1,0:T(8,128)(2,1)S(1)}, bf16[1536,1536]{1,0:T(8,128)(2,1)S(1)}) custom-call(f32[16,96,128]{2,1,0:T(8,128)S(1)} %all_to_all.50.received_ref.refs_7_, bf16[256,320]{1,0:T(8,128)(2,1)S(1)} %copy-done.1, f32[1536,1536]{1,0:T(8,128)} %bitcast.31), custom_call_target="tpu_custom_call" | custom-call | tf_op jit(solution)/shard_map/spread/pallas_call | solution.py:227
  45.8 3.2 %update0.1 = (bf16[1536,256]{1,0:T(8,128)(2,1)S(1)}, f32[2,384,128]{2,1,0:T(8,128)S(1)}, f32[384,128]{1,0:T(8,128)S(1)}, f32[384,128]{1,0:T(8,128)S(1)}, f32[768,128]{1,0:T(8,128)S(1)}) custom-call(s32[6]{0:T(128)S(1)} %stack.43.place_ref.refs_0_.refs_5_, bf16[1536,1536]{1,0:T(8,128)(2,1)S(1)} %get-tuple-element.91.refs_1_, ...), custom_call_target="tpu_custom_call" | custom-call | flops 1207959552 | bytes 4096 | tf_op jit(solution)/shard_map/update0/pallas_call | solution.py:428
  49.0 2.4 %apply0.1 = (f32[2,384,128]{2,1,0:T(8,128)S(1)}, f32[384,128]{1,0:T(8,128)S(1)}, f32[384,128]{1,0:T(8,128)S(1)}) custom-call(s32[6]{0:T(128)S(1)} %stack.43.place_ref.refs_0_.refs_5_, bf16[1536,1536]{1,0:T(8,128)(2,1)S(1)} %get-tuple-element.91.refs_1_, bf16[1536,1536]{1,0:T(8,128)(2,1)S(1)} %get-tuple-element.92.refs_2_, ...), custom_call_target="tpu_custom_call" | custom-call | flops 1207959552 | bytes 4096 | tf_op jit(solution)/shard_map/apply0/pallas_call | solution.py:428
  55.7 9.7 %all_to_all.51.terms_ref = f32[8,40,128]{2,1,0:T(8,128)S(1)} all-to-all(f32[8,40,128]{2,1,0:T(8,128)S(1)} %terms0.1), channel_id=1, replica_groups=mesh['gx'=16,'gy'=8] {'gy'}, dimensions={0} | all-to-all | bytes 327680 | tf_op jit(solution)/shard_map/all_to_all | solution.py:585
  65.9 12.0 %all_to_all.52.refs_7_ = f32[16,40,128]{2,1,0:T(8,128)S(1)} all-to-all(f32[16,40,128]{2,1,0:T(8,128)S(1)} %solve.4), channel_id=1, replica_groups=mesh['gx'=16,'gy'=8] {'gx'}, dimensions={0} | all-to-all | bytes 655360 | tf_op jit(solution)/shard_map/all_to_all | solution.py:589
  77.9 3.0 %update1.1 = (bf16[1536,256]{1,0:T(8,128)(2,1)S(1)}, f32[2,384,128]{2,1,0:T(8,128)S(1)}, f32[384,128]{1,0:T(8,128)S(1)}, f32[384,128]{1,0:T(8,128)S(1)}, f32[1536,128]{1,0:T(8,128)S(1)}) custom-call(s32[6]{0:T(128)S(1)} %stack.43.place_ref.refs_0_.refs_5_, bf16[1536,1536]{1,0:T(8,128)(2,1)S(1)} %get-tuple-element.91.refs_1_, ...), custom_call_target="tpu_custom_call" | custom-call | flops 1207959552 | bytes 4096 | tf_op jit(solution)/shard_map/update1/pallas_call | solution.py:428
  80.8 2.4 %apply1.1 = (f32[2,384,128]{2,1,0:T(8,128)S(1)}, f32[384,128]{1,0:T(8,128)S(1)}, f32[384,128]{1,0:T(8,128)S(1)}) custom-call(s32[6]{0:T(128)S(1)} %stack.43.place_ref.refs_0_.refs_5_, bf16[1536,1536]{1,0:T(8,128)(2,1)S(1)} %get-tuple-element.91.refs_1_, bf16[1536,1536]{1,0:T(8,128)(2,1)S(1)} %get-tuple-element.92.refs_2_, ...), custom_call_target="tpu_custom_call" | custom-call | flops 1207959552 | bytes 4096 | tf_op jit(solution)/shard_map/apply1/pallas_call | solution.py:428
  83.2 2.4 %collective-permute-start.7 = (f32[384,128]{1,0:T(8,128)S(1)}, f32[384,128]{1,0:T(8,128)S(1)}, u32[]{:S(2)}, u32[]{:S(2)}) collective-permute-start(f32[384,128]{1,0:T(8,128)S(1)} %get-tuple-element.118), channel_id=1, source_target_pairs={{0,1},{1,0},{2,3},{3,2},{4,5},{5,4},{6,7},{7,6},{8,9},{9,8},{10,11... | collective-permute-start | bytes 589832 | tf_op jit(solution)/shard_map/ppermute | solution.py:581
  88.1 9.7 %all_to_all.53.terms_ref = f32[8,40,128]{2,1,0:T(8,128)S(1)} all-to-all(f32[8,40,128]{2,1,0:T(8,128)S(1)} %terms1.1), channel_id=1, replica_groups=mesh['gx'=16,'gy'=8] {'gy'}, dimensions={0} | all-to-all | bytes 327680 | tf_op jit(solution)/shard_map/all_to_all | solution.py:585
  98.3 12.0 %all_to_all.54.refs_7_ = f32[16,40,128]{2,1,0:T(8,128)S(1)} all-to-all(f32[16,40,128]{2,1,0:T(8,128)S(1)} %solve.5), channel_id=1, replica_groups=mesh['gx'=16,'gy'=8] {'gx'}, dimensions={0} | all-to-all | bytes 655360 | tf_op jit(solution)/shard_map/all_to_all | solution.py:589
  110.3 2.9 %update2.1 = (bf16[1536,256]{1,0:T(8,128)(2,1)S(1)}, f32[2,384,128]{2,1,0:T(8,128)S(1)}, f32[384,128]{1,0:T(8,128)S(1)}, f32[384,128]{1,0:T(8,128)S(1)}, f32[153...) custom-call(s32[6]{0:T(128)S(1)} %stack.43.place_ref.refs_0_.refs_5_, ...), custom_call_target="tpu_custom_call" | custom-call | flops 1207959552 | bytes 4096 | tf_op jit(solution)/shard_map/update2/pallas_call | solution.py:428
  113.2 2.4 %apply2.1 = (f32[2,384,128]{2,1,0:T(8,128)S(1)}, f32[384,128]{1,0:T(8,128)S(1)}, f32[384,128]{1,0:T(8,128)S(1)}) custom-call(s32[6]{0:T(128)S(1)} %stack.43.place_ref.refs_0_.refs_5_, bf16[1536,1536]{1,0:T(8,128)(2,1)S(1)} %get-tuple-element.91.refs_1_, bf16[1536,1536]{1,0:T(8,128)(2,1)S(1)} %get-tuple-element.92.refs_2_, ...), custom_call_target="tpu_custom_call" | custom-call | flops 1207959552 | bytes 4096 | tf_op jit(solution)/shard_map/apply2/pallas_call | solution.py:428
  115.6 2.4 %collective-permute-start.11 = (f32[384,128]{1,0:T(8,128)S(1)}, f32[384,128]{1,0:T(8,128)S(1)}, u32[]{:S(2)}, u32[]{:S(2)}) collective-permute-start(f32[384,128]{1,0:T(8,128)S(1)} %get-tuple-element.134), channel_id=1, source_target_pairs={{0,1},{1,0},{2,3},{3,2},{4,5},{5,4},{6,7},{7,6},{8,9},{9,8},{10,11... | collective-permute-start | bytes 589832 | tf_op jit(solution)/shard_map/ppermute | solution.py:581
  120.7 9.7 %all_to_all.55.terms_ref = f32[8,40,128]{2,1,0:T(8,128)S(1)} all-to-all(f32[8,40,128]{2,1,0:T(8,128)S(1)} %get-tuple-element.132), channel_id=1, replica_groups=mesh['gx'=16,'gy'=8] {'gy'}, dimensions={0} | all-to-all | bytes 327680 | tf_op jit(solution)/shard_map/all_to_all | solution.py:585
  130.8 12.0 %all_to_all.56.refs_7_ = f32[16,40,128]{2,1,0:T(8,128)S(1)} all-to-all(f32[16,40,128]{2,1,0:T(8,128)S(1)} %solve.6), channel_id=1, replica_groups=mesh['gx'=16,'gy'=8] {'gx'}, dimensions={0} | all-to-all | bytes 655360 | tf_op jit(solution)/shard_map/all_to_all | solution.py:589
  142.8 3.0 %update3.1 = (bf16[1536,256]{1,0:T(8,128)(2,1)S(1)}, f32[2,384,128]{2,1,0:T(8,128)S(1)}, f32[384,128]{1,0:T(8,128)S(1)}, f32[1536,128]{1,0:T(8,128)S(1)}, f32[1536,128]{1,0:T(8,128)S(1)}, /*index=5*/f32[8,128]{1,0:T(8,128)S(1)}) custom-call(s32[6]{0:T(128)S(1)} %stack.43.place_ref.refs_0_.refs_5_, bf16[1536,1536]{1,0:T(8,128)(2,1)S(1)} %get-tuple-element.91.refs_1_, ...), custom_call_target="tpu_custom_call" | custom-call | flops 1207959552 | bytes 4096 | tf_op jit(solution)/shard_map/update3/pallas_call | solution.py:428
  145.8 2.3 %apply3.1 = (f32[2,384,128]{2,1,0:T(8,128)S(1)}, f32[384,128]{1,0:T(8,128)S(1)}) custom-call(s32[6]{0:T(128)S(1)} %stack.43.place_ref.refs_0_.refs_5_, bf16[1536,1536]{1,0:T(8,128)(2,1)S(1)} %get-tuple-element.91.refs_1_, bf16[1536,1536]{1,0:T(8,128)(2,1)S(1)} %get-tuple-element.92.refs_2_, bf16[2,384,384]{2,1,0:T(8,128)(2,1)S(1)} %get-tuple-element.93.refs_3_, ...), custom_call_target="tpu_custom_call" | custom-call | flops 1207959552 | bytes 4096 | tf_op jit(solution)/shard_map/apply3/pallas_call | solution.py:428
  148.1 2.3 %collective-permute-start.15 = (f32[384,128]{1,0:T(8,128)S(1)}, f32[384,128]{1,0:T(8,128)S(1)}, u32[]{:S(2)}, u32[]{:S(2)}) collective-permute-start(f32[384,128]{1,0:T(8,128)S(1)} %get-tuple-element.151), channel_id=1, source_target_pairs={{0,7},{1,0},{2,1},{3,2},{4,3},{5,4},{6,5},{7,6},{8,15},{9,8},{10,9... | collective-permute-start | bytes 589832 | tf_op jit(solution)/shard_map/ppermute | solution.py:576
  152.1 8.3 %all_to_all.57.terms_ref = f32[8,40,128]{2,1,0:T(8,128)S(1)} all-to-all(f32[8,40,128]{2,1,0:T(8,128)S(1)} %get-tuple-element.149), channel_id=1, replica_groups=mesh['gx'=16,'gy'=8] {'gy'}, dimensions={0} | all-to-all | bytes 327680 | tf_op jit(solution)/shard_map/all_to_all | solution.py:585
  160.9 9.8 %all_to_all.58.refs_0_ = f32[16,24,128]{2,1,0:T(8,128)S(1)} all-to-all(f32[16,24,128]{2,1,0:T(8,128)S(1)} %solve.7), channel_id=1, replica_groups=mesh['gx'=16,'gy'=8] {'gx'}, dimensions={0} | all-to-all | bytes 393216 | tf_op jit(solution)/shard_map/all_to_all | solution.py:589
  (53 shorter events, 23.6 us)
Async XLA Ops:
  2.9 0.7 copy-start.2
  4.2 14.0 %collective-permute-start = (f32[16,768]{1,0:T(8,128)S(1)}, f32[16,768]{1,0:T(8,128)S(1)}, u32[]{:S(2)}, u32[]{:S(2)}) collective-permute-start(f32[16,768]{1,0:T(8,128)S(1)} %get-tuple-element.82), channel_id=1, source_target_pairs={{0,1},{1,2},{2,3},{3,4},{4,5},{5,6},{6,7},{7,0},{8,9},{9,10},{10,1... | collective-permute-start | bytes 147464 | tf_op jit(solution)/shard_map/ppermute | solution.py:558
  7.3 11.0 %collective-permute-start.1 = (f32[16,768]{1,0:T(8,128)S(1)}, f32[16,768]{1,0:T(8,128)S(1)}, u32[]{:S(2)}, u32[]{:S(2)}) collective-permute-start(f32[16,768]{1,0:T(8,128)S(1)} %get-tuple-element.83), channel_id=1, source_target_pairs={{0,8},{8,16},{16,24},{24,32},{32,40},{40,48},{48,56},{56,64},{64,7... | collective-permute-start | bytes 147464 | tf_op jit(solution)/shard_map/ppermute | solution.py:559
  8.6 9.7 %all-to-all-start = ((f32[8,8,128]{2,1,0:T(8,128)}), f32[8,8,128]{2,1,0:T(8,128)S(1)}, u32[]{:S(2)}, u32[]{:S(2)}) async-start(f32[8,8,128]{2,1,0:T(8,128)} %get-tuple-element.81), calls=%async_computation | async-start | bytes 65536 | tf_op jit(solution)/shard_map/all_to_all | solution.py:560
  18.3 0.7 copy-start.3
  18.9 0.7 copy-start.4
  40.7 0.9 copy-start.1
  41.6 4.1 %copy-start = (f32[1,1,2,384,128]{4,3,2,1,0:T(8,128)S(1)}, f32[1,1,2,384,128]{4,3,2,1,0:T(8,128)}, u32[]{:S(2)}) copy-start(f32[1,1,2,384,128]{4,3,2,1,0:T(8,128)} %param.9) | copy-start | bytes 1179652
  51.4 14.0 %collective-permute-start.3 = (f32[384,128]{1,0:T(8,128)S(1)}, f32[384,128]{1,0:T(8,128)S(1)}, u32[]{:S(2)}, u32[]{:S(2)}) collective-permute-start(f32[384,128]{1,0:T(8,128)S(1)} %get-tuple-element.102), channel_id=1, source_target_pairs={{0,1},{1,0},{2,3},{3,2},{4,5},{5,4},{6,7},{7,6},{8,9},{9,8},{10,11... | collective-permute-start | bytes 589832 | tf_op jit(solution)/shard_map/ppermute | solution.py:581
  53.2 12.2 %collective-permute-start.5 = (f32[384,128]{1,0:T(8,128)S(1)}, f32[384,128]{1,0:T(8,128)S(1)}, u32[]{:S(2)}, u32[]{:S(2)}) collective-permute-start(f32[384,128]{1,0:T(8,128)S(1)} %get-tuple-element.104), channel_id=1, source_target_pairs={{0,7},{1,2},{2,1},{3,4},{4,3},{5,6},{6,5},{7,0},{8,15},{9,10},{10,... | collective-permute-start | bytes 589832 | tf_op jit(solution)/shard_map/ppermute | solution.py:583
  53.5 11.9 %collective-permute-start.2 = (f32[384,128]{1,0:T(8,128)S(1)}, f32[384,128]{1,0:T(8,128)S(1)}, u32[]{:S(2)}, u32[]{:S(2)}) collective-permute-start(f32[384,128]{1,0:T(8,128)S(1)} %get-tuple-element.101), channel_id=1, source_target_pairs={{0,8},{8,0},{16,24},{24,16},{32,40},{40,32},{48,56},{56,48},{64,72... | collective-permute-start | bytes 589832 | tf_op jit(solution)/shard_map/ppermute | solution.py:580
  53.6 11.8 %collective-permute-start.4 = (f32[384,128]{1,0:T(8,128)S(1)}, f32[384,128]{1,0:T(8,128)S(1)}, u32[]{:S(2)}, u32[]{:S(2)}) collective-permute-start(f32[384,128]{1,0:T(8,128)S(1)} %get-tuple-element.103), channel_id=1, source_target_pairs={{0,120},{8,16},{16,8},{24,32},{32,24},{40,48},{48,40},{56,64},{64,... | collective-permute-start | bytes 589832 | tf_op jit(solution)/shard_map/ppermute | solution.py:582
  83.2 14.6 %collective-permute-start.7 = (f32[384,128]{1,0:T(8,128)S(1)}, f32[384,128]{1,0:T(8,128)S(1)}, u32[]{:S(2)}, u32[]{:S(2)}) collective-permute-start(f32[384,128]{1,0:T(8,128)S(1)} %get-tuple-element.118), channel_id=1, source_target_pairs={{0,1},{1,0},{2,3},{3,2},{4,5},{5,4},{6,7},{7,6},{8,9},{9,8},{10,11... | collective-permute-start | bytes 589832 | tf_op jit(solution)/shard_map/ppermute | solution.py:581
  85.6 12.2 %collective-permute-start.9 = (f32[384,128]{1,0:T(8,128)S(1)}, f32[384,128]{1,0:T(8,128)S(1)}, u32[]{:S(2)}, u32[]{:S(2)}) collective-permute-start(f32[384,128]{1,0:T(8,128)S(1)} %get-tuple-element.120), channel_id=1, source_target_pairs={{0,7},{1,2},{2,1},{3,4},{4,3},{5,6},{6,5},{7,0},{8,15},{9,10},{10,... | collective-permute-start | bytes 589832 | tf_op jit(solution)/shard_map/ppermute | solution.py:583
  85.9 12.0 %collective-permute-start.6 = (f32[384,128]{1,0:T(8,128)S(1)}, f32[384,128]{1,0:T(8,128)S(1)}, u32[]{:S(2)}, u32[]{:S(2)}) collective-permute-start(f32[384,128]{1,0:T(8,128)S(1)} %get-tuple-element.117), channel_id=1, source_target_pairs={{0,8},{8,0},{16,24},{24,16},{32,40},{40,32},{48,56},{56,48},{64,72... | collective-permute-start | bytes 589832 | tf_op jit(solution)/shard_map/ppermute | solution.py:580
  86.0 11.8 %collective-permute-start.8 = (f32[384,128]{1,0:T(8,128)S(1)}, f32[384,128]{1,0:T(8,128)S(1)}, u32[]{:S(2)}, u32[]{:S(2)}) collective-permute-start(f32[384,128]{1,0:T(8,128)S(1)} %get-tuple-element.119), channel_id=1, source_target_pairs={{0,120},{8,16},{16,8},{24,32},{32,24},{40,48},{48,40},{56,64},{64,... | collective-permute-start | bytes 589832 | tf_op jit(solution)/shard_map/ppermute | solution.py:582
  115.6 14.8 %collective-permute-start.11 = (f32[384,128]{1,0:T(8,128)S(1)}, f32[384,128]{1,0:T(8,128)S(1)}, u32[]{:S(2)}, u32[]{:S(2)}) collective-permute-start(f32[384,128]{1,0:T(8,128)S(1)} %get-tuple-element.134), channel_id=1, source_target_pairs={{0,1},{1,0},{2,3},{3,2},{4,5},{5,4},{6,7},{7,6},{8,9},{9,8},{10,11... | collective-permute-start | bytes 589832 | tf_op jit(solution)/shard_map/ppermute | solution.py:581
  118.0 12.4 %collective-permute-start.13 = (f32[384,128]{1,0:T(8,128)S(1)}, f32[384,128]{1,0:T(8,128)S(1)}, u32[]{:S(2)}, u32[]{:S(2)}) collective-permute-start(f32[384,128]{1,0:T(8,128)S(1)} %get-tuple-element.136), channel_id=1, source_target_pairs={{0,7},{1,2},{2,1},{3,4},{4,3},{5,6},{6,5},{7,0},{8,15},{9,10},{10,... | collective-permute-start | bytes 589832 | tf_op jit(solution)/shard_map/ppermute | solution.py:583
  118.3 12.1 %collective-permute-start.10 = (f32[384,128]{1,0:T(8,128)S(1)}, f32[384,128]{1,0:T(8,128)S(1)}, u32[]{:S(2)}, u32[]{:S(2)}) collective-permute-start(f32[384,128]{1,0:T(8,128)S(1)} %get-tuple-element.133), channel_id=1, source_target_pairs={{0,8},{8,0},{16,24},{24,16},{32,40},{40,32},{48,56},{56,48},{64,72... | collective-permute-start | bytes 589832 | tf_op jit(solution)/shard_map/ppermute | solution.py:580
  118.4 12.0 %collective-permute-start.12 = (f32[384,128]{1,0:T(8,128)S(1)}, f32[384,128]{1,0:T(8,128)S(1)}, u32[]{:S(2)}, u32[]{:S(2)}) collective-permute-start(f32[384,128]{1,0:T(8,128)S(1)} %get-tuple-element.135), channel_id=1, source_target_pairs={{0,120},{8,16},{16,8},{24,32},{32,24},{40,48},{48,40},{56,64},{64,... | collective-permute-start | bytes 589832 | tf_op jit(solution)/shard_map/ppermute | solution.py:582
  148.1 12.3 %collective-permute-start.15 = (f32[384,128]{1,0:T(8,128)S(1)}, f32[384,128]{1,0:T(8,128)S(1)}, u32[]{:S(2)}, u32[]{:S(2)}) collective-permute-start(f32[384,128]{1,0:T(8,128)S(1)} %get-tuple-element.151), channel_id=1, source_target_pairs={{0,7},{1,0},{2,1},{3,2},{4,3},{5,4},{6,5},{7,6},{8,15},{9,8},{10,9... | collective-permute-start | bytes 589832 | tf_op jit(solution)/shard_map/ppermute | solution.py:576
  150.5 10.0 %collective-permute-start.14 = (f32[384,128]{1,0:T(8,128)S(1)}, f32[384,128]{1,0:T(8,128)S(1)}, u32[]{:S(2)}, u32[]{:S(2)}) collective-permute-start(f32[384,128]{1,0:T(8,128)S(1)} %get-tuple-element.150), channel_id=1, source_target_pairs={{0,120},{8,0},{16,8},{24,16},{32,24},{40,32},{48,40},{56,48},{64,5... | collective-permute-start | bytes 589832 | tf_op jit(solution)/shard_map/ppermute | solution.py:575

commit v3 on v2

--- a/solution.py
+++ b/solution.py
@@ -22,6 +22,7 @@
 KEPT = 3 * GROUP
 TAIL = 16
 STEP_MB = 16
+PACK_MB = 60
 NORM_ROW, ENERGY_ROW, CROSS_ROW = 6, 7, 14
 
 
@@ -54,54 +55,96 @@
     return wide[:, :columns] + wide[:, columns:] + mm(left_low, pair[:, :columns])
 
 
-def pack_kernel(rows_ref, modes_ref, free_ref, rhs_ref, east_ref, south_ref, message_ref):
-    slots = free_ref.shape[1]
-    for face, out in enumerate((east_ref, south_ref)):
-        out[...] = jnp.zeros_like(out)
-        out[0:MODES, :] = rows_ref[0]
-        out[6:7, :slots] = free_ref[face : face + 1, :].astype(F32)
-        for side in range(2):
-            out[8 : 8 + MODES, side * slots : (side + 1) * slots] = modes_ref[face, side]
-    message_ref[...] = jnp.zeros_like(message_ref)
-    for peer in range(message_ref.shape[0]):
-        message_ref[peer, 0:MODES, :] = rhs_ref[...]
-
-
-def pack(rows, modes, free, rhs, peers):
+def pack_kernel(
+    rows_in, modes_in, free_in, match_in, rhs_in,
+    east_ref, south_ref, message_ref, own_ref,
+    rows_held, modes_held, free_held, match_held, rhs_held, sems,
+):
+    copies = [
+        pltpu.make_async_copy(source, target, sems.at[at])
+        for at, (source, target) in enumerate(
+            (
+                (rows_in, rows_held), (modes_in, modes_held), (free_in, free_held),
+                (match_in, match_held), (rhs_in, rhs_held),
+            )
+        )
+    ]
+    for copy in copies:
+        copy.start()
+    for ref in (own_ref, message_ref):
+        ref[...] = jnp.zeros_like(ref)
+    for copy in copies:
+        copy.wait()
+    slots = free_held.shape[1]
+    for mode in range(MODES):
+        for at, member in ((0, 0), (16, 0), (32, 1), (40, 2)):
+            own_ref[at + mode : at + mode + 1, :] = rows_held[member, mode]
+        for face in range(2):
+            at = 16 * face + 8 + mode
+            for side in range(2):
+                own_ref[at : at + 1, side * slots : (side + 1) * slots] = modes_held[
+                    face, mode, side : side + 1, :
+                ]
+        for peer in range(message_ref.shape[0]):
+            message_ref[peer, mode : mode + 1, :] = rhs_held[mode]
+    for face in range(2):
+        at = 16 * face + MODES
+        own_ref[at : at + 1, :slots] = free_held[face : face + 1, :].astype(F32)
+        own_ref[at + 1 : at + 2, :slots] = match_held[face : face + 1, :].astype(F32)
+    east_ref[...] = own_ref[0:16, :]
+    south_ref[...] = own_ref[16:32, :]
+
+
+def pack(rows, modes, free, match, rhs, peers):
     width = rows.shape[-1]
+    cases = rhs.shape[-1]
+    rows = rows[:, :, None]
+    modes = jnp.swapaxes(modes, 1, 2)
+    rhs = rhs[:, None]
     return pl.pallas_call(
         pack_kernel,
-        in_specs=[VMEM_SPEC] * 4,
-        out_specs=[VMEM_SPEC] * 3,
+        in_specs=[pl.BlockSpec(memory_space=pl.ANY)] * 5,
+        out_specs=[VMEM_SPEC] * 4,
         out_shape=[
             jax.ShapeDtypeStruct((16, width), F32),
             jax.ShapeDtypeStruct((16, width), F32),
-            jax.ShapeDtypeStruct((peers, GROUP, rhs.shape[-1]), F32),
+            jax.ShapeDtypeStruct((peers, GROUP, cases), F32),
+            jax.ShapeDtypeStruct((48, width), F32),
         ],
-        compiler_params=params(8),
+        scratch_shapes=[
+            pltpu.VMEM(rows.shape, F32), pltpu.VMEM(modes.shape, F32),
+            pltpu.VMEM(free.shape, jnp.int32), pltpu.VMEM(match.shape, jnp.int32),
+            pltpu.VMEM(rhs.shape, F32), pltpu.SemaphoreType.DMA((5,)),
+        ],
+        compiler_params=params(PACK_MB),
         name="pack",
-    )(rows, modes, free, rhs)
+    )(rows, modes, free, match, rhs)
 
 
 def frame_kernel(
-    lines, place_ref, modes_ref, free_ref, match_ref, rows_ref, west_ref, north_ref, rhs_ref,
+    lines, slots, place_ref, own_ref, west_ref, north_ref, rhs_ref,
     mask_ref, t_high_ref, t_low_ref, g_high_ref, g_low_ref, gives_ref, takes_ref,
-    coarse_ref, pieces_ref, table_ref, held_ref,
+    coarse_ref, pieces_ref,
+    table_ref, held_ref,
 ):
-    slots = free_ref.shape[1]
     cases = mask_ref.shape[1]
     span = MODES * lines[1]
+    modes = [
+        own_ref[16 * face + 8 : 16 * face + 8 + MODES, side * slots : (side + 1) * slots]
+        for face in range(2)
+        for side in range(2)
+    ]
     no_north, no_west = place_ref[4] != 0, place_ref[5] != 0
     west = jnp.where(no_west, 0.0, west_ref[...])
     north = jnp.where(no_north, 0.0, north_ref[...])
     table_ref[...] = jnp.zeros_like(table_ref)
     masks = [
-        free_ref[0:1, :].astype(F32), free_ref[1:2, :].astype(F32),
+        own_ref[6:7, :slots], own_ref[22:23, :slots],
         west[6:7, :slots], north[6:7, :slots],
     ]
     entries = [
-        (0, 0, modes_ref[0, 0]), (0, 1, modes_ref[1, 0]),
-        (1, 0, modes_ref[0, 1]), (2, 1, modes_ref[1, 1]),
+        (0, 0, modes[0]), (0, 1, modes[2]),
+        (1, 0, modes[1]), (2, 1, modes[3]),
         (3, 2, west[8 : 8 + MODES, :slots]), (0, 2, west[8 : 8 + MODES, slots : 2 * slots]),
         (4, 3, north[8 : 8 + MODES, :slots]), (0, 3, north[8 : 8 + MODES, slots : 2 * slots]),
     ]
@@ -119,13 +162,14 @@
     for face in range(4):
         spread = jnp.broadcast_to(masks[face], (cases, slots))
         mask_ref[face * slots : (face + 1) * slots, :] = spread.T
-    order = lax.broadcasted_iota(jnp.int32, (slots, slots), 0)
+    order = lax.broadcasted_iota(jnp.int32, (slots, slots), 0).astype(F32)
     for side in range(2):
-        moves = jnp.where(order == match_ref[side : side + 1, :], 1.0, 0.0)
+        moves = jnp.where(order == own_ref[16 * side + 7 : 16 * side + 8, :slots], 1.0, 0.0)
         gives_ref[side] = moves.astype(BF16)
         takes_ref[side] = moves.T.astype(BF16)
     coarse_ref[...] = jnp.zeros_like(coarse_ref)
-    members = [rows_ref[0], rows_ref[1], rows_ref[2], west[0:MODES, :], north[0:MODES, :]]
+    members = [own_ref[at : at + MODES, :] for at in (0, 32, 40)]
+    members += [west[0:MODES, :], north[0:MODES, :]]
     for member, values in enumerate(members):
         coarse_ref[member * GROUP : member * GROUP + MODES, :] = values
     edge = jnp.zeros((ROWS, span), F32)
@@ -145,15 +189,14 @@
         pieces_ref[line, ROWS + GROUP :] = held_ref[...]
 
 
-def frame(lines, place, modes, free, match, rows, west, north, rhs):
-    slots = free.shape[1]
+def frame(lines, slots, place, own, west, north, rhs):
     size = 4 * slots
-    width = rows.shape[-1]
+    width = own.shape[1]
     cases = rhs.shape[-1]
     span = MODES * lines[1]
     return pl.pallas_call(
-        functools.partial(frame_kernel, lines),
-        in_specs=[SMEM_SPEC] + [VMEM_SPEC] * 7,
+        functools.partial(frame_kernel, lines, slots),
+        in_specs=[SMEM_SPEC] + [VMEM_SPEC] * 4,
         out_specs=[VMEM_SPEC] * 9,
         out_shape=[
             jax.ShapeDtypeStruct((size, cases), F32),
@@ -166,10 +209,12 @@
             jax.ShapeDtypeStruct((ROWS, width), F32),
             jax.ShapeDtypeStruct((lines[0], ROWS + GROUP + span, cases), F32),
         ],
-        scratch_shapes=[pltpu.VMEM((128, size), F32), pltpu.VMEM((span, cases), F32)],
+        scratch_shapes=[
+            pltpu.VMEM((128, size), F32), pltpu.VMEM((span, cases), F32),
+        ],
         compiler_params=params(12),
         name="frame",
-    )(place, modes, free, match, rows, west, north, rhs)
+    )(place, own, west, north, rhs)
 
 
 def expansion(lines):
@@ -186,12 +231,15 @@
 
 
 def spread_kernel(
-    received_ref, expand_ref, operator_ref,
-    high_ref, low_ref, a_high_ref, a_low_ref, tail_ref, held_ref, sems,
+    received_ref, expand_in, operator_ref, loads_in,
+    high_ref, low_ref, a_high_ref, a_low_ref, loads_ref,
+    tail_ref, held_ref, expand_ref, sems, loads_sem, expand_sem,
 ):
     size = operator_ref.shape[0]
     count = sems.shape[0]
     block = size // count
+    expand_copy = pltpu.make_async_copy(expand_in, expand_ref, expand_sem)
+    expand_copy.start()
     copies = []
     for part in range(count):
         rows = pl.ds(part * block, block)
@@ -199,6 +247,8 @@
             pltpu.make_async_copy(operator_ref.at[rows], held_ref.at[rows], sems.at[part])
         )
         copies[-1].start()
+    loads_copy = pltpu.make_async_copy(loads_in, loads_ref, loads_sem)
+    loads_copy.start()
     lines, _, cases = received_ref.shape
     tail = TAIL
     tail_ref[...] = jnp.zeros_like(tail_ref)
@@ -207,6 +257,7 @@
         tail_ref[:, member * GROUP : (member + 1) * GROUP, 0:tail] = packed[
             :, :, member * tail : (member + 1) * tail
         ]
+    expand_copy.wait()
     head = split(received_ref[:, 0:ROWS, :].reshape(lines * ROWS, cases))
     rest = split(tail_ref[...].reshape(lines * ROWS, cases))
     for first, last, out in zip(head, rest, (high_ref, low_ref)):
@@ -218,25 +269,28 @@
         high, low = split(held_ref[rows, :])
         a_high_ref[rows, :] = high
         a_low_ref[rows, :] = low
-
-
-def spread(received, expand, operator):
+    loads_copy.wait()
+
+
+def spread(received, expand, operator, loads):
     lines, _, cases = received.shape
     shape = (lines * ROWS, expand.shape[1])
     size = operator.shape[0]
     return pl.pallas_call(
         spread_kernel,
-        in_specs=[VMEM_SPEC] * 2 + [pl.BlockSpec(memory_space=pl.ANY)],
-        out_specs=[VMEM_SPEC] * 4,
+        in_specs=[VMEM_SPEC] + [pl.BlockSpec(memory_space=pl.ANY)] * 3,
+        out_specs=[VMEM_SPEC] * 5,
         out_shape=[jax.ShapeDtypeStruct(shape, BF16)] * 2
-        + [jax.ShapeDtypeStruct((size, size), BF16)] * 2,
+        + [jax.ShapeDtypeStruct((size, size), BF16)] * 2
+        + [jax.ShapeDtypeStruct(loads.shape, F32)],
         scratch_shapes=[
             pltpu.VMEM((lines, ROWS, cases), F32), pltpu.VMEM((size, size), F32),
-            pltpu.SemaphoreType.DMA((8,)),
+            pltpu.VMEM(expand.shape, BF16),
+            pltpu.SemaphoreType.DMA((8,)), pltpu.SemaphoreType.DMA, pltpu.SemaphoreType.DMA,
         ],
         compiler_params=params(40),
         name="spread",
-    )(received, expand, operator)
+    )(received, expand, operator, loads)
 
 
 def solve_kernel(terms_ref, high_ref, low_ref, out_ref):
@@ -304,7 +358,7 @@
 
 def apply_faces(r, side, z_ref, first_ref, second_ref, loaded):
     slots = r.gives.shape[1]
-    for index in range(2):
+    for index in (1, 0):
         face = side + 2 * index
         rows = slice(face * slots, (face + 1) * slots)
         out = mm3(r.a_high[rows, :], r.a_low[rows, :], r.pair[...])
@@ -540,9 +594,6 @@
 
 def local(dual_ops, loads, coarse_rhs, coarse_modes, free_mask, face_match, coarse_rows):
     operator = dual_ops[0, 0]
-    modes = coarse_modes[0, 0]
-    free = free_mask[0, 0]
-    rows = coarse_rows[0, 0]
     slots, cases = loads.shape[-2:]
     lines = (lax.axis_size("gx"), lax.axis_size("gy"))
     peers = lines[0] * lines[1]
@@ -554,16 +605,21 @@
         ]
     ).astype(jnp.int32)
 
-    pack_east, pack_south, message = pack(rows, modes, free, coarse_rhs[0, 0], lines[1])
+    pack_east, pack_south, message, own = pack(
+        coarse_rows[0, 0], coarse_modes[0, 0], free_mask[0, 0], face_match[0, 0],
+        coarse_rhs[0, 0], lines[1],
+    )
     west = lax.ppermute(pack_east, "gy", shift(lines[1], 1))
     north = lax.ppermute(pack_south, "gx", shift(lines[0], 1))
     gathered = lax.all_to_all(message, "gy", 0, 0)
     gathered, west, north, parity = lax.optimization_barrier((gathered, west, north, parity))
     mask, t_high, t_low, g_high, g_low, gives, takes, coarse, pieces = frame(
-        lines, parity, modes, free, face_match[0, 0], rows, west, north, gathered
+        lines, slots, parity, own, west, north, gathered
     )
     received = lax.all_to_all(pieces, "gx", 0, 0)
-    *solver, a_high, a_low = spread(received, expansion(lines), operator)
+    *solver, a_high, a_low, held_loads = spread(
+        received, expansion(lines), operator, loads[0, 0]
+    )
     table = SimpleNamespace(
         parity=parity, a_high=a_high, a_low=a_low, mask=mask, t_high=t_high, t_low=t_low,
         g_high=g_high, g_low=g_low, gives=gives, takes=takes,
@@ -590,7 +646,7 @@
         out.z_x, out.z_y = out.z_x_out, out.z_y_out
 
     run = functools.partial(step, lines=lines, table=table, exchange=exchange)
-    start = run(0, before=None, state=dict(received=received, coarse=coarse, loads=loads[0, 0]))
+    start = run(0, before=None, state=dict(received=received, coarse=coarse, loads=held_loads))
     first = run(1, before=start, state=None)
     second = run(
         2, before=first, state=SimpleNamespace(p=first.p_out, d=first.p_out, lam=start.lam_out)

time: 174 us -> 172 us (0.989)
  local copies, waits for them, and re-layouts: 5.34 us -> 2.91 us
    unnamed x13 -> x6, local copies, waits for them, and re-layouts: 5.26 us -> 2.83 us
where the time goes in v3:
time: 172 us; the launch traced here: 170 us
  blocking collectives  103 us (60%)
  Pallas kernels  32.9 us (19%)
  starting transfers between devices  25.8 us (15%)
  waiting for transfers between devices  4.68 us (3%)
  local copies, waits for them, and re-layouts  2.91 us (2%)
    all_to_all x4, blocking collectives, exchange(): lax.all_to_all(solve(terms, *solver, KEPT if last else ROWS), 'gx', 0, 0)  45.8 us
    all_to_all x4, blocking collectives, exchange(): terms = lax.all_to_all(out.message, 'gy', 0, 0)  37.4 us
    pallas_call x13, Pallas kernels, call(): pl.pallas_call(functools.partial(kernel, keys), in_specs=[VMEM_SPEC if v....  23.9 us
    all_to_all x1, blocking collectives, local(): received = lax.all_to_all(pieces, 'gx', 0, 0)  19.6 us
    ppermute x3, starting transfers between devices, exchange(): lax.ppermute(out.send_y_first, 'gy', swap_first(lines[1]))  6.63 us
    ppermute x3, starting transfers between devices, exchange(): lax.ppermute(out.send_x_second, 'gx', swap_second(lines[0]))  5.31 us
    all_to_all x1, starting transfers between devices, local(): gathered = lax.all_to_all(message, 'gy', 0, 0)  4.97 us
    all_to_all x1, waiting for transfers between devices, local(): gathered = lax.all_to_all(message, 'gy', 0, 0)  4.64 us
  transfers between devices with their start and end apart: 17, of which 1 were waited for; matrix products, arithmetic and copies ran while one was open for 0% of the time, Pallas kernels for 1%

profile of v3, /device:TPU:1, one launch (start us, length us, event | category | flops | bytes accessed | tf_op | source)
XLA Modules:
  0.0 169.9 jit_solution(4466391286383547470)
XLA Ops:
  2.2 3.0 %collective-permute-start = (f32[16,768]{1,0:T(8,128)}, f32[16,768]{1,0:T(8,128)S(1)}, u32[]{:S(2)}, u32[]{:S(2)}) collective-permute-start(f32[16,768]{1,0:T(8,128)} %get-tuple-element.84), channel_id=1, source_target_pairs={{0,1},{1,2},{2,3},{3,4},{4,5},{5,6},{6,7},{7,0},{8,9},{9,10},{10,1... | collective-permute-start | bytes 147464 | tf_op jit(solution)/shard_map/ppermute | solution.py:612
  6.6 5.0 %all-to-all-start = ((f32[8,8,128]{2,1,0:T(8,128)}), f32[8,8,128]{2,1,0:T(8,128)S(1)}, u32[]{:S(2)}, u32[]{:S(2)}) async-start(f32[8,8,128]{2,1,0:T(8,128)} %get-tuple-element.83), calls=%async_computation | async-start | bytes 65536 | tf_op jit(solution)/shard_map/all_to_all | solution.py:614
  11.6 4.6 %all-to-all-done.rhs_ref = f32[8,8,128]{2,1,0:T(8,128)S(1)} async-done(((f32[8,8,128]{2,1,0:T(8,128)}), f32[8,8,128]{2,1,0:T(8,128)S(1)}, u32[]{:S(2)}, u32[]{:S(2)}) %all-to-all-start) | async-done | bytes 32800 | tf_op jit(solution)/shard_map/all_to_all | solution.py:614
  18.7 19.6 %all_to_all.50.received_ref.refs_7_ = f32[16,96,128]{2,1,0:T(8,128)S(1)} all-to-all(f32[16,96,128]{2,1,0:T(8,128)S(1)} %get-tuple-element.93), channel_id=1, replica_groups=mesh['gx'=16,'gy'=8] {'gx'}, dimensions={0} | all-to-all | bytes 1572864 | tf_op jit(solution)/shard_map/all_to_all | solution.py:619
  40.2 4.2 %spread.1 = (bf16[640,320]{1,0:T(8,128)(2,1)S(1)}, bf16[640,320]{1,0:T(8,128)(2,1)S(1)}, bf16[1536,1536]{1,0:T(8,128)(2,1)S(1)}, bf16[1536,1536]{1,0:T(8,128)(2,1)S(1)}, f32[2,384,128]{2,1,0:T(8,128)S(1)}) custom-call(f32[16,96,128]{2,1,0:T(8,128)S(1)} %all_to_all.50.received_ref.refs_7_, bf16[256,320]{1,0:T(8,128)(2,1)S(1)} %copy-done.1, ...), custom_call_target="tpu_custom_call" | custom-call | tf_op jit(solution)/shard_map/spread/pallas_call | solution.py:279
  44.4 3.1 %update0.1 = (bf16[1536,256]{1,0:T(8,128)(2,1)S(1)}, f32[2,384,128]{2,1,0:T(8,128)S(1)}, f32[384,128]{1,0:T(8,128)S(1)}, f32[384,128]{1,0:T(8,128)S(1)}, f32[768,128]{1,0:T(8,128)S(1)}) custom-call(s32[6]{0:T(128)S(1)} %stack.43.place_ref.refs_0_.refs_5_, bf16[1536,1536]{1,0:T(8,128)(2,1)S(1)} %get-tuple-element.94.refs_1_, ...), custom_call_target="tpu_custom_call" | custom-call | flops 1207959552 | bytes 4096 | tf_op jit(solution)/shard_map/update0/pallas_call | solution.py:482
  47.5 2.2 %apply0.1 = (f32[2,384,128]{2,1,0:T(8,128)S(1)}, f32[384,128]{1,0:T(8,128)S(1)}, f32[384,128]{1,0:T(8,128)S(1)}) custom-call(s32[6]{0:T(128)S(1)} %stack.43.place_ref.refs_0_.refs_5_, bf16[1536,1536]{1,0:T(8,128)(2,1)S(1)} %get-tuple-element.94.refs_1_, bf16[1536,1536]{1,0:T(8,128)(2,1)S(1)} %get-tuple-element.95.refs_2_, ...), custom_call_target="tpu_custom_call" | custom-call | flops 1207959552 | bytes 4096 | tf_op jit(solution)/shard_map/apply0/pallas_call | solution.py:482
  54.0 9.7 %all_to_all.51.terms_ref = f32[8,40,128]{2,1,0:T(8,128)S(1)} all-to-all(f32[8,40,128]{2,1,0:T(8,128)S(1)} %terms0.1), channel_id=1, replica_groups=mesh['gx'=16,'gy'=8] {'gy'}, dimensions={0} | all-to-all | bytes 327680 | tf_op jit(solution)/shard_map/all_to_all | solution.py:641
  64.2 12.0 %all_to_all.52.refs_7_ = f32[16,40,128]{2,1,0:T(8,128)S(1)} all-to-all(f32[16,40,128]{2,1,0:T(8,128)S(1)} %solve.4), channel_id=1, replica_groups=mesh['gx'=16,'gy'=8] {'gx'}, dimensions={0} | all-to-all | bytes 655360 | tf_op jit(solution)/shard_map/all_to_all | solution.py:645
  76.1 2.9 %update1.1 = (bf16[1536,256]{1,0:T(8,128)(2,1)S(1)}, f32[2,384,128]{2,1,0:T(8,128)S(1)}, f32[384,128]{1,0:T(8,128)S(1)}, f32[384,128]{1,0:T(8,128)S(1)}, f32[1536,128]{1,0:T(8,128)S(1)}) custom-call(s32[6]{0:T(128)S(1)} %stack.43.place_ref.refs_0_.refs_5_, bf16[1536,1536]{1,0:T(8,128)(2,1)S(1)} %get-tuple-element.94.refs_1_, ...), custom_call_target="tpu_custom_call" | custom-call | flops 1207959552 | bytes 4096 | tf_op jit(solution)/shard_map/update1/pallas_call | solution.py:482
  79.0 2.2 %apply1.1 = (f32[2,384,128]{2,1,0:T(8,128)S(1)}, f32[384,128]{1,0:T(8,128)S(1)}, f32[384,128]{1,0:T(8,128)S(1)}) custom-call(s32[6]{0:T(128)S(1)} %stack.43.place_ref.refs_0_.refs_5_, bf16[1536,1536]{1,0:T(8,128)(2,1)S(1)} %get-tuple-element.94.refs_1_, bf16[1536,1536]{1,0:T(8,128)(2,1)S(1)} %get-tuple-element.95.refs_2_, ...), custom_call_target="tpu_custom_call" | custom-call | flops 1207959552 | bytes 4096 | tf_op jit(solution)/shard_map/apply1/pallas_call | solution.py:482
  81.2 2.4 %collective-permute-start.7 = (f32[384,128]{1,0:T(8,128)S(1)}, f32[384,128]{1,0:T(8,128)S(1)}, u32[]{:S(2)}, u32[]{:S(2)}) collective-permute-start(f32[384,128]{1,0:T(8,128)S(1)} %get-tuple-element.122), channel_id=1, source_target_pairs={{0,1},{1,0},{2,3},{3,2},{4,5},{5,4},{6,7},{7,6},{8,9},{9,8},{10,11... | collective-permute-start | bytes 589832 | tf_op jit(solution)/shard_map/ppermute | solution.py:637
  86.1 9.7 %all_to_all.53.terms_ref = f32[8,40,128]{2,1,0:T(8,128)S(1)} all-to-all(f32[8,40,128]{2,1,0:T(8,128)S(1)} %terms1.1), channel_id=1, replica_groups=mesh['gx'=16,'gy'=8] {'gy'}, dimensions={0} | all-to-all | bytes 327680 | tf_op jit(solution)/shard_map/all_to_all | solution.py:641
  96.2 12.0 %all_to_all.54.refs_7_ = f32[16,40,128]{2,1,0:T(8,128)S(1)} all-to-all(f32[16,40,128]{2,1,0:T(8,128)S(1)} %solve.5), channel_id=1, replica_groups=mesh['gx'=16,'gy'=8] {'gx'}, dimensions={0} | all-to-all | bytes 655360 | tf_op jit(solution)/shard_map/all_to_all | solution.py:645
  108.2 2.9 %update2.1 = (bf16[1536,256]{1,0:T(8,128)(2,1)S(1)}, f32[2,384,128]{2,1,0:T(8,128)S(1)}, f32[384,128]{1,0:T(8,128)S(1)}, f32[384,128]{1,0:T(8,128)S(1)}, f32[153...) custom-call(s32[6]{0:T(128)S(1)} %stack.43.place_ref.refs_0_.refs_5_, ...), custom_call_target="tpu_custom_call" | custom-call | flops 1207959552 | bytes 4096 | tf_op jit(solution)/shard_map/update2/pallas_call | solution.py:482
  111.2 2.2 %apply2.1 = (f32[2,384,128]{2,1,0:T(8,128)S(1)}, f32[384,128]{1,0:T(8,128)S(1)}, f32[384,128]{1,0:T(8,128)S(1)}) custom-call(s32[6]{0:T(128)S(1)} %stack.43.place_ref.refs_0_.refs_5_, bf16[1536,1536]{1,0:T(8,128)(2,1)S(1)} %get-tuple-element.94.refs_1_, bf16[1536,1536]{1,0:T(8,128)(2,1)S(1)} %get-tuple-element.95.refs_2_, ...), custom_call_target="tpu_custom_call" | custom-call | flops 1207959552 | bytes 4096 | tf_op jit(solution)/shard_map/apply2/pallas_call | solution.py:482
  113.3 2.4 %collective-permute-start.11 = (f32[384,128]{1,0:T(8,128)S(1)}, f32[384,128]{1,0:T(8,128)S(1)}, u32[]{:S(2)}, u32[]{:S(2)}) collective-permute-start(f32[384,128]{1,0:T(8,128)S(1)} %get-tuple-element.138), channel_id=1, source_target_pairs={{0,1},{1,0},{2,3},{3,2},{4,5},{5,4},{6,7},{7,6},{8,9},{9,8},{10,11... | collective-permute-start | bytes 589832 | tf_op jit(solution)/shard_map/ppermute | solution.py:637
  118.3 9.7 %all_to_all.55.terms_ref = f32[8,40,128]{2,1,0:T(8,128)S(1)} all-to-all(f32[8,40,128]{2,1,0:T(8,128)S(1)} %get-tuple-element.136), channel_id=1, replica_groups=mesh['gx'=16,'gy'=8] {'gy'}, dimensions={0} | all-to-all | bytes 327680 | tf_op jit(solution)/shard_map/all_to_all | solution.py:641
  128.5 12.0 %all_to_all.56.refs_7_ = f32[16,40,128]{2,1,0:T(8,128)S(1)} all-to-all(f32[16,40,128]{2,1,0:T(8,128)S(1)} %solve.6), channel_id=1, replica_groups=mesh['gx'=16,'gy'=8] {'gx'}, dimensions={0} | all-to-all | bytes 655360 | tf_op jit(solution)/shard_map/all_to_all | solution.py:645
  140.5 2.9 %update3.1 = (bf16[1536,256]{1,0:T(8,128)(2,1)S(1)}, f32[2,384,128]{2,1,0:T(8,128)S(1)}, f32[384,128]{1,0:T(8,128)S(1)}, f32[1536,128]{1,0:T(8,128)S(1)}, f32[1536,128]{1,0:T(8,128)S(1)}, /*index=5*/f32[8,128]{1,0:T(8,128)S(1)}) custom-call(s32[6]{0:T(128)S(1)} %stack.43.place_ref.refs_0_.refs_5_, bf16[1536,1536]{1,0:T(8,128)(2,1)S(1)} %get-tuple-element.94.refs_1_, ...), custom_call_target="tpu_custom_call" | custom-call | flops 1207959552 | bytes 4096 | tf_op jit(solution)/shard_map/update3/pallas_call | solution.py:482
  143.4 2.1 %apply3.1 = (f32[2,384,128]{2,1,0:T(8,128)S(1)}, f32[384,128]{1,0:T(8,128)S(1)}) custom-call(s32[6]{0:T(128)S(1)} %stack.43.place_ref.refs_0_.refs_5_, bf16[1536,1536]{1,0:T(8,128)(2,1)S(1)} %get-tuple-element.94.refs_1_, bf16[1536,1536]{1,0:T(8,128)(2,1)S(1)} %get-tuple-element.95.refs_2_, bf16[2,384,384]{2,1,0:T(8,128)(2,1)S(1)} %get-tuple-element.96.refs_3_, ...), custom_call_target="tpu_custom_call" | custom-call | flops 1207959552 | bytes 4096 | tf_op jit(solution)/shard_map/apply3/pallas_call | solution.py:482
  145.5 2.3 %collective-permute-start.15 = (f32[384,128]{1,0:T(8,128)S(1)}, f32[384,128]{1,0:T(8,128)S(1)}, u32[]{:S(2)}, u32[]{:S(2)}) collective-permute-start(f32[384,128]{1,0:T(8,128)S(1)} %get-tuple-element.155), channel_id=1, source_target_pairs={{0,7},{1,0},{2,1},{3,2},{4,3},{5,4},{6,5},{7,6},{8,15},{9,8},{10,9... | collective-permute-start | bytes 589832 | tf_op jit(solution)/shard_map/ppermute | solution.py:632
  149.5 8.3 %all_to_all.57.terms_ref = f32[8,40,128]{2,1,0:T(8,128)S(1)} all-to-all(f32[8,40,128]{2,1,0:T(8,128)S(1)} %get-tuple-element.153), channel_id=1, replica_groups=mesh['gx'=16,'gy'=8] {'gy'}, dimensions={0} | all-to-all | bytes 327680 | tf_op jit(solution)/shard_map/all_to_all | solution.py:641
  158.3 9.8 %all_to_all.58.refs_0_ = f32[16,24,128]{2,1,0:T(8,128)S(1)} all-to-all(f32[16,24,128]{2,1,0:T(8,128)S(1)} %solve.7), channel_id=1, replica_groups=mesh['gx'=16,'gy'=8] {'gx'}, dimensions={0} | all-to-all | bytes 393216 | tf_op jit(solution)/shard_map/all_to_all | solution.py:645
  (46 shorter events, 21.9 us)
Async XLA Ops:
  2.2 14.0 %collective-permute-start = (f32[16,768]{1,0:T(8,128)}, f32[16,768]{1,0:T(8,128)S(1)}, u32[]{:S(2)}, u32[]{:S(2)}) collective-permute-start(f32[16,768]{1,0:T(8,128)} %get-tuple-element.84), channel_id=1, source_target_pairs={{0,1},{1,2},{2,3},{3,4},{4,5},{5,6},{6,7},{7,0},{8,9},{9,10},{10,1... | collective-permute-start | bytes 147464 | tf_op jit(solution)/shard_map/ppermute | solution.py:612
  5.3 11.0 %collective-permute-start.1 = (f32[16,768]{1,0:T(8,128)}, f32[16,768]{1,0:T(8,128)S(1)}, u32[]{:S(2)}, u32[]{:S(2)}) collective-permute-start(f32[16,768]{1,0:T(8,128)} %get-tuple-element.85), channel_id=1, source_target_pairs={{0,8},{8,16},{16,24},{24,32},{32,40},{40,48},{48,56},{56,64},{64,7... | collective-permute-start | bytes 147464 | tf_op jit(solution)/shard_map/ppermute | solution.py:613
  6.6 9.7 %all-to-all-start = ((f32[8,8,128]{2,1,0:T(8,128)}), f32[8,8,128]{2,1,0:T(8,128)S(1)}, u32[]{:S(2)}, u32[]{:S(2)}) async-start(f32[8,8,128]{2,1,0:T(8,128)} %get-tuple-element.83), calls=%async_computation | async-start | bytes 65536 | tf_op jit(solution)/shard_map/all_to_all | solution.py:614
  16.3 0.9 copy-start.2
  38.3 1.0 copy-start
  39.3 0.9 copy-start.1
  49.7 14.0 %collective-permute-start.3 = (f32[384,128]{1,0:T(8,128)S(1)}, f32[384,128]{1,0:T(8,128)S(1)}, u32[]{:S(2)}, u32[]{:S(2)}) collective-permute-start(f32[384,128]{1,0:T(8,128)S(1)} %get-tuple-element.106), channel_id=1, source_target_pairs={{0,1},{1,0},{2,3},{3,2},{4,5},{5,4},{6,7},{7,6},{8,9},{9,8},{10,11... | collective-permute-start | bytes 589832 | tf_op jit(solution)/shard_map/ppermute | solution.py:637
  51.5 12.2 %collective-permute-start.5 = (f32[384,128]{1,0:T(8,128)S(1)}, f32[384,128]{1,0:T(8,128)S(1)}, u32[]{:S(2)}, u32[]{:S(2)}) collective-permute-start(f32[384,128]{1,0:T(8,128)S(1)} %get-tuple-element.108), channel_id=1, source_target_pairs={{0,7},{1,2},{2,1},{3,4},{4,3},{5,6},{6,5},{7,0},{8,15},{9,10},{10,... | collective-permute-start | bytes 589832 | tf_op jit(solution)/shard_map/ppermute | solution.py:639
  51.8 11.9 %collective-permute-start.2 = (f32[384,128]{1,0:T(8,128)S(1)}, f32[384,128]{1,0:T(8,128)S(1)}, u32[]{:S(2)}, u32[]{:S(2)}) collective-permute-start(f32[384,128]{1,0:T(8,128)S(1)} %get-tuple-element.105), channel_id=1, source_target_pairs={{0,8},{8,0},{16,24},{24,16},{32,40},{40,32},{48,56},{56,48},{64,72... | collective-permute-start | bytes 589832 | tf_op jit(solution)/shard_map/ppermute | solution.py:636
  51.9 11.8 %collective-permute-start.4 = (f32[384,128]{1,0:T(8,128)S(1)}, f32[384,128]{1,0:T(8,128)S(1)}, u32[]{:S(2)}, u32[]{:S(2)}) collective-permute-start(f32[384,128]{1,0:T(8,128)S(1)} %get-tuple-element.107), channel_id=1, source_target_pairs={{0,120},{8,16},{16,8},{24,32},{32,24},{40,48},{48,40},{56,64},{64,... | collective-permute-start | bytes 589832 | tf_op jit(solution)/shard_map/ppermute | solution.py:638
  81.2 14.6 %collective-permute-start.7 = (f32[384,128]{1,0:T(8,128)S(1)}, f32[384,128]{1,0:T(8,128)S(1)}, u32[]{:S(2)}, u32[]{:S(2)}) collective-permute-start(f32[384,128]{1,0:T(8,128)S(1)} %get-tuple-element.122), channel_id=1, source_target_pairs={{0,1},{1,0},{2,3},{3,2},{4,5},{5,4},{6,7},{7,6},{8,9},{9,8},{10,11... | collective-permute-start | bytes 589832 | tf_op jit(solution)/shard_map/ppermute | solution.py:637
  83.6 12.2 %collective-permute-start.9 = (f32[384,128]{1,0:T(8,128)S(1)}, f32[384,128]{1,0:T(8,128)S(1)}, u32[]{:S(2)}, u32[]{:S(2)}) collective-permute-start(f32[384,128]{1,0:T(8,128)S(1)} %get-tuple-element.124), channel_id=1, source_target_pairs={{0,7},{1,2},{2,1},{3,4},{4,3},{5,6},{6,5},{7,0},{8,15},{9,10},{10,... | collective-permute-start | bytes 589832 | tf_op jit(solution)/shard_map/ppermute | solution.py:639
  83.8 11.9 %collective-permute-start.6 = (f32[384,128]{1,0:T(8,128)S(1)}, f32[384,128]{1,0:T(8,128)S(1)}, u32[]{:S(2)}, u32[]{:S(2)}) collective-permute-start(f32[384,128]{1,0:T(8,128)S(1)} %get-tuple-element.121), channel_id=1, source_target_pairs={{0,8},{8,0},{16,24},{24,16},{32,40},{40,32},{48,56},{56,48},{64,72... | collective-permute-start | bytes 589832 | tf_op jit(solution)/shard_map/ppermute | solution.py:636
  84.0 11.8 %collective-permute-start.8 = (f32[384,128]{1,0:T(8,128)S(1)}, f32[384,128]{1,0:T(8,128)S(1)}, u32[]{:S(2)}, u32[]{:S(2)}) collective-permute-start(f32[384,128]{1,0:T(8,128)S(1)} %get-tuple-element.123), channel_id=1, source_target_pairs={{0,120},{8,16},{16,8},{24,32},{32,24},{40,48},{48,40},{56,64},{64,... | collective-permute-start | bytes 589832 | tf_op jit(solution)/shard_map/ppermute | solution.py:638
  113.3 14.7 %collective-permute-start.11 = (f32[384,128]{1,0:T(8,128)S(1)}, f32[384,128]{1,0:T(8,128)S(1)}, u32[]{:S(2)}, u32[]{:S(2)}) collective-permute-start(f32[384,128]{1,0:T(8,128)S(1)} %get-tuple-element.138), channel_id=1, source_target_pairs={{0,1},{1,0},{2,3},{3,2},{4,5},{5,4},{6,7},{7,6},{8,9},{9,8},{10,11... | collective-permute-start | bytes 589832 | tf_op jit(solution)/shard_map/ppermute | solution.py:637
  115.7 12.3 %collective-permute-start.13 = (f32[384,128]{1,0:T(8,128)S(1)}, f32[384,128]{1,0:T(8,128)S(1)}, u32[]{:S(2)}, u32[]{:S(2)}) collective-permute-start(f32[384,128]{1,0:T(8,128)S(1)} %get-tuple-element.140), channel_id=1, source_target_pairs={{0,7},{1,2},{2,1},{3,4},{4,3},{5,6},{6,5},{7,0},{8,15},{9,10},{10,... | collective-permute-start | bytes 589832 | tf_op jit(solution)/shard_map/ppermute | solution.py:639
  116.0 12.0 %collective-permute-start.10 = (f32[384,128]{1,0:T(8,128)S(1)}, f32[384,128]{1,0:T(8,128)S(1)}, u32[]{:S(2)}, u32[]{:S(2)}) collective-permute-start(f32[384,128]{1,0:T(8,128)S(1)} %get-tuple-element.137), channel_id=1, source_target_pairs={{0,8},{8,0},{16,24},{24,16},{32,40},{40,32},{48,56},{56,48},{64,72... | collective-permute-start | bytes 589832 | tf_op jit(solution)/shard_map/ppermute | solution.py:636
  116.1 11.9 %collective-permute-start.12 = (f32[384,128]{1,0:T(8,128)S(1)}, f32[384,128]{1,0:T(8,128)S(1)}, u32[]{:S(2)}, u32[]{:S(2)}) collective-permute-start(f32[384,128]{1,0:T(8,128)S(1)} %get-tuple-element.139), channel_id=1, source_target_pairs={{0,120},{8,16},{16,8},{24,32},{32,24},{40,48},{48,40},{56,64},{64,... | collective-permute-start | bytes 589832 | tf_op jit(solution)/shard_map/ppermute | solution.py:638
  145.5 12.3 %collective-permute-start.15 = (f32[384,128]{1,0:T(8,128)S(1)}, f32[384,128]{1,0:T(8,128)S(1)}, u32[]{:S(2)}, u32[]{:S(2)}) collective-permute-start(f32[384,128]{1,0:T(8,128)S(1)} %get-tuple-element.155), channel_id=1, source_target_pairs={{0,7},{1,0},{2,1},{3,2},{4,3},{5,4},{6,5},{7,6},{8,15},{9,8},{10,9... | collective-permute-start | bytes 589832 | tf_op jit(solution)/shard_map/ppermute | solution.py:632
  147.9 10.0 %collective-permute-start.14 = (f32[384,128]{1,0:T(8,128)S(1)}, f32[384,128]{1,0:T(8,128)S(1)}, u32[]{:S(2)}, u32[]{:S(2)}) collective-permute-start(f32[384,128]{1,0:T(8,128)S(1)} %get-tuple-element.154), channel_id=1, source_target_pairs={{0,120},{8,0},{16,8},{24,16},{32,24},{40,32},{48,40},{56,48},{64,5... | collective-permute-start | bytes 589832 | tf_op jit(solution)/shard_map/ppermute | solution.py:631

commit v4 on v3

--- a/solution.py
+++ b/solution.py
@@ -3,7 +3,6 @@
 
 import jax
 import jax.numpy as jnp
-import numpy as np
 from jax import lax
 from jax.experimental import pallas as pl
 from jax.experimental.pallas import tpu as pltpu
@@ -19,6 +18,7 @@
 TROWS = 48
 LAST = 3
 FLAGS = 6
+PACKED = 32
 KEPT = 3 * GROUP
 TAIL = 16
 STEP_MB = 16
@@ -217,29 +217,28 @@
     )(place, own, west, north, rhs)
 
 
-def expansion(lines):
-    span = MODES * lines[1]
-    out = np.zeros((256, lines[1] * ROWS), np.float32)
-    for source in range(lines[1]):
+def expansion(table_ref, columns):
+    span = MODES * columns
+    table_ref[...] = jnp.zeros_like(table_ref)
+    row = lax.broadcasted_iota(jnp.int32, (MODES, MODES), 0)
+    one = jnp.where(row == lax.broadcasted_iota(jnp.int32, (MODES, MODES), 1), 1.0, 0.0)
+    for source in range(columns):
         places = [(0, source), (0, source + 1), (1, source), (0, source - 1), (-1, source)]
         for member, (down, column) in enumerate(places):
-            if 0 <= column < lines[1]:
-                for mode in range(MODES):
-                    at = span * (1 + down) + MODES * column + mode
-                    out[at, source * ROWS + member * GROUP + mode] = 1.0
-    return jnp.asarray(out, BF16)
+            if 0 <= column < columns:
+                to = span * (1 + down) + MODES * column
+                at = source * ROWS + member * GROUP
+                table_ref[to : to + MODES, at : at + MODES] = one
 
 
 def spread_kernel(
-    received_ref, expand_in, operator_ref, loads_in,
+    received_ref, operator_ref, loads_in,
     high_ref, low_ref, a_high_ref, a_low_ref, loads_ref,
-    tail_ref, held_ref, expand_ref, sems, loads_sem, expand_sem,
+    tail_ref, held_ref, expand_ref, sems, loads_sem,
 ):
     size = operator_ref.shape[0]
     count = sems.shape[0]
     block = size // count
-    expand_copy = pltpu.make_async_copy(expand_in, expand_ref, expand_sem)
-    expand_copy.start()
     copies = []
     for part in range(count):
         rows = pl.ds(part * block, block)
@@ -257,11 +256,12 @@
         tail_ref[:, member * GROUP : (member + 1) * GROUP, 0:tail] = packed[
             :, :, member * tail : (member + 1) * tail
         ]
-    expand_copy.wait()
+    expansion(expand_ref, expand_ref.shape[1] // ROWS)
+    expand = expand_ref[...].astype(BF16)
     head = split(received_ref[:, 0:ROWS, :].reshape(lines * ROWS, cases))
     rest = split(tail_ref[...].reshape(lines * ROWS, cases))
     for first, last, out in zip(head, rest, (high_ref, low_ref)):
-        result = mm(first, expand_ref[0:cases]) + mm(last, expand_ref[cases : 2 * cases])
+        result = mm(first, expand[0:cases]) + mm(last, expand[cases : 2 * cases])
         out[...] = result.astype(BF16)
     for part in range(count):
         copies[part].wait()
@@ -272,25 +272,25 @@
     loads_copy.wait()
 
 
-def spread(received, expand, operator, loads):
+def spread(received, columns, operator, loads):
     lines, _, cases = received.shape
-    shape = (lines * ROWS, expand.shape[1])
+    shape = (lines * ROWS, columns * ROWS)
     size = operator.shape[0]
     return pl.pallas_call(
         spread_kernel,
-        in_specs=[VMEM_SPEC] + [pl.BlockSpec(memory_space=pl.ANY)] * 3,
+        in_specs=[VMEM_SPEC] + [pl.BlockSpec(memory_space=pl.ANY)] * 2,
         out_specs=[VMEM_SPEC] * 5,
         out_shape=[jax.ShapeDtypeStruct(shape, BF16)] * 2
         + [jax.ShapeDtypeStruct((size, size), BF16)] * 2
         + [jax.ShapeDtypeStruct(loads.shape, F32)],
         scratch_shapes=[
             pltpu.VMEM((lines, ROWS, cases), F32), pltpu.VMEM((size, size), F32),
-            pltpu.VMEM(expand.shape, BF16),
-            pltpu.SemaphoreType.DMA((8,)), pltpu.SemaphoreType.DMA, pltpu.SemaphoreType.DMA,
+            pltpu.VMEM((2 * cases, columns * ROWS), F32),
+            pltpu.SemaphoreType.DMA((8,)), pltpu.SemaphoreType.DMA,
         ],
         compiler_params=params(40),
         name="spread",
-    )(received, expand, operator, loads)
+    )(received, operator, loads)
 
 
 def solve_kernel(terms_ref, high_ref, low_ref, out_ref):
@@ -302,7 +302,17 @@
     total = jnp.sum(terms, axis=0)
     place = lax.broadcasted_iota(jnp.int32, (rows, cases), 0)
     scalar = (place % GROUP) >= MODES
-    out_ref[...] = jnp.where(scalar[None], total[None], result)[:, :kept]
+    if kept == PACKED:
+        for member in range(MEMBERS):
+            out_ref[:, member * MODES : (member + 1) * MODES, :] = result[
+                :, member * GROUP : member * GROUP + MODES
+            ]
+        sums = total[MODES:GROUP]
+        out_ref[:, MEMBERS * MODES : PACKED, :] = jnp.broadcast_to(
+            sums[None], (out_ref.shape[0],) + sums.shape
+        )
+    else:
+        out_ref[...] = jnp.where(scalar[None], total[None], result)[:, :kept]
 
 
 def solve(terms, high, low, kept):
@@ -393,6 +403,12 @@
         r.lam_out[...] = field[:half]
     else:
         total = jnp.sum(r.parts[...], axis=0)
+        if total.shape[0] == PACKED:
+            for member in range(MEMBERS):
+                at = member * GROUP
+                r.grouped[at : at + MODES, :] = total[member * MODES : (member + 1) * MODES]
+                r.grouped[at + MODES : at + GROUP, :] = total[MEMBERS * MODES : PACKED]
+            total = r.grouped[...]
         moved = field_image(r) - lift(member_alpha(total), r.g_high, r.g_low)
         if phase == 1:
             field = moved
@@ -520,6 +536,7 @@
         scratch = dict(rhs=pltpu.VMEM((MODES * lines[0] * lines[1], cases), F32))
     else:
         shapes.update(p_out=field)
+        scratch = dict(grouped=pltpu.VMEM((ROWS, cases), F32))
     if phase >= 2:
         shapes.update(q_out=field, scal_out=(8, cases))
     update = call(
@@ -555,7 +572,7 @@
         flops=half_flops // 4,
     )
     out = SimpleNamespace(**{**vars(update), **vars(apply), **vars(terms)})
-    exchange(out, phase == LAST)
+    exchange(out, phase)
     return out
 
 
@@ -618,14 +635,16 @@
     )
     received = lax.all_to_all(pieces, "gx", 0, 0)
     *solver, a_high, a_low, held_loads = spread(
-        received, expansion(lines), operator, loads[0, 0]
+        received, lines[1], operator, loads[0, 0]
     )
     table = SimpleNamespace(
         parity=parity, a_high=a_high, a_low=a_low, mask=mask, t_high=t_high, t_low=t_low,
         g_high=g_high, g_low=g_low, gives=gives, takes=takes,
     )
 
-    def exchange(out, last):
+    def exchange(out, phase):
+        last = phase == LAST
+        kept = {0: PACKED, 1: PACKED, LAST: KEPT}.get(phase, ROWS)
         if last:
             halos = [
                 lax.ppermute(out.send_x_first, "gx", shift(lines[0], -1)),
@@ -642,7 +661,7 @@
         terms, *halos = lax.optimization_barrier((terms, *halos))
         out.x_first, out.y_first = halos[:2]
         out.x_second, out.y_second = (None, None) if last else halos[2:]
-        out.parts = lax.all_to_all(solve(terms, *solver, KEPT if last else ROWS), "gx", 0, 0)
+        out.parts = lax.all_to_all(solve(terms, *solver, kept), "gx", 0, 0)
         out.z_x, out.z_y = out.z_x_out, out.z_y_out
 
     run = functools.partial(step, lines=lines, table=table, exchange=exchange)

time: 172 us -> 170 us (0.988)
  no operation moved by 1% of the time
where the time goes in v4:
time: 170 us; the launch traced here: 168 us
  blocking collectives  102 us (60%)
  Pallas kernels  32.8 us (19%)
  starting transfers between devices  25.7 us (15%)
  waiting for transfers between devices  4.68 us (3%)
  local copies, waits for them, and re-layouts  1.99 us (1%)
    all_to_all x4, blocking collectives, exchange(): out.parts = lax.all_to_all(solve(terms, *solver, kept), 'gx', 0, 0)  45 us
    all_to_all x4, blocking collectives, exchange(): terms = lax.all_to_all(out.message, 'gy', 0, 0)  37.4 us
    pallas_call x13, Pallas kernels, call(): pl.pallas_call(functools.partial(kernel, keys), in_specs=[VMEM_SPEC if v....  24 us
    all_to_all x1, blocking collectives, local(): received = lax.all_to_all(pieces, 'gx', 0, 0)  19.6 us
    ppermute x3, starting transfers between devices, exchange(): lax.ppermute(out.send_y_first, 'gy', swap_first(lines[1]))  6.6 us
    ppermute x3, starting transfers between devices, exchange(): lax.ppermute(out.send_x_second, 'gx', swap_second(lines[0]))  5.35 us
    all_to_all x1, starting transfers between devices, local(): gathered = lax.all_to_all(message, 'gy', 0, 0)  4.97 us
    all_to_all x1, waiting for transfers between devices, local(): gathered = lax.all_to_all(message, 'gy', 0, 0)  4.64 us
  transfers between devices with their start and end apart: 17, of which 1 were waited for; matrix products, arithmetic and copies ran while one was open for 0% of the time, Pallas kernels for 1%

profile of v4, /device:TPU:1, one launch (start us, length us, event | category | flops | bytes accessed | tf_op | source)
XLA Modules:
  0.0 168.0 jit_solution(8183169080573750108)
XLA Ops:
  2.2 3.0 %collective-permute-start = (f32[16,768]{1,0:T(8,128)}, f32[16,768]{1,0:T(8,128)S(1)}, u32[]{:S(2)}, u32[]{:S(2)}) collective-permute-start(f32[16,768]{1,0:T(8,128)} %get-tuple-element.84), channel_id=1, source_target_pairs={{0,1},{1,2},{2,3},{3,4},{4,5},{5,6},{6,7},{7,0},{8,9},{9,10},{10,1... | collective-permute-start | bytes 147464 | tf_op jit(solution)/shard_map/ppermute | solution.py:629
  6.6 5.0 %all-to-all-start = ((f32[8,8,128]{2,1,0:T(8,128)}), f32[8,8,128]{2,1,0:T(8,128)S(1)}, u32[]{:S(2)}, u32[]{:S(2)}) async-start(f32[8,8,128]{2,1,0:T(8,128)} %get-tuple-element.83), calls=%async_computation | async-start | bytes 65536 | tf_op jit(solution)/shard_map/all_to_all | solution.py:631
  11.6 4.6 %all-to-all-done.rhs_ref = f32[8,8,128]{2,1,0:T(8,128)S(1)} async-done(((f32[8,8,128]{2,1,0:T(8,128)}), f32[8,8,128]{2,1,0:T(8,128)S(1)}, u32[]{:S(2)}, u32[]{:S(2)}) %all-to-all-start) | async-done | bytes 32800 | tf_op jit(solution)/shard_map/all_to_all | solution.py:631
  18.7 19.6 %all_to_all.50.received_ref.refs_7_ = f32[16,96,128]{2,1,0:T(8,128)S(1)} all-to-all(f32[16,96,128]{2,1,0:T(8,128)S(1)} %get-tuple-element.93), channel_id=1, replica_groups=mesh['gx'=16,'gy'=8] {'gx'}, dimensions={0} | all-to-all | bytes 1572864 | tf_op jit(solution)/shard_map/all_to_all | solution.py:636
  39.2 4.0 %spread.1 = (bf16[640,320]{1,0:T(8,128)(2,1)S(1)}, bf16[640,320]{1,0:T(8,128)(2,1)S(1)}, bf16[1536,1536]{1,0:T(8,128)(2,1)S(1)}, bf16[1536,1536]{1,0:T(8,128)(2,1)S(1)}, f32[2,384,128]{2,1,0:T(8,128)S(1)}) custom-call(f32[16,96,128]{2,1,0:T(8,128)S(1)} %all_to_all.50.received_ref.refs_7_, f32[1536,1536]{1,0:T(8,128)} %bitcast.18, f32[2,384,128]{2,1,0:T(8,128)S(1)} %bitcast.17), custom_call_target="tpu_custom_call" | custom-call | tf_op jit(solution)/shard_map/spread/pallas_call | solution.py:279
  43.2 3.2 %update0.1 = (bf16[1536,256]{1,0:T(8,128)(2,1)S(1)}, f32[2,384,128]{2,1,0:T(8,128)S(1)}, f32[384,128]{1,0:T(8,128)S(1)}, f32[384,128]{1,0:T(8,128)S(1)}, f32[768,128]{1,0:T(8,128)S(1)}) custom-call(s32[6]{0:T(128)S(1)} %stack.43.place_ref.refs_0_.refs_5_, bf16[1536,1536]{1,0:T(8,128)(2,1)S(1)} %get-tuple-element.94.refs_1_, ...), custom_call_target="tpu_custom_call" | custom-call | flops 1207959552 | bytes 4096 | tf_op jit(solution)/shard_map/update0/pallas_call | solution.py:498
  46.4 2.2 %apply0.1 = (f32[2,384,128]{2,1,0:T(8,128)S(1)}, f32[384,128]{1,0:T(8,128)S(1)}, f32[384,128]{1,0:T(8,128)S(1)}) custom-call(s32[6]{0:T(128)S(1)} %stack.43.place_ref.refs_0_.refs_5_, bf16[1536,1536]{1,0:T(8,128)(2,1)S(1)} %get-tuple-element.94.refs_1_, bf16[1536,1536]{1,0:T(8,128)(2,1)S(1)} %get-tuple-element.95.refs_2_, ...), custom_call_target="tpu_custom_call" | custom-call | flops 1207959552 | bytes 4096 | tf_op jit(solution)/shard_map/apply0/pallas_call | solution.py:498
  52.8 9.7 %all_to_all.51.terms_ref = f32[8,40,128]{2,1,0:T(8,128)S(1)} all-to-all(f32[8,40,128]{2,1,0:T(8,128)S(1)} %terms0.1), channel_id=1, replica_groups=mesh['gx'=16,'gy'=8] {'gy'}, dimensions={0} | all-to-all | bytes 327680 | tf_op jit(solution)/shard_map/all_to_all | solution.py:660
  63.0 11.6 %all_to_all.52.refs_7_ = f32[16,32,128]{2,1,0:T(8,128)S(1)} all-to-all(f32[16,32,128]{2,1,0:T(8,128)S(1)} %solve.4), channel_id=1, replica_groups=mesh['gx'=16,'gy'=8] {'gx'}, dimensions={0} | all-to-all | bytes 524288 | tf_op jit(solution)/shard_map/all_to_all | solution.py:664
  74.6 2.9 %update1.1 = (bf16[1536,256]{1,0:T(8,128)(2,1)S(1)}, f32[2,384,128]{2,1,0:T(8,128)S(1)}, f32[384,128]{1,0:T(8,128)S(1)}, f32[384,128]{1,0:T(8,128)S(1)}, f32[1536,128]{1,0:T(8,128)S(1)}) custom-call(s32[6]{0:T(128)S(1)} %stack.43.place_ref.refs_0_.refs_5_, bf16[1536,1536]{1,0:T(8,128)(2,1)S(1)} %get-tuple-element.94.refs_1_, ...), custom_call_target="tpu_custom_call" | custom-call | flops 1207959552 | bytes 4096 | tf_op jit(solution)/shard_map/update1/pallas_call | solution.py:498
  77.5 2.2 %apply1.1 = (f32[2,384,128]{2,1,0:T(8,128)S(1)}, f32[384,128]{1,0:T(8,128)S(1)}, f32[384,128]{1,0:T(8,128)S(1)}) custom-call(s32[6]{0:T(128)S(1)} %stack.43.place_ref.refs_0_.refs_5_, bf16[1536,1536]{1,0:T(8,128)(2,1)S(1)} %get-tuple-element.94.refs_1_, bf16[1536,1536]{1,0:T(8,128)(2,1)S(1)} %get-tuple-element.95.refs_2_, ...), custom_call_target="tpu_custom_call" | custom-call | flops 1207959552 | bytes 4096 | tf_op jit(solution)/shard_map/apply1/pallas_call | solution.py:498
  79.7 2.4 %collective-permute-start.7 = (f32[384,128]{1,0:T(8,128)S(1)}, f32[384,128]{1,0:T(8,128)S(1)}, u32[]{:S(2)}, u32[]{:S(2)}) collective-permute-start(f32[384,128]{1,0:T(8,128)S(1)} %get-tuple-element.122), channel_id=1, source_target_pairs={{0,1},{1,0},{2,3},{3,2},{4,5},{5,4},{6,7},{7,6},{8,9},{9,8},{10,11... | collective-permute-start | bytes 589832 | tf_op jit(solution)/shard_map/ppermute | solution.py:656
  84.5 9.7 %all_to_all.53.terms_ref = f32[8,40,128]{2,1,0:T(8,128)S(1)} all-to-all(f32[8,40,128]{2,1,0:T(8,128)S(1)} %terms1.1), channel_id=1, replica_groups=mesh['gx'=16,'gy'=8] {'gy'}, dimensions={0} | all-to-all | bytes 327680 | tf_op jit(solution)/shard_map/all_to_all | solution.py:660
  94.7 11.6 %all_to_all.54.refs_7_ = f32[16,32,128]{2,1,0:T(8,128)S(1)} all-to-all(f32[16,32,128]{2,1,0:T(8,128)S(1)} %solve.5), channel_id=1, replica_groups=mesh['gx'=16,'gy'=8] {'gx'}, dimensions={0} | all-to-all | bytes 524288 | tf_op jit(solution)/shard_map/all_to_all | solution.py:664
  106.3 2.9 %update2.1 = (bf16[1536,256]{1,0:T(8,128)(2,1)S(1)}, f32[2,384,128]{2,1,0:T(8,128)S(1)}, f32[384,128]{1,0:T(8,128)S(1)}, f32[384,128]{1,0:T(8,128)S(1)}, f32[153...) custom-call(s32[6]{0:T(128)S(1)} %stack.43.place_ref.refs_0_.refs_5_, ...), custom_call_target="tpu_custom_call" | custom-call | flops 1207959552 | bytes 4096 | tf_op jit(solution)/shard_map/update2/pallas_call | solution.py:498
  109.2 2.2 %apply2.1 = (f32[2,384,128]{2,1,0:T(8,128)S(1)}, f32[384,128]{1,0:T(8,128)S(1)}, f32[384,128]{1,0:T(8,128)S(1)}) custom-call(s32[6]{0:T(128)S(1)} %stack.43.place_ref.refs_0_.refs_5_, bf16[1536,1536]{1,0:T(8,128)(2,1)S(1)} %get-tuple-element.94.refs_1_, bf16[1536,1536]{1,0:T(8,128)(2,1)S(1)} %get-tuple-element.95.refs_2_, ...), custom_call_target="tpu_custom_call" | custom-call | flops 1207959552 | bytes 4096 | tf_op jit(solution)/shard_map/apply2/pallas_call | solution.py:498
  111.4 2.4 %collective-permute-start.11 = (f32[384,128]{1,0:T(8,128)S(1)}, f32[384,128]{1,0:T(8,128)S(1)}, u32[]{:S(2)}, u32[]{:S(2)}) collective-permute-start(f32[384,128]{1,0:T(8,128)S(1)} %get-tuple-element.138), channel_id=1, source_target_pairs={{0,1},{1,0},{2,3},{3,2},{4,5},{5,4},{6,7},{7,6},{8,9},{9,8},{10,11... | collective-permute-start | bytes 589832 | tf_op jit(solution)/shard_map/ppermute | solution.py:656
  116.4 9.7 %all_to_all.55.terms_ref = f32[8,40,128]{2,1,0:T(8,128)S(1)} all-to-all(f32[8,40,128]{2,1,0:T(8,128)S(1)} %get-tuple-element.136), channel_id=1, replica_groups=mesh['gx'=16,'gy'=8] {'gy'}, dimensions={0} | all-to-all | bytes 327680 | tf_op jit(solution)/shard_map/all_to_all | solution.py:660
  126.5 12.0 %all_to_all.56.refs_7_ = f32[16,40,128]{2,1,0:T(8,128)S(1)} all-to-all(f32[16,40,128]{2,1,0:T(8,128)S(1)} %solve.6), channel_id=1, replica_groups=mesh['gx'=16,'gy'=8] {'gx'}, dimensions={0} | all-to-all | bytes 655360 | tf_op jit(solution)/shard_map/all_to_all | solution.py:664
  138.5 2.9 %update3.1 = (bf16[1536,256]{1,0:T(8,128)(2,1)S(1)}, f32[2,384,128]{2,1,0:T(8,128)S(1)}, f32[384,128]{1,0:T(8,128)S(1)}, f32[1536,128]{1,0:T(8,128)S(1)}, f32[1536,128]{1,0:T(8,128)S(1)}, /*index=5*/f32[8,128]{1,0:T(8,128)S(1)}) custom-call(s32[6]{0:T(128)S(1)} %stack.43.place_ref.refs_0_.refs_5_, bf16[1536,1536]{1,0:T(8,128)(2,1)S(1)} %get-tuple-element.94.refs_1_, ...), custom_call_target="tpu_custom_call" | custom-call | flops 1207959552 | bytes 4096 | tf_op jit(solution)/shard_map/update3/pallas_call | solution.py:498
  141.5 2.1 %apply3.1 = (f32[2,384,128]{2,1,0:T(8,128)S(1)}, f32[384,128]{1,0:T(8,128)S(1)}) custom-call(s32[6]{0:T(128)S(1)} %stack.43.place_ref.refs_0_.refs_5_, bf16[1536,1536]{1,0:T(8,128)(2,1)S(1)} %get-tuple-element.94.refs_1_, bf16[1536,1536]{1,0:T(8,128)(2,1)S(1)} %get-tuple-element.95.refs_2_, bf16[2,384,384]{2,1,0:T(8,128)(2,1)S(1)} %get-tuple-element.96.refs_3_, ...), custom_call_target="tpu_custom_call" | custom-call | flops 1207959552 | bytes 4096 | tf_op jit(solution)/shard_map/apply3/pallas_call | solution.py:498
  143.6 2.3 %collective-permute-start.15 = (f32[384,128]{1,0:T(8,128)S(1)}, f32[384,128]{1,0:T(8,128)S(1)}, u32[]{:S(2)}, u32[]{:S(2)}) collective-permute-start(f32[384,128]{1,0:T(8,128)S(1)} %get-tuple-element.155), channel_id=1, source_target_pairs={{0,7},{1,0},{2,1},{3,2},{4,3},{5,4},{6,5},{7,6},{8,15},{9,8},{10,9... | collective-permute-start | bytes 589832 | tf_op jit(solution)/shard_map/ppermute | solution.py:651
  147.6 8.3 %all_to_all.57.terms_ref = f32[8,40,128]{2,1,0:T(8,128)S(1)} all-to-all(f32[8,40,128]{2,1,0:T(8,128)S(1)} %get-tuple-element.153), channel_id=1, replica_groups=mesh['gx'=16,'gy'=8] {'gy'}, dimensions={0} | all-to-all | bytes 327680 | tf_op jit(solution)/shard_map/all_to_all | solution.py:660
  156.3 9.8 %all_to_all.58.refs_0_ = f32[16,24,128]{2,1,0:T(8,128)S(1)} all-to-all(f32[16,24,128]{2,1,0:T(8,128)S(1)} %solve.7), channel_id=1, replica_groups=mesh['gx'=16,'gy'=8] {'gx'}, dimensions={0} | all-to-all | bytes 393216 | tf_op jit(solution)/shard_map/all_to_all | solution.py:664
  (44 shorter events, 21.0 us)
Async XLA Ops:
  2.2 14.0 %collective-permute-start = (f32[16,768]{1,0:T(8,128)}, f32[16,768]{1,0:T(8,128)S(1)}, u32[]{:S(2)}, u32[]{:S(2)}) collective-permute-start(f32[16,768]{1,0:T(8,128)} %get-tuple-element.84), channel_id=1, source_target_pairs={{0,1},{1,2},{2,3},{3,4},{4,5},{5,6},{6,7},{7,0},{8,9},{9,10},{10,1... | collective-permute-start | bytes 147464 | tf_op jit(solution)/shard_map/ppermute | solution.py:629
  5.3 11.0 %collective-permute-start.1 = (f32[16,768]{1,0:T(8,128)}, f32[16,768]{1,0:T(8,128)S(1)}, u32[]{:S(2)}, u32[]{:S(2)}) collective-permute-start(f32[16,768]{1,0:T(8,128)} %get-tuple-element.85), channel_id=1, source_target_pairs={{0,8},{8,16},{16,24},{24,32},{32,40},{40,48},{48,56},{56,64},{64,7... | collective-permute-start | bytes 147464 | tf_op jit(solution)/shard_map/ppermute | solution.py:630
  6.6 9.7 %all-to-all-start = ((f32[8,8,128]{2,1,0:T(8,128)}), f32[8,8,128]{2,1,0:T(8,128)S(1)}, u32[]{:S(2)}, u32[]{:S(2)}) async-start(f32[8,8,128]{2,1,0:T(8,128)} %get-tuple-element.83), calls=%async_computation | async-start | bytes 65536 | tf_op jit(solution)/shard_map/all_to_all | solution.py:631
  16.3 0.9 copy-start.1
  38.3 1.0 copy-start
  48.5 14.0 %collective-permute-start.3 = (f32[384,128]{1,0:T(8,128)S(1)}, f32[384,128]{1,0:T(8,128)S(1)}, u32[]{:S(2)}, u32[]{:S(2)}) collective-permute-start(f32[384,128]{1,0:T(8,128)S(1)} %get-tuple-element.106), channel_id=1, source_target_pairs={{0,1},{1,0},{2,3},{3,2},{4,5},{5,4},{6,7},{7,6},{8,9},{9,8},{10,11... | collective-permute-start | bytes 589832 | tf_op jit(solution)/shard_map/ppermute | solution.py:656
  50.4 12.2 %collective-permute-start.5 = (f32[384,128]{1,0:T(8,128)S(1)}, f32[384,128]{1,0:T(8,128)S(1)}, u32[]{:S(2)}, u32[]{:S(2)}) collective-permute-start(f32[384,128]{1,0:T(8,128)S(1)} %get-tuple-element.108), channel_id=1, source_target_pairs={{0,7},{1,2},{2,1},{3,4},{4,3},{5,6},{6,5},{7,0},{8,15},{9,10},{10,... | collective-permute-start | bytes 589832 | tf_op jit(solution)/shard_map/ppermute | solution.py:658
  50.6 11.9 %collective-permute-start.2 = (f32[384,128]{1,0:T(8,128)S(1)}, f32[384,128]{1,0:T(8,128)S(1)}, u32[]{:S(2)}, u32[]{:S(2)}) collective-permute-start(f32[384,128]{1,0:T(8,128)S(1)} %get-tuple-element.105), channel_id=1, source_target_pairs={{0,8},{8,0},{16,24},{24,16},{32,40},{40,32},{48,56},{56,48},{64,72... | collective-permute-start | bytes 589832 | tf_op jit(solution)/shard_map/ppermute | solution.py:655
  50.8 11.8 %collective-permute-start.4 = (f32[384,128]{1,0:T(8,128)S(1)}, f32[384,128]{1,0:T(8,128)S(1)}, u32[]{:S(2)}, u32[]{:S(2)}) collective-permute-start(f32[384,128]{1,0:T(8,128)S(1)} %get-tuple-element.107), channel_id=1, source_target_pairs={{0,120},{8,16},{16,8},{24,32},{32,24},{40,48},{48,40},{56,64},{64,... | collective-permute-start | bytes 589832 | tf_op jit(solution)/shard_map/ppermute | solution.py:657
  79.7 14.5 %collective-permute-start.7 = (f32[384,128]{1,0:T(8,128)S(1)}, f32[384,128]{1,0:T(8,128)S(1)}, u32[]{:S(2)}, u32[]{:S(2)}) collective-permute-start(f32[384,128]{1,0:T(8,128)S(1)} %get-tuple-element.122), channel_id=1, source_target_pairs={{0,1},{1,0},{2,3},{3,2},{4,5},{5,4},{6,7},{7,6},{8,9},{9,8},{10,11... | collective-permute-start | bytes 589832 | tf_op jit(solution)/shard_map/ppermute | solution.py:656
  82.1 12.2 %collective-permute-start.9 = (f32[384,128]{1,0:T(8,128)S(1)}, f32[384,128]{1,0:T(8,128)S(1)}, u32[]{:S(2)}, u32[]{:S(2)}) collective-permute-start(f32[384,128]{1,0:T(8,128)S(1)} %get-tuple-element.124), channel_id=1, source_target_pairs={{0,7},{1,2},{2,1},{3,4},{4,3},{5,6},{6,5},{7,0},{8,15},{9,10},{10,... | collective-permute-start | bytes 589832 | tf_op jit(solution)/shard_map/ppermute | solution.py:658
  82.3 11.9 %collective-permute-start.6 = (f32[384,128]{1,0:T(8,128)S(1)}, f32[384,128]{1,0:T(8,128)S(1)}, u32[]{:S(2)}, u32[]{:S(2)}) collective-permute-start(f32[384,128]{1,0:T(8,128)S(1)} %get-tuple-element.121), channel_id=1, source_target_pairs={{0,8},{8,0},{16,24},{24,16},{32,40},{40,32},{48,56},{56,48},{64,72... | collective-permute-start | bytes 589832 | tf_op jit(solution)/shard_map/ppermute | solution.py:655
  82.4 11.8 %collective-permute-start.8 = (f32[384,128]{1,0:T(8,128)S(1)}, f32[384,128]{1,0:T(8,128)S(1)}, u32[]{:S(2)}, u32[]{:S(2)}) collective-permute-start(f32[384,128]{1,0:T(8,128)S(1)} %get-tuple-element.123), channel_id=1, source_target_pairs={{0,120},{8,16},{16,8},{24,32},{32,24},{40,48},{48,40},{56,64},{64,... | collective-permute-start | bytes 589832 | tf_op jit(solution)/shard_map/ppermute | solution.py:657
  111.4 14.7 %collective-permute-start.11 = (f32[384,128]{1,0:T(8,128)S(1)}, f32[384,128]{1,0:T(8,128)S(1)}, u32[]{:S(2)}, u32[]{:S(2)}) collective-permute-start(f32[384,128]{1,0:T(8,128)S(1)} %get-tuple-element.138), channel_id=1, source_target_pairs={{0,1},{1,0},{2,3},{3,2},{4,5},{5,4},{6,7},{7,6},{8,9},{9,8},{10,11... | collective-permute-start | bytes 589832 | tf_op jit(solution)/shard_map/ppermute | solution.py:656
  113.8 12.3 %collective-permute-start.13 = (f32[384,128]{1,0:T(8,128)S(1)}, f32[384,128]{1,0:T(8,128)S(1)}, u32[]{:S(2)}, u32[]{:S(2)}) collective-permute-start(f32[384,128]{1,0:T(8,128)S(1)} %get-tuple-element.140), channel_id=1, source_target_pairs={{0,7},{1,2},{2,1},{3,4},{4,3},{5,6},{6,5},{7,0},{8,15},{9,10},{10,... | collective-permute-start | bytes 589832 | tf_op jit(solution)/shard_map/ppermute | solution.py:658
  114.0 12.0 %collective-permute-start.10 = (f32[384,128]{1,0:T(8,128)S(1)}, f32[384,128]{1,0:T(8,128)S(1)}, u32[]{:S(2)}, u32[]{:S(2)}) collective-permute-start(f32[384,128]{1,0:T(8,128)S(1)} %get-tuple-element.137), channel_id=1, source_target_pairs={{0,8},{8,0},{16,24},{24,16},{32,40},{40,32},{48,56},{56,48},{64,72... | collective-permute-start | bytes 589832 | tf_op jit(solution)/shard_map/ppermute | solution.py:655
  114.1 11.9 %collective-permute-start.12 = (f32[384,128]{1,0:T(8,128)S(1)}, f32[384,128]{1,0:T(8,128)S(1)}, u32[]{:S(2)}, u32[]{:S(2)}) collective-permute-start(f32[384,128]{1,0:T(8,128)S(1)} %get-tuple-element.139), channel_id=1, source_target_pairs={{0,120},{8,16},{16,8},{24,32},{32,24},{40,48},{48,40},{56,64},{64,... | collective-permute-start | bytes 589832 | tf_op jit(solution)/shard_map/ppermute | solution.py:657
  143.6 12.3 %collective-permute-start.15 = (f32[384,128]{1,0:T(8,128)S(1)}, f32[384,128]{1,0:T(8,128)S(1)}, u32[]{:S(2)}, u32[]{:S(2)}) collective-permute-start(f32[384,128]{1,0:T(8,128)S(1)} %get-tuple-element.155), channel_id=1, source_target_pairs={{0,7},{1,0},{2,1},{3,2},{4,3},{5,4},{6,5},{7,6},{8,15},{9,8},{10,9... | collective-permute-start | bytes 589832 | tf_op jit(solution)/shard_map/ppermute | solution.py:651
  145.9 10.0 %collective-permute-start.14 = (f32[384,128]{1,0:T(8,128)S(1)}, f32[384,128]{1,0:T(8,128)S(1)}, u32[]{:S(2)}, u32[]{:S(2)}) collective-permute-start(f32[384,128]{1,0:T(8,128)S(1)} %get-tuple-element.154), channel_id=1, source_target_pairs={{0,120},{8,0},{16,8},{24,16},{32,24},{40,32},{48,40},{56,48},{64,5... | collective-permute-start | bytes 589832 | tf_op jit(solution)/shard_map/ppermute | solution.py:650

commit v5 on v4

--- a/solution.py
+++ b/solution.py
@@ -628,8 +628,9 @@
     )
     west = lax.ppermute(pack_east, "gy", shift(lines[1], 1))
     north = lax.ppermute(pack_south, "gx", shift(lines[0], 1))
+    message, parity = lax.optimization_barrier((message, parity))
     gathered = lax.all_to_all(message, "gy", 0, 0)
-    gathered, west, north, parity = lax.optimization_barrier((gathered, west, north, parity))
+    gathered, west, north = lax.optimization_barrier((gathered, west, north))
     mask, t_high, t_low, g_high, g_low, gives, takes, coarse, pieces = frame(
         lines, slots, parity, own, west, north, gathered
     )

time: 170 us -> 170 us (level)
  blocking collectives: 102 us -> 112 us
  starting transfers between devices: 25.7 us -> 20.8 us
  waiting for transfers between devices: 4.68 us -> 0.04 us
    all_to_all x0 -> x1, blocking collectives: none -> 9.69 us  [local(): gathered = lax.all_to_all(message, 'gy', 0, 0)]
    all_to_all x1 -> x0, starting transfers between devices: 4.97 us -> none  [local(): gathered = lax.all_to_all(message, 'gy', 0, 0)]
    all_to_all x1 -> x0, waiting for transfers between devices: 4.64 us -> none  [local(): gathered = lax.all_to_all(message, 'gy', 0, 0)]
  transfers between devices with their start and end apart: 17 -> 16, of which waited for: 1 -> 0; matrix products, arithmetic and copies ran while one was open for 0% -> 0% of each run, Pallas kernels for 1% -> 1%
where the time goes in v5:
time: 170 us; the launch traced here: 168 us
  blocking collectives  112 us (66%)
  Pallas kernels  33 us (19%)
  starting transfers between devices  20.8 us (12%)
  local copies, waits for them, and re-layouts  1.99 us (1%)
    all_to_all x4, blocking collectives, exchange(): out.parts = lax.all_to_all(solve(terms, *solver, kept), 'gx', 0, 0)  45 us
    all_to_all x4, blocking collectives, exchange(): terms = lax.all_to_all(out.message, 'gy', 0, 0)  37.4 us
    pallas_call x13, Pallas kernels, call(): pl.pallas_call(functools.partial(kernel, keys), in_specs=[VMEM_SPEC if v....  24.1 us
    all_to_all x1, blocking collectives, local(): received = lax.all_to_all(pieces, 'gx', 0, 0)  19.6 us
    all_to_all x1, blocking collectives, local(): gathered = lax.all_to_all(message, 'gy', 0, 0)  9.69 us
    ppermute x3, starting transfers between devices, exchange(): lax.ppermute(out.send_y_first, 'gy', swap_first(lines[1]))  6.59 us
    ppermute x3, starting transfers between devices, exchange(): lax.ppermute(out.send_x_second, 'gx', swap_second(lines[0]))  5.35 us
    pallas_call x1, Pallas kernels, spread(): pl.pallas_call(spread_kernel, in_specs=[VMEM_SPEC] + [pl.BlockSpec(memory...  3.95 us
  transfers between devices with their start and end apart: 16, of which 0 were waited for; matrix products, arithmetic and copies ran while one was open for 0% of the time, Pallas kernels for 1%

profile of v5, /device:TPU:1, one launch (start us, length us, event | category | flops | bytes accessed | tf_op | source)
XLA Modules:
  0.0 168.2 jit_solution(3972789824580131394)
XLA Ops:
  2.2 3.0 %collective-permute-start = (f32[16,768]{1,0:T(8,128)}, f32[16,768]{1,0:T(8,128)S(1)}, u32[]{:S(2)}, u32[]{:S(2)}) collective-permute-start(f32[16,768]{1,0:T(8,128)} %get-tuple-element.88), channel_id=1, source_target_pairs={{0,1},{1,2},{2,3},{3,4},{4,5},{5,6},{6,7},{7,0},{8,9},{9,10},{10,1... | collective-permute-start | bytes 147464 | tf_op jit(solution)/shard_map/ppermute | solution.py:629
  6.7 9.7 %all_to_all.50.rhs_ref = f32[8,8,128]{2,1,0:T(8,128)S(1)} all-to-all(f32[8,8,128]{2,1,0:T(8,128)} %get-tuple-element.87), channel_id=1, replica_groups=mesh['gx'=16,'gy'=8] {'gy'}, dimensions={0} | all-to-all | bytes 65536 | tf_op jit(solution)/shard_map/all_to_all | solution.py:632
  18.8 19.6 %all_to_all.51.received_ref.refs_7_ = f32[16,96,128]{2,1,0:T(8,128)S(1)} all-to-all(f32[16,96,128]{2,1,0:T(8,128)S(1)} %get-tuple-element.95), channel_id=1, replica_groups=mesh['gx'=16,'gy'=8] {'gx'}, dimensions={0} | all-to-all | bytes 1572864 | tf_op jit(solution)/shard_map/all_to_all | solution.py:637
  39.3 4.0 %spread.1 = (bf16[640,320]{1,0:T(8,128)(2,1)S(1)}, bf16[640,320]{1,0:T(8,128)(2,1)S(1)}, bf16[1536,1536]{1,0:T(8,128)(2,1)S(1)}, bf16[1536,1536]{1,0:T(8,128)(2,1)S(1)}, f32[2,384,128]{2,1,0:T(8,128)S(1)}) custom-call(f32[16,96,128]{2,1,0:T(8,128)S(1)} %all_to_all.51.received_ref.refs_7_, f32[1536,1536]{1,0:T(8,128)} %bitcast.18, f32[2,384,128]{2,1,0:T(8,128)S(1)} %bitcast.17), custom_call_target="tpu_custom_call" | custom-call | tf_op jit(solution)/shard_map/spread/pallas_call | solution.py:279
  43.3 3.2 %update0.1 = (bf16[1536,256]{1,0:T(8,128)(2,1)S(1)}, f32[2,384,128]{2,1,0:T(8,128)S(1)}, f32[384,128]{1,0:T(8,128)S(1)}, f32[384,128]{1,0:T(8,128)S(1)}, f32[768,128]{1,0:T(8,128)S(1)}) custom-call(s32[6]{0:T(128)S(1)} %stack.43.place_ref.refs_0_.refs_5_, bf16[1536,1536]{1,0:T(8,128)(2,1)S(1)} %get-tuple-element.96.refs_1_, ...), custom_call_target="tpu_custom_call" | custom-call | flops 1207959552 | bytes 4096 | tf_op jit(solution)/shard_map/update0/pallas_call | solution.py:498
  46.5 2.2 %apply0.1 = (f32[2,384,128]{2,1,0:T(8,128)S(1)}, f32[384,128]{1,0:T(8,128)S(1)}, f32[384,128]{1,0:T(8,128)S(1)}) custom-call(s32[6]{0:T(128)S(1)} %stack.43.place_ref.refs_0_.refs_5_, bf16[1536,1536]{1,0:T(8,128)(2,1)S(1)} %get-tuple-element.96.refs_1_, bf16[1536,1536]{1,0:T(8,128)(2,1)S(1)} %get-tuple-element.97.refs_2_, ...), custom_call_target="tpu_custom_call" | custom-call | flops 1207959552 | bytes 4096 | tf_op jit(solution)/shard_map/apply0/pallas_call | solution.py:498
  48.6 1.8 %collective-permute-start.3 = (f32[384,128]{1,0:T(8,128)S(1)}, f32[384,128]{1,0:T(8,128)S(1)}, u32[]{:S(2)}, u32[]{:S(2)}) collective-permute-start(f32[384,128]{1,0:T(8,128)S(1)} %get-tuple-element.108), channel_id=1, source_target_pairs={{0,1},{1,0},{2,3},{3,2},{4,5},{5,4},{6,7},{7,6},{8,9},{9,8},{10,11... | collective-permute-start | bytes 589832 | tf_op jit(solution)/shard_map/ppermute | solution.py:657
  52.9 9.7 %all_to_all.52.terms_ref = f32[8,40,128]{2,1,0:T(8,128)S(1)} all-to-all(f32[8,40,128]{2,1,0:T(8,128)S(1)} %terms0.1), channel_id=1, replica_groups=mesh['gx'=16,'gy'=8] {'gy'}, dimensions={0} | all-to-all | bytes 327680 | tf_op jit(solution)/shard_map/all_to_all | solution.py:661
  63.1 11.6 %all_to_all.53.refs_7_ = f32[16,32,128]{2,1,0:T(8,128)S(1)} all-to-all(f32[16,32,128]{2,1,0:T(8,128)S(1)} %solve.4), channel_id=1, replica_groups=mesh['gx'=16,'gy'=8] {'gx'}, dimensions={0} | all-to-all | bytes 524288 | tf_op jit(solution)/shard_map/all_to_all | solution.py:665
  74.7 2.9 %update1.1 = (bf16[1536,256]{1,0:T(8,128)(2,1)S(1)}, f32[2,384,128]{2,1,0:T(8,128)S(1)}, f32[384,128]{1,0:T(8,128)S(1)}, f32[384,128]{1,0:T(8,128)S(1)}, f32[1536,128]{1,0:T(8,128)S(1)}) custom-call(s32[6]{0:T(128)S(1)} %stack.43.place_ref.refs_0_.refs_5_, bf16[1536,1536]{1,0:T(8,128)(2,1)S(1)} %get-tuple-element.96.refs_1_, ...), custom_call_target="tpu_custom_call" | custom-call | flops 1207959552 | bytes 4096 | tf_op jit(solution)/shard_map/update1/pallas_call | solution.py:498
  77.6 2.2 %apply1.1 = (f32[2,384,128]{2,1,0:T(8,128)S(1)}, f32[384,128]{1,0:T(8,128)S(1)}, f32[384,128]{1,0:T(8,128)S(1)}) custom-call(s32[6]{0:T(128)S(1)} %stack.43.place_ref.refs_0_.refs_5_, bf16[1536,1536]{1,0:T(8,128)(2,1)S(1)} %get-tuple-element.96.refs_1_, bf16[1536,1536]{1,0:T(8,128)(2,1)S(1)} %get-tuple-element.97.refs_2_, ...), custom_call_target="tpu_custom_call" | custom-call | flops 1207959552 | bytes 4096 | tf_op jit(solution)/shard_map/apply1/pallas_call | solution.py:498
  79.8 2.4 %collective-permute-start.7 = (f32[384,128]{1,0:T(8,128)S(1)}, f32[384,128]{1,0:T(8,128)S(1)}, u32[]{:S(2)}, u32[]{:S(2)}) collective-permute-start(f32[384,128]{1,0:T(8,128)S(1)} %get-tuple-element.124), channel_id=1, source_target_pairs={{0,1},{1,0},{2,3},{3,2},{4,5},{5,4},{6,7},{7,6},{8,9},{9,8},{10,11... | collective-permute-start | bytes 589832 | tf_op jit(solution)/shard_map/ppermute | solution.py:657
  84.7 9.7 %all_to_all.54.terms_ref = f32[8,40,128]{2,1,0:T(8,128)S(1)} all-to-all(f32[8,40,128]{2,1,0:T(8,128)S(1)} %terms1.1), channel_id=1, replica_groups=mesh['gx'=16,'gy'=8] {'gy'}, dimensions={0} | all-to-all | bytes 327680 | tf_op jit(solution)/shard_map/all_to_all | solution.py:661
  94.9 11.6 %all_to_all.55.refs_7_ = f32[16,32,128]{2,1,0:T(8,128)S(1)} all-to-all(f32[16,32,128]{2,1,0:T(8,128)S(1)} %solve.5), channel_id=1, replica_groups=mesh['gx'=16,'gy'=8] {'gx'}, dimensions={0} | all-to-all | bytes 524288 | tf_op jit(solution)/shard_map/all_to_all | solution.py:665
  106.4 2.9 %update2.1 = (bf16[1536,256]{1,0:T(8,128)(2,1)S(1)}, f32[2,384,128]{2,1,0:T(8,128)S(1)}, f32[384,128]{1,0:T(8,128)S(1)}, f32[384,128]{1,0:T(8,128)S(1)}, f32[153...) custom-call(s32[6]{0:T(128)S(1)} %stack.43.place_ref.refs_0_.refs_5_, ...), custom_call_target="tpu_custom_call" | custom-call | flops 1207959552 | bytes 4096 | tf_op jit(solution)/shard_map/update2/pallas_call | solution.py:498
  109.4 2.2 %apply2.1 = (f32[2,384,128]{2,1,0:T(8,128)S(1)}, f32[384,128]{1,0:T(8,128)S(1)}, f32[384,128]{1,0:T(8,128)S(1)}) custom-call(s32[6]{0:T(128)S(1)} %stack.43.place_ref.refs_0_.refs_5_, bf16[1536,1536]{1,0:T(8,128)(2,1)S(1)} %get-tuple-element.96.refs_1_, bf16[1536,1536]{1,0:T(8,128)(2,1)S(1)} %get-tuple-element.97.refs_2_, ...), custom_call_target="tpu_custom_call" | custom-call | flops 1207959552 | bytes 4096 | tf_op jit(solution)/shard_map/apply2/pallas_call | solution.py:498
  111.5 2.4 %collective-permute-start.11 = (f32[384,128]{1,0:T(8,128)S(1)}, f32[384,128]{1,0:T(8,128)S(1)}, u32[]{:S(2)}, u32[]{:S(2)}) collective-permute-start(f32[384,128]{1,0:T(8,128)S(1)} %get-tuple-element.140), channel_id=1, source_target_pairs={{0,1},{1,0},{2,3},{3,2},{4,5},{5,4},{6,7},{7,6},{8,9},{9,8},{10,11... | collective-permute-start | bytes 589832 | tf_op jit(solution)/shard_map/ppermute | solution.py:657
  116.6 9.7 %all_to_all.56.terms_ref = f32[8,40,128]{2,1,0:T(8,128)S(1)} all-to-all(f32[8,40,128]{2,1,0:T(8,128)S(1)} %get-tuple-element.138), channel_id=1, replica_groups=mesh['gx'=16,'gy'=8] {'gy'}, dimensions={0} | all-to-all | bytes 327680 | tf_op jit(solution)/shard_map/all_to_all | solution.py:661
  126.8 12.0 %all_to_all.57.refs_7_ = f32[16,40,128]{2,1,0:T(8,128)S(1)} all-to-all(f32[16,40,128]{2,1,0:T(8,128)S(1)} %solve.6), channel_id=1, replica_groups=mesh['gx'=16,'gy'=8] {'gx'}, dimensions={0} | all-to-all | bytes 655360 | tf_op jit(solution)/shard_map/all_to_all | solution.py:665
  138.7 2.9 %update3.1 = (bf16[1536,256]{1,0:T(8,128)(2,1)S(1)}, f32[2,384,128]{2,1,0:T(8,128)S(1)}, f32[384,128]{1,0:T(8,128)S(1)}, f32[1536,128]{1,0:T(8,128)S(1)}, f32[1536,128]{1,0:T(8,128)S(1)}, /*index=5*/f32[8,128]{1,0:T(8,128)S(1)}) custom-call(s32[6]{0:T(128)S(1)} %stack.43.place_ref.refs_0_.refs_5_, bf16[1536,1536]{1,0:T(8,128)(2,1)S(1)} %get-tuple-element.96.refs_1_, ...), custom_call_target="tpu_custom_call" | custom-call | flops 1207959552 | bytes 4096 | tf_op jit(solution)/shard_map/update3/pallas_call | solution.py:498
  141.7 2.1 %apply3.1 = (f32[2,384,128]{2,1,0:T(8,128)S(1)}, f32[384,128]{1,0:T(8,128)S(1)}) custom-call(s32[6]{0:T(128)S(1)} %stack.43.place_ref.refs_0_.refs_5_, bf16[1536,1536]{1,0:T(8,128)(2,1)S(1)} %get-tuple-element.96.refs_1_, bf16[1536,1536]{1,0:T(8,128)(2,1)S(1)} %get-tuple-element.97.refs_2_, bf16[2,384,384]{2,1,0:T(8,128)(2,1)S(1)} %get-tuple-element.98.refs_3_, ...), custom_call_target="tpu_custom_call" | custom-call | flops 1207959552 | bytes 4096 | tf_op jit(solution)/shard_map/apply3/pallas_call | solution.py:498
  143.8 2.3 %collective-permute-start.15 = (f32[384,128]{1,0:T(8,128)S(1)}, f32[384,128]{1,0:T(8,128)S(1)}, u32[]{:S(2)}, u32[]{:S(2)}) collective-permute-start(f32[384,128]{1,0:T(8,128)S(1)} %get-tuple-element.157), channel_id=1, source_target_pairs={{0,7},{1,0},{2,1},{3,2},{4,3},{5,4},{6,5},{7,6},{8,15},{9,8},{10,9... | collective-permute-start | bytes 589832 | tf_op jit(solution)/shard_map/ppermute | solution.py:652
  147.8 8.3 %all_to_all.58.terms_ref = f32[8,40,128]{2,1,0:T(8,128)S(1)} all-to-all(f32[8,40,128]{2,1,0:T(8,128)S(1)} %get-tuple-element.155), channel_id=1, replica_groups=mesh['gx'=16,'gy'=8] {'gy'}, dimensions={0} | all-to-all | bytes 327680 | tf_op jit(solution)/shard_map/all_to_all | solution.py:661
  156.6 9.8 %all_to_all.59.refs_0_ = f32[16,24,128]{2,1,0:T(8,128)S(1)} all-to-all(f32[16,24,128]{2,1,0:T(8,128)S(1)} %solve.7), channel_id=1, replica_groups=mesh['gx'=16,'gy'=8] {'gx'}, dimensions={0} | all-to-all | bytes 393216 | tf_op jit(solution)/shard_map/all_to_all | solution.py:665
  (43 shorter events, 19.3 us)
Async XLA Ops:
  2.2 14.1 %collective-permute-start = (f32[16,768]{1,0:T(8,128)}, f32[16,768]{1,0:T(8,128)S(1)}, u32[]{:S(2)}, u32[]{:S(2)}) collective-permute-start(f32[16,768]{1,0:T(8,128)} %get-tuple-element.88), channel_id=1, source_target_pairs={{0,1},{1,2},{2,3},{3,4},{4,5},{5,6},{6,7},{7,0},{8,9},{9,10},{10,1... | collective-permute-start | bytes 147464 | tf_op jit(solution)/shard_map/ppermute | solution.py:629
  5.3 11.1 %collective-permute-start.1 = (f32[16,768]{1,0:T(8,128)}, f32[16,768]{1,0:T(8,128)S(1)}, u32[]{:S(2)}, u32[]{:S(2)}) collective-permute-start(f32[16,768]{1,0:T(8,128)} %get-tuple-element.89), channel_id=1, source_target_pairs={{0,8},{8,16},{16,24},{24,32},{32,40},{40,48},{48,56},{56,64},{64,7... | collective-permute-start | bytes 147464 | tf_op jit(solution)/shard_map/ppermute | solution.py:630
  16.3 0.9 copy-start.1
  38.3 1.0 copy-start
  48.6 14.0 %collective-permute-start.3 = (f32[384,128]{1,0:T(8,128)S(1)}, f32[384,128]{1,0:T(8,128)S(1)}, u32[]{:S(2)}, u32[]{:S(2)}) collective-permute-start(f32[384,128]{1,0:T(8,128)S(1)} %get-tuple-element.108), channel_id=1, source_target_pairs={{0,1},{1,0},{2,3},{3,2},{4,5},{5,4},{6,7},{7,6},{8,9},{9,8},{10,11... | collective-permute-start | bytes 589832 | tf_op jit(solution)/shard_map/ppermute | solution.py:657
  50.5 12.2 %collective-permute-start.5 = (f32[384,128]{1,0:T(8,128)S(1)}, f32[384,128]{1,0:T(8,128)S(1)}, u32[]{:S(2)}, u32[]{:S(2)}) collective-permute-start(f32[384,128]{1,0:T(8,128)S(1)} %get-tuple-element.110), channel_id=1, source_target_pairs={{0,7},{1,2},{2,1},{3,4},{4,3},{5,6},{6,5},{7,0},{8,15},{9,10},{10,... | collective-permute-start | bytes 589832 | tf_op jit(solution)/shard_map/ppermute | solution.py:659
  50.7 11.9 %collective-permute-start.2 = (f32[384,128]{1,0:T(8,128)S(1)}, f32[384,128]{1,0:T(8,128)S(1)}, u32[]{:S(2)}, u32[]{:S(2)}) collective-permute-start(f32[384,128]{1,0:T(8,128)S(1)} %get-tuple-element.107), channel_id=1, source_target_pairs={{0,8},{8,0},{16,24},{24,16},{32,40},{40,32},{48,56},{56,48},{64,72... | collective-permute-start | bytes 589832 | tf_op jit(solution)/shard_map/ppermute | solution.py:656
  50.8 11.8 %collective-permute-start.4 = (f32[384,128]{1,0:T(8,128)S(1)}, f32[384,128]{1,0:T(8,128)S(1)}, u32[]{:S(2)}, u32[]{:S(2)}) collective-permute-start(f32[384,128]{1,0:T(8,128)S(1)} %get-tuple-element.109), channel_id=1, source_target_pairs={{0,120},{8,16},{16,8},{24,32},{32,24},{40,48},{48,40},{56,64},{64,... | collective-permute-start | bytes 589832 | tf_op jit(solution)/shard_map/ppermute | solution.py:658
  79.8 14.6 %collective-permute-start.7 = (f32[384,128]{1,0:T(8,128)S(1)}, f32[384,128]{1,0:T(8,128)S(1)}, u32[]{:S(2)}, u32[]{:S(2)}) collective-permute-start(f32[384,128]{1,0:T(8,128)S(1)} %get-tuple-element.124), channel_id=1, source_target_pairs={{0,1},{1,0},{2,3},{3,2},{4,5},{5,4},{6,7},{7,6},{8,9},{9,8},{10,11... | collective-permute-start | bytes 589832 | tf_op jit(solution)/shard_map/ppermute | solution.py:657
  82.2 12.2 %collective-permute-start.9 = (f32[384,128]{1,0:T(8,128)S(1)}, f32[384,128]{1,0:T(8,128)S(1)}, u32[]{:S(2)}, u32[]{:S(2)}) collective-permute-start(f32[384,128]{1,0:T(8,128)S(1)} %get-tuple-element.126), channel_id=1, source_target_pairs={{0,7},{1,2},{2,1},{3,4},{4,3},{5,6},{6,5},{7,0},{8,15},{9,10},{10,... | collective-permute-start | bytes 589832 | tf_op jit(solution)/shard_map/ppermute | solution.py:659
  82.4 12.0 %collective-permute-start.6 = (f32[384,128]{1,0:T(8,128)S(1)}, f32[384,128]{1,0:T(8,128)S(1)}, u32[]{:S(2)}, u32[]{:S(2)}) collective-permute-start(f32[384,128]{1,0:T(8,128)S(1)} %get-tuple-element.123), channel_id=1, source_target_pairs={{0,8},{8,0},{16,24},{24,16},{32,40},{40,32},{48,56},{56,48},{64,72... | collective-permute-start | bytes 589832 | tf_op jit(solution)/shard_map/ppermute | solution.py:656
  82.5 11.8 %collective-permute-start.8 = (f32[384,128]{1,0:T(8,128)S(1)}, f32[384,128]{1,0:T(8,128)S(1)}, u32[]{:S(2)}, u32[]{:S(2)}) collective-permute-start(f32[384,128]{1,0:T(8,128)S(1)} %get-tuple-element.125), channel_id=1, source_target_pairs={{0,120},{8,16},{16,8},{24,32},{32,24},{40,48},{48,40},{56,64},{64,... | collective-permute-start | bytes 589832 | tf_op jit(solution)/shard_map/ppermute | solution.py:658
  111.5 14.7 %collective-permute-start.11 = (f32[384,128]{1,0:T(8,128)S(1)}, f32[384,128]{1,0:T(8,128)S(1)}, u32[]{:S(2)}, u32[]{:S(2)}) collective-permute-start(f32[384,128]{1,0:T(8,128)S(1)} %get-tuple-element.140), channel_id=1, source_target_pairs={{0,1},{1,0},{2,3},{3,2},{4,5},{5,4},{6,7},{7,6},{8,9},{9,8},{10,11... | collective-permute-start | bytes 589832 | tf_op jit(solution)/shard_map/ppermute | solution.py:657
  113.9 12.4 %collective-permute-start.13 = (f32[384,128]{1,0:T(8,128)S(1)}, f32[384,128]{1,0:T(8,128)S(1)}, u32[]{:S(2)}, u32[]{:S(2)}) collective-permute-start(f32[384,128]{1,0:T(8,128)S(1)} %get-tuple-element.142), channel_id=1, source_target_pairs={{0,7},{1,2},{2,1},{3,4},{4,3},{5,6},{6,5},{7,0},{8,15},{9,10},{10,... | collective-permute-start | bytes 589832 | tf_op jit(solution)/shard_map/ppermute | solution.py:659
  114.2 12.1 %collective-permute-start.10 = (f32[384,128]{1,0:T(8,128)S(1)}, f32[384,128]{1,0:T(8,128)S(1)}, u32[]{:S(2)}, u32[]{:S(2)}) collective-permute-start(f32[384,128]{1,0:T(8,128)S(1)} %get-tuple-element.139), channel_id=1, source_target_pairs={{0,8},{8,0},{16,24},{24,16},{32,40},{40,32},{48,56},{56,48},{64,72... | collective-permute-start | bytes 589832 | tf_op jit(solution)/shard_map/ppermute | solution.py:656
  114.3 12.0 %collective-permute-start.12 = (f32[384,128]{1,0:T(8,128)S(1)}, f32[384,128]{1,0:T(8,128)S(1)}, u32[]{:S(2)}, u32[]{:S(2)}) collective-permute-start(f32[384,128]{1,0:T(8,128)S(1)} %get-tuple-element.141), channel_id=1, source_target_pairs={{0,120},{8,16},{16,8},{24,32},{32,24},{40,48},{48,40},{56,64},{64,... | collective-permute-start | bytes 589832 | tf_op jit(solution)/shard_map/ppermute | solution.py:658
  143.8 12.3 %collective-permute-start.15 = (f32[384,128]{1,0:T(8,128)S(1)}, f32[384,128]{1,0:T(8,128)S(1)}, u32[]{:S(2)}, u32[]{:S(2)}) collective-permute-start(f32[384,128]{1,0:T(8,128)S(1)} %get-tuple-element.157), channel_id=1, source_target_pairs={{0,7},{1,0},{2,1},{3,2},{4,3},{5,4},{6,5},{7,6},{8,15},{9,8},{10,9... | collective-permute-start | bytes 589832 | tf_op jit(solution)/shard_map/ppermute | solution.py:652
  146.1 10.0 %collective-permute-start.14 = (f32[384,128]{1,0:T(8,128)S(1)}, f32[384,128]{1,0:T(8,128)S(1)}, u32[]{:S(2)}, u32[]{:S(2)}) collective-permute-start(f32[384,128]{1,0:T(8,128)S(1)} %get-tuple-element.156), channel_id=1, source_target_pairs={{0,120},{8,0},{16,8},{24,16},{32,24},{40,32},{48,40},{56,48},{64,5... | collective-permute-start | bytes 589832 | tf_op jit(solution)/shard_map/ppermute | solution.py:651
